TPU v7x, 256 devices: a whole 4x4x8 slice. The times are simulated.
256 devices in a mesh: dp: 64 (over x_lo, y, z), tensor: 4 (over x_hi, core).
Axes of the slice: x: 4 (x_hi: 2, x_lo: 2; x = x_hi * 2 + x_lo), y: 4, z: 8, core: 2. Of those that a mesh axis runs over, the one named last changes fastest.
Arguments:
- attn: bfloat16 [16384, 8192], P('dp', 'tensor'), may hold values from -6 to 6
- output_gradient: bfloat16 [16384, 8192], P(('dp', 'tensor')), may hold values from -0.29882812 to 0.29882812
- down_weight: bfloat16 [512, 8192], P('dp', 'tensor'), may hold values from -0.0625 to 0.0625
- up_weight: bfloat16 [512, 8192], P('dp', 'tensor'), may hold values from -0.0625 to 0.0625
- adapter_of_row: int32 [16384], P('dp'), may hold values from -1 to 31, as said below
- lengths: int32 [64], P('dp'), may hold values from 1 to 256, 12288 in all
Outputs:
- attention_gradient: bfloat16 [16384, 8192], P('dp', 'tensor')
- grad_a: float32 [512, 8192], P('dp', 'tensor')
- grad_b: float32 [512, 8192], P('dp', 'tensor')
Inputs may be any that keep to these rules, and one draw needn't show every extreme that they name: `adapter_of_row`: within each aligned block of 128 rows the first 32 to 128 rows carry one adapter id and the rest are -1; along the rows of one sequence the blocks' ids never fall.
All inputs are finite; a program needn't handle non-finite values. No bound on the sum of `lengths` on one device may be relied on, other than what follows from the above.
Results may differ from a plain program's by a relative error of at most 0.0049.
Values may be sent and summed in bfloat16 or wider, within the bound.
No kernel may reach another device: no remote copies, remote signals or barrier semaphores. Data moves between devices by JAX's collectives and lax.ppermute only.
A program may use at most 64 MiB of HBM per device.

v0:
```python
import jax
import jax.numpy as jnp
from jax import lax
from jax.sharding import PartitionSpec as P

ADAPTER_COUNT = 32
ADAPTER_RANK = 16


adapter_scale = 2.0


def per_device(attn, output_gradient, down_weight, up_weight, adapter_of_row, lengths):
    row_count = attn.shape[0]
    layer_width = attn.shape[1]
    blocks = row_count // 128
    tables_a, tables_b = (
        lax.all_gather(down_weight, "dp", axis=0, tiled=True),
        lax.all_gather(up_weight, "dp", axis=0, tiled=True),
    )
    labels = adapter_of_row.reshape(blocks, 128)
    which = jnp.maximum(labels[:, 0], 0)
    picked_a = jnp.take(tables_a.reshape(ADAPTER_COUNT, ADAPTER_RANK, layer_width), which, axis=0)
    picked_b = jnp.take(tables_b.reshape(ADAPTER_COUNT, ADAPTER_RANK, layer_width), which, axis=0)
    offsets = jnp.arange(row_count, dtype=jnp.int32)
    live = (adapter_of_row >= 0) & (offsets < lengths[0])
    gathered = lax.all_gather(output_gradient, "tensor", axis=0, tiled=True)
    first_col = lax.axis_index("tensor") * layer_width
    gradient_list = lax.dynamic_slice_in_dim(gathered, first_col, layer_width, 1)
    gradient_list = jnp.where(live[:, None], gradient_list, jnp.zeros_like(gradient_list))
    input_blocks = attn.reshape(blocks, 128, layer_width)
    grad_blocks = gradient_list.reshape(blocks, 128, layer_width)
    inner_part = jnp.einsum(
        "bti,bri->btr", input_blocks, picked_a, preferred_element_type=jnp.float32
    )
    outer_part = jnp.einsum(
        "bti,bri->btr", grad_blocks, picked_b, preferred_element_type=jnp.float32
    )
    inner_product = lax.psum(inner_part, "tensor")
    outer_product = lax.psum(outer_part, "tensor")
    inner_product = inner_product.astype(jnp.bfloat16)
    outer_product = outer_product.astype(jnp.bfloat16)
    backward_pass = jnp.einsum(
        "btr,bri->bti", outer_product, picked_a, preferred_element_type=jnp.float32
    )
    attention_gradient = (
        (adapter_scale * backward_pass).reshape(row_count, layer_width).astype(jnp.bfloat16)
    )
    block_a = jnp.einsum(
        "btr,bti->bri", outer_product, input_blocks, preferred_element_type=jnp.float32
    )
    block_b = jnp.einsum(
        "btr,bti->bri", inner_product, grad_blocks, preferred_element_type=jnp.float32
    )
    selector = (which[:, None] == jnp.arange(ADAPTER_COUNT, dtype=jnp.int32)[None, :]).astype(
        jnp.float32
    )
    down_term = adapter_scale * jnp.einsum(
        "ba,bri->ari", selector, block_a, precision=lax.Precision.HIGHEST
    )
    up_term = adapter_scale * jnp.einsum(
        "ba,bri->ari", selector, block_b, precision=lax.Precision.HIGHEST
    )
    down_term = down_term.reshape(ADAPTER_COUNT * ADAPTER_RANK, layer_width)
    up_term = up_term.reshape(ADAPTER_COUNT * ADAPTER_RANK, layer_width)
    grad_a, grad_b = (
        lax.psum_scatter(down_term, "dp", scatter_dimension=0, tiled=True),
        lax.psum_scatter(up_term, "dp", scatter_dimension=0, tiled=True),
    )
    return (attention_gradient, grad_a, grad_b)


def solution(mesh):
    return jax.shard_map(
        per_device,
        mesh=mesh,
        in_specs=(
            P("dp", "tensor"),
            P(("dp", "tensor"), None),
            P("dp", "tensor"),
            P("dp", "tensor"),
            P("dp"),
            P("dp"),
        ),
        out_specs=(P("dp", "tensor"), P("dp", "tensor"), P("dp", "tensor")),
        check_vma=False,
    )
```

profile of v0, /device:TPU:2, one launch (start us, length us, event | category | flops | bytes accessed | tf_op | source)
XLA Modules:
  0.0 1322.1 jit_solution(15791407003032505003)
XLA Ops:
  7.2 0.0 copy-start
  7.2 0.0 all-gather.6.cloned.1.call-start
  7.2 0.7 all-gather.6.cloned.1.call-update
  7.9 0.0 all-gather.8.cloned.1.call-start
  8.0 0.7 all-gather.8.cloned.1.call-update
  8.7 0.0 all-gather.4.cloned.1.call-start
  8.7 0.7 all-gather.4.cloned.1.call-update
  9.4 0.0 reduce-scatter.5.cloned.1.call-start
  10.1 0.8 maximum_reduce_fusion
  10.9 0.7 compare_and_fusion.1
  11.6 300.2 %all-gather.6.cloned.1.call-done = bf16[512,2048]{1,0:T(8,128)(2,1)} async-done(((bf16[8,2048]{1,0:T(8,128)(2,1)}), bf16[512,2048]{1,0:T(8,128)(2,1)}) %all-gather.6.cloned.1.call-update) | async-done | bytes 2097168 | tf_op jit(solution)/shard_map/all_gather | solution.py:19
  311.8 2.1 gather_fusion
  314.0 296.9 %all-gather.8.cloned.1.call-done = bf16[512,2048]{1,0:T(8,128)(2,1)} async-done(((bf16[8,2048]{1,0:T(8,128)(2,1)}), bf16[512,2048]{1,0:T(8,128)(2,1)}) %all-gather.8.cloned.1.call-update) | async-done | bytes 2097168 | tf_op jit(solution)/shard_map/all_gather | solution.py:18
  610.9 2.1 gather_fusion.1
  613.0 0.0 copy-done
  613.0 0.4 convolution_bitcast_fusion
  613.4 37.6 %all-gather.4.cloned.1.call-done = bf16[256,8192]{1,0:T(8,128)(2,1)} async-done(((bf16[64,8192]{1,0:T(8,128)(2,1)}), bf16[256,8192]{1,0:T(8,128)(2,1)}) %all-gather.4.cloned.1.call-update) | async-done | bytes 4194320 | tf_op jit(solution)/shard_map/all_gather | solution.py:27
  651.1 1.5 dynamic-slice_select_fusion
  652.6 0.4 fusion.3
  653.0 14.5 %all-reduce = (bf16[2,128,16]{1,2,0:T(8,128)(2,1)S(1)}, bf16[2,128,16]{1,2,0:T(8,128)(2,1)S(1)}) all-reduce(f32[2,128,16]{1,2,0:T(8,128)S(1)} %fusion.3, f32[2,128,16]{1,2,0:T(8,128)S(1)} %convolution_bitcast_fusion), channel_id=1, replica_groups=mesh['dp'=64,'tensor'=4] {'tensor'}, use_global_device_ids=true, to_apply=%region_0.0 | all-reduce | flops 8192 | bytes 49152 | tf_op jit(solution)/shard_map/psum | solution.py:40
  667.5 0.3 fusion.19
  667.7 2.0 convolution_multiply_fusion
  669.7 4.4 copy.14
  674.1 0.0 reduce-scatter.5.cloned.1.call-update
  674.2 0.0 reduce-scatter.3.cloned.1.call-start
  674.2 0.3 fusion.20
  674.5 2.0 convolution_multiply_fusion.1
  676.5 4.4 copy.12
  680.8 0.0 reduce-scatter.3.cloned.1.call-update
  680.9 1.5 fusion
  682.3 314.1 %reduce-scatter.5.cloned.1.call-done = f32[8,2048]{1,0:T(8,128)} async-done(((f32[512,2048]{1,0:T(8,128)}), f32[8,2048]{1,0:T(8,128)}) %reduce-scatter.5.cloned.1.call-update) | async-done | bytes 65552 | tf_op jit(solution)/shard_map/reduce_scatter | solution.py:68
  996.4 319.1 %reduce-scatter.3.cloned.1.call-done = f32[8,2048]{1,0:T(8,128)} async-done(((f32[512,2048]{1,0:T(8,128)}), f32[8,2048]{1,0:T(8,128)}) %reduce-scatter.3.cloned.1.call-update) | async-done | bytes 65552 | tf_op jit(solution)/shard_map/reduce_scatter | solution.py:67
  (3 shorter events, 0.0 us)
Async XLA Ops:
  7.2 605.9 %copy-start = (bf16[256,2048]{1,0:T(8,128)(2,1)S(1)}, bf16[256,2048]{1,0:T(8,128)(2,1)}, u32[]{:S(2)}) copy-start(bf16[256,2048]{1,0:T(8,128)(2,1)} %param.8) | copy-start | bytes 3145732
  7.2 304.7 %all-gather.6.cloned.1.call-start = ((), (), s32[]{:S(2)}) async-start(), calls=%async_computation.3 | async-start | bytes 2129920 | tf_op jit(solution)/shard_map/all_gather | solution.py:19
  7.9 603.0 %all-gather.8.cloned.1.call-start = ((), (), s32[]{:S(2)}) async-start(), calls=%async_computation.4 | async-start | bytes 2129920 | tf_op jit(solution)/shard_map/all_gather | solution.py:18
  8.7 642.4 %all-gather.4.cloned.1.call-start = ((), (), s32[]{:S(2)}) async-start(), calls=%async_computation.2 | async-start | bytes 5242880 | tf_op jit(solution)/shard_map/all_gather | solution.py:27
  9.4 987.0 %reduce-scatter.5.cloned.1.call-start = ((), (), s32[]{:S(2)}) async-start(), calls=%async_computation.6 | async-start | bytes 4259840 | tf_op jit(solution)/shard_map/reduce_scatter | solution.py:68
  674.2 641.4 %reduce-scatter.3.cloned.1.call-start = ((), (), s32[]{:S(2)}) async-start(), calls=%async_computation.5 | async-start | bytes 4259840 | tf_op jit(solution)/shard_map/reduce_scatter | solution.py:67
Sparse Core Ops, SparseCore 0:
  9.8 301.9 all-gather.5
  313.6 297.2 all-gather.7
  612.7 38.3 all-gather.3
  674.3 322.0 reduce-scatter.4
  999.5 315.9 reduce-scatter.2
where the time goes:
time: 1320 us
  waiting for transfers between devices  1270 us (96%)
  blocking collectives  14.5 us (1%)
  between operations  14.5 us (1%)
    reduce_scatter x1, waiting for transfers between devices, per_device(): lax.psum_scatter(down_term, 'dp', scatter_dimension=0, tiled=True)  319 us
    reduce_scatter x1, waiting for transfers between devices, per_device(): lax.psum_scatter(up_term, 'dp', scatter_dimension=0, tiled=True)  314 us
    all_gather x1, waiting for transfers between devices, per_device(): lax.all_gather(up_weight, 'dp', axis=0, tiled=True)  300 us
    all_gather x1, waiting for transfers between devices, per_device(): lax.all_gather(down_weight, 'dp', axis=0, tiled=True)  297 us
    all_gather x1, waiting for transfers between devices, per_device(): gathered = lax.all_gather(output_gradient, 'tensor', axis=0, tiled=True)  37.6 us
  transfers between devices with their start and end apart: 5, of which 5 were waited for; matrix products, arithmetic and copies ran while one was open for 1% of the time, Pallas kernels for 0%

commit v1 on v0

v1 whole, which is shorter than its diff:
```python
import jax
import jax.numpy as jnp
from jax import lax
from jax.experimental import pallas as pl
from jax.experimental.pallas import tpu as pltpu
from jax.sharding import PartitionSpec as P

LANES = 128
BLOCK = 128
PEERS = 64
BANDS = 16
QUARTERS = 4

F32 = jnp.float32
BF16 = jnp.bfloat16

adapter_scale = 2.0

VMEM = pl.BlockSpec(memory_space=pltpu.VMEM)
SMEM = pl.BlockSpec(memory_space=pltpu.SMEM)
PARAMS = pltpu.CompilerParams(vmem_limit_bytes=40 * 1024 * 1024)


def rows_of(first, size, stride):
    return pl.ds(first, size, stride=stride)


def pack_tables(down_ref, up_ref, label_ref, out_ref, rows_f, out_f):
    for m, map_ref in enumerate((down_ref, up_ref)):
        for c in range(BANDS):
            rows_f[c * 8:(c + 1) * 8, :] = map_ref[:, c * LANES:(c + 1) * LANES].astype(F32)
        for i in range(2):
            out_f[rows_of(2 * m + i, PEERS, 8), :] = rows_f[rows_of(i, PEERS, 2), :]
    for b in range(2):
        which = jnp.maximum(label_ref[b * BLOCK], 0).astype(F32)
        out_f[rows_of(4 + b, PEERS, 8), :] = jnp.full((PEERS, LANES), which, F32)
        out_f[rows_of(6 + b, PEERS, 8), :] = jnp.zeros((PEERS, LANES), F32)
    out_ref[...] = out_f[...].astype(BF16)


def pick_rows(in_ref, out_ref, in_f, out_f):
    in_f[...] = in_ref[...].astype(F32)
    table = jnp.concatenate([in_f[rows_of(k, PEERS, 8), :] for k in range(4)], axis=1).astype(BF16)
    lane = lax.broadcasted_iota(jnp.int32, (PEERS, LANES), 1)
    for b in range(2):
        which = in_f[rows_of(4 + b, PEERS, 8), :].astype(jnp.int32)
        for h in range(2):
            chosen = (lane == 2 * which + h).astype(F32).astype(BF16)[:, :PEERS]
            picked = jnp.dot(chosen, table, preferred_element_type=F32)
            for k in range(4):
                out_f[rows_of(b * 8 + h * 4 + k, PEERS, 16), :] = picked[:, k * LANES:(k + 1) * LANES]
    out_ref[...] = out_f[...].astype(BF16)


def project(picked_ref, attn_ref, own_ref, one_ref, two_ref, three_ref, place_ref, maps_ref, grad_ref, part_ref):
    me = place_ref[0]
    for k, piece in enumerate((own_ref, one_ref, two_ref, three_ref)):
        first = pl.multiple_of(lax.bitwise_xor(me, k) * 64, 64)
        grad_ref[pl.ds(first, 64), :] = piece[...]
    for c in range(BANDS):
        rows = picked_ref[c * 64:(c + 1) * 64, :].astype(F32).reshape(QUARTERS, 2, 8, LANES)
        for b in range(2):
            maps_ref[b * 32:(b + 1) * 32, c * LANES:(c + 1) * LANES] = rows[:, b].reshape(32, LANES).astype(BF16)
    row = lax.broadcasted_iota(jnp.int32, (32, BLOCK), 0)
    over_last = (((1,), (1,)), ((), ()))
    for b in range(2):
        maps = maps_ref[b * 32:(b + 1) * 32, :]
        block = slice(b * BLOCK, (b + 1) * BLOCK)
        inner = lax.dot_general(maps, attn_ref[block, :], over_last, preferred_element_type=F32)
        outer = lax.dot_general(maps, grad_ref[block, :], over_last, preferred_element_type=F32)
        part_ref[:, block] = jnp.where((row & 2) == 0, inner, outer)


def expand(own_ref, one_ref, two_ref, three_ref, label_ref, length_ref, maps_ref, attn_ref, grad_ref, back_ref, term_ref):
    total = (own_ref[...] + one_ref[...]) + (two_ref[...] + three_ref[...])
    offset = lax.broadcasted_iota(jnp.int32, (1, 2 * BLOCK), 1)
    live = (label_ref[...] >= 0) & (offset < length_ref[0])
    total = jnp.where(live, total, 0.0).astype(BF16)
    row = lax.broadcasted_iota(jnp.int32, (32, BLOCK), 0)
    row_w = lax.broadcasted_iota(jnp.int32, (32, LANES), 0)
    over_first = (((0,), (0,)), ((), ()))
    terms = []
    for b in range(2):
        block = slice(b * BLOCK, (b + 1) * BLOCK)
        ranks = total[:, block]
        down = jnp.dot(ranks, attn_ref[block, :], preferred_element_type=F32)
        up = jnp.dot(ranks, grad_ref[block, :], preferred_element_type=F32)
        terms.append((down, up))
        shifted = pltpu.roll(ranks.astype(F32), 30, 0)
        outer = jnp.where((row & 2) == 0, shifted, 0.0).astype(BF16)
        back = lax.dot_general(outer, maps_ref[b * 32:(b + 1) * 32, :], over_first, preferred_element_type=F32)
        back_ref[block, :] = (adapter_scale * back).astype(BF16)
    for c in range(BANDS):
        band = slice(c * LANES, (c + 1) * LANES)
        both = [
            adapter_scale * jnp.where((row_w & 2) == 0, up[:, band], down[:, band])
            for down, up in terms
        ]
        for q in range(QUARTERS):
            pair = jnp.concatenate([one[q * 8:(q + 1) * 8] for one in both], axis=0)
            term_ref[c * 64 + q * 16:c * 64 + (q + 1) * 16, :] = pair.astype(BF16)


def add_up(in_ref, ids_ref, out_ref, in_f, ids_f):
    in_f[...] = in_ref[...].astype(F32)
    ids_f[...] = ids_ref[...].astype(F32)
    lane = lax.broadcasted_iota(jnp.int32, (PEERS, LANES), 1)
    over_first = (((0,), (0,)), ((), ()))
    total = jnp.zeros((LANES, 8 * LANES), F32)
    for b in range(2):
        which = ids_f[rows_of(4 + b, PEERS, 8), :].astype(jnp.int32)
        chosen = (lane == which).astype(F32).astype(BF16)
        terms = jnp.concatenate(
            [in_f[rows_of(b * 8 + k, PEERS, 16), :] for k in range(8)], axis=1
        ).astype(BF16)
        total += lax.dot_general(chosen, terms, over_first, preferred_element_type=F32)
    for k in range(8):
        out_ref[rows_of(k, 32, 8), :] = total[:32, k * LANES:(k + 1) * LANES]


def unpack(in_ref, down_ref, up_ref, rows_f):
    for m, map_ref in ((0, up_ref), (1, down_ref)):
        for i in range(2):
            rows_f[rows_of(i, PEERS, 2), :] = in_ref[rows_of(2 * m + i, PEERS, 4), :]
        for c in range(BANDS):
            map_ref[:, c * LANES:(c + 1) * LANES] = rows_f[c * 8:(c + 1) * 8, :]


def call(kernel, outs, specs, scratch=()):
    return pl.pallas_call(
        kernel,
        out_shape=[jax.ShapeDtypeStruct(shape, dtype) for shape, dtype in outs],
        in_specs=specs,
        out_specs=[VMEM] * len(outs),
        scratch_shapes=[pltpu.VMEM(shape, dtype) for shape, dtype in scratch],
        compiler_params=PARAMS,
    )


def swap(x):
    chunks = x.reshape(PEERS, x.shape[0] // PEERS, LANES)
    return lax.all_to_all(chunks, "dp", 0, 0, tiled=True).reshape(x.shape)


def from_peer(x, k):
    return lax.ppermute(x, "tensor", [(i, i ^ k) for i in range(4)])


def per_device(attn, output_gradient, down_weight, up_weight, adapter_of_row, lengths):
    width = attn.shape[1]
    me = lax.axis_index("tensor")
    slices = [
        lax.dynamic_slice_in_dim(output_gradient, (me ^ k) * width, width, 1) for k in range(4)
    ]
    pieces = [slices[0]] + [from_peer(slices[k], k) for k in (1, 2, 3)]

    (packed,) = call(
        pack_tables,
        [((8 * PEERS, LANES), BF16)],
        [VMEM, VMEM, SMEM],
        [((2 * PEERS, LANES), F32), ((8 * PEERS, LANES), F32)],
    )(down_weight, up_weight, adapter_of_row)
    tables = swap(packed)
    (picked,) = call(
        pick_rows,
        [((16 * PEERS, LANES), BF16)],
        [VMEM],
        [((8 * PEERS, LANES), F32), ((16 * PEERS, LANES), F32)],
    )(tables)
    picked = swap(picked)
    maps, grad, part = call(
        project,
        [((64, width), BF16), ((2 * BLOCK, width), BF16), ((32, 2 * BLOCK), F32)],
        [VMEM] * 6 + [SMEM],
    )(picked, attn, *pieces, me.astype(jnp.int32).reshape(1))
    parts = [part] + [from_peer(part, k) for k in (1, 2, 3)]
    attention_gradient, terms = call(
        expand,
        [((2 * BLOCK, width), BF16), ((16 * PEERS, LANES), BF16)],
        [VMEM] * 5 + [SMEM] + [VMEM] * 3,
    )(*parts, adapter_of_row.reshape(1, -1), lengths, maps, attn, grad)
    terms = swap(terms)
    (sums,) = call(
        add_up,
        [((4 * PEERS, LANES), F32)],
        [VMEM, VMEM],
        [((16 * PEERS, LANES), F32), ((8 * PEERS, LANES), F32)],
    )(terms, tables)
    sums = swap(sums)
    grad_a, grad_b = call(
        unpack, [((8, width), F32), ((8, width), F32)], [VMEM], [((2 * PEERS, LANES), F32)]
    )(sums)
    return attention_gradient, grad_a, grad_b


def solution(mesh):
    return jax.shard_map(
        per_device,
        mesh=mesh,
        in_specs=(
            P("dp", "tensor"),
            P(("dp", "tensor"), None),
            P("dp", "tensor"),
            P("dp", "tensor"),
            P("dp"),
            P("dp"),
        ),
        out_specs=(P("dp", "tensor"), P("dp", "tensor"), P("dp", "tensor")),
        check_vma=False,
    )
```

time: 1320 us -> 99.5 us (0.08)
  waiting for transfers between devices: 1270 us -> 15.4 us
  blocking collectives: 14.5 us -> 61.3 us
    all_gather x3 -> x0, waiting for transfers between devices: 635 us -> none  [the longest x1 300 us: per_device(): lax.all_gather(up_weight, 'dp', axis=0, tiled=True)]
    reduce_scatter x2 -> x0, waiting for transfers between devices: 633 us -> none  [the longest x1 319 us: per_device(): lax.psum_scatter(down_term, 'dp', scatter_dimension=0, tiled=True)]
    all_to_all x0 -> x3, blocking collectives: none -> 61.3 us  [swap(): return lax.all_to_all(chunks, 'dp', 0, 0, tiled=True).reshape(x.shape)]
    ppermute x0 -> x6, waiting for transfers between devices: none -> 15.4 us  [from_peer(): return lax.ppermute(x, 'tensor', [(i, i ^ k) for i in range(4)])]
    psum x1 -> x0, blocking collectives: 14.5 us -> none  [per_device(): outer_product = lax.psum(outer_part, 'tensor')]
  transfers between devices with their start and end apart: 5 -> 7, of which waited for: 5 -> 4; matrix products, arithmetic and copies ran while one was open for 1% -> 0% of each run, Pallas kernels for 0% -> 0%
where the time goes in v1:
time: 99.5 us; the launch traced here: 98.6 us
  blocking collectives  61.3 us (62%)
  waiting for transfers between devices  15.4 us (15%)
  starting transfers between devices  12.4 us (12%)
  Pallas kernels  5.07 us (5%)
  local copies, waits for them, and re-layouts  2.96 us (3%)
  between operations  1.4 us (1%)
    all_to_all x3, blocking collectives, swap(): return lax.all_to_all(chunks, 'dp', 0, 0, tiled=True).reshape(x.shape)  61.3 us
    ppermute x6, waiting for transfers between devices, from_peer(): return lax.ppermute(x, 'tensor', [(i, i ^ k) for i in range(4)])  15.4 us
    ppermute x6, starting transfers between devices, from_peer(): return lax.ppermute(x, 'tensor', [(i, i ^ k) for i in range(4)])  7.24 us
    all_to_all x1, starting transfers between devices, swap(): return lax.all_to_all(chunks, 'dp', 0, 0, tiled=True).reshape(x.shape)  5.19 us
    unnamed x12, local copies, waits for them, and re-layouts  2.88 us
  transfers between devices with their start and end apart: 7, of which 4 were waited for; matrix products, arithmetic and copies ran while one was open for 0% of the time, Pallas kernels for 0%

profile of v1, /device:TPU:2, one launch (start us, length us, event | category | flops | bytes accessed | tf_op | source)
XLA Modules:
  0.0 98.6 jit_solution(16223296831268940907)
XLA Ops:
  0.6 0.0 copy-start.1
  0.6 0.7 copy-done.1
  1.4 0.8 copy-done.2
  2.2 0.7 copy-done.3
  2.8 0.6 shard_map.85
  3.5 23.6 %all_to_all.20 = bf16[64,8,128]{2,1,0:T(8,128)(2,1)S(1)} all-to-all(bf16[64,8,128]{2,1,0:T(8,128)(2,1)S(1)} %bitcast.15), channel_id=1, replica_groups=mesh['dp'=64,'tensor'=4] {'dp'}, dimensions={0} | all-to-all | bytes 262144 | tf_op jit(solution)/shard_map/all_to_all | solution.py:142
  27.1 1.0 %shard_map.86 = bf16[1024,128]{1,0:T(8,128)(2,1)} custom-call(bf16[512,128]{1,0:T(8,128)(2,1)S(1)} %bitcast.10), custom_call_target="tpu_custom_call" | custom-call | tf_op jit(solution)/shard_map/pallas_call | solution.py:164
  28.1 5.2 %all-to-all-start.1 = ((bf16[64,16,128]{2,1,0:T(8,128)(2,1)}), bf16[64,16,128]{2,1,0:T(8,128)(2,1)S(1)}, u32[]{:S(2)}, u32[]{:S(2)}) async-start(bf16[64,16,128]{2,1,0:T(8,128)(2,1)} %bitcast.2), calls=%async_computation.1 | async-start | bytes 524288 | tf_op jit(solution)/shard_map/all_to_all | solution.py:142
  33.3 0.0 copy-done.5
  33.3 0.0 copy-start
  33.4 0.1 constant_dynamic-slice_fusion
  33.5 0.1 collective-permute-start.2
  33.6 2.2 %collective-permute-start = (bf16[64,2048]{1,0:T(8,128)(2,1)S(1)}, bf16[64,2048]{1,0:T(8,128)(2,1)S(1)}, u32[]{:S(2)}, u32[]{:S(2)}) collective-permute-start(bf16[64,2048]{1,0:T(8,128)(2,1)S(1)} %get-tuple-element.18), channel_id=1, source_target_pairs={{0,1},{1,0},{2,3},{3,2},{4,5},{5,4},{6,7},{7,6},{8,9},{9,8},{10,11... | collective-permute-start | bytes 786440 | tf_op jit(solution)/shard_map/ppermute | solution.py:146
  35.8 1.4 %collective-permute-start.1 = (bf16[64,2048]{1,0:T(8,128)(2,1)S(1)}, bf16[64,2048]{1,0:T(8,128)(2,1)S(1)}, u32[]{:S(2)}, u32[]{:S(2)}) collective-permute-start(bf16[64,2048]{1,0:T(8,128)(2,1)S(1)} %get-tuple-element.20), channel_id=1, source_target_pairs={{0,2},{1,3},{2,0},{3,1},{4,6},{5,7},{6,4},{7,5},{8,10},{9,11},{10,... | collective-permute-start | bytes 786440 | tf_op jit(solution)/shard_map/ppermute | solution.py:146
  37.2 8.1 %collective-permute-done.2.three_ref = bf16[64,2048]{1,0:T(8,128)(2,1)S(1)} collective-permute-done((bf16[64,2048]{1,0:T(8,128)(2,1)S(1)}, bf16[64,2048]{1,0:T(8,128)(2,1)S(1)}, u32[]{:S(2)}, u32[]{:S(2)}) %collective-permute-start.2) | collective-permute-done | bytes 262176 | tf_op jit(solution)/shard_map/ppermute | solution.py:146
  45.3 0.0 collective-permute-done.one_ref
  45.3 4.7 %collective-permute-done.1.two_ref = bf16[64,2048]{1,0:T(8,128)(2,1)S(1)} collective-permute-done((bf16[64,2048]{1,0:T(8,128)(2,1)S(1)}, bf16[64,2048]{1,0:T(8,128)(2,1)S(1)}, u32[]{:S(2)}, u32[]{:S(2)}) %collective-permute-start.1) | collective-permute-done | bytes 262176 | tf_op jit(solution)/shard_map/ppermute | solution.py:146
  50.0 0.0 all-to-all-done.1
  50.0 0.0 copy-done
  50.0 0.7 shard_map.87
  50.7 1.4 %collective-permute-start.5 = (f32[32,256]{1,0:T(8,128)S(1)}, f32[32,256]{1,0:T(8,128)S(1)}, u32[]{:S(2)}, u32[]{:S(2)}) collective-permute-start(f32[32,256]{1,0:T(8,128)S(1)} %get-tuple-element.10.own_ref), channel_id=1, source_target_pairs={{0,3},{1,2},{2,1},{3,0},{4,7},{5,6},{6,5},{7,4},{8,11},{9,10},{10,... | collective-permute-start | bytes 98312 | tf_op jit(solution)/shard_map/ppermute | solution.py:146
  52.1 2.1 %collective-permute-start.4 = (f32[32,256]{1,0:T(8,128)S(1)}, f32[32,256]{1,0:T(8,128)S(1)}, u32[]{:S(2)}, u32[]{:S(2)}) collective-permute-start(f32[32,256]{1,0:T(8,128)S(1)} %get-tuple-element.10.own_ref), channel_id=1, source_target_pairs={{0,2},{1,3},{2,0},{3,1},{4,6},{5,7},{6,4},{7,5},{8,10},{9,11},{10,... | collective-permute-start | bytes 98312 | tf_op jit(solution)/shard_map/ppermute | solution.py:146
  54.2 0.0 collective-permute-start.3
  54.9 0.8 collective-permute-done.5.three_ref
  55.6 1.9 %collective-permute-done.4.two_ref = f32[32,256]{1,0:T(8,128)S(1)} collective-permute-done((f32[32,256]{1,0:T(8,128)S(1)}, f32[32,256]{1,0:T(8,128)S(1)}, u32[]{:S(2)}, u32[]{:S(2)}) %collective-permute-start.4) | collective-permute-done | bytes 32800 | tf_op jit(solution)/shard_map/ppermute | solution.py:146
  57.5 0.0 collective-permute-done.3.one_ref
  57.5 0.7 copy-done.4
  58.2 1.7 %shard_map.88 = (bf16[256,2048]{1,0:T(8,128)(2,1)}, bf16[1024,128]{1,0:T(8,128)(2,1)S(1)}) custom-call(f32[32,256]{1,0:T(8,128)S(1)} %get-tuple-element.10.own_ref, f32[32,256]{1,0:T(8,128)S(1)} %collective-permute-done.3.one_ref, f32[32,256]{1,0:T(8,128)S(1)} %collective-permute-done.4.two_ref, f32[32,256]{1,0:T(8,128)S(1)} %collective-permute-done.5.three_ref, ...), custom_call_target="tpu_custom_call" | custom-call | tf_op jit(solution)/shard_map/pallas_call | solution.py:177
  59.9 22.5 %all_to_all.21 = bf16[64,16,128]{2,1,0:T(8,128)(2,1)S(1)} all-to-all(bf16[64,16,128]{2,1,0:T(8,128)(2,1)S(1)} %bitcast.17), channel_id=1, replica_groups=mesh['dp'=64,'tensor'=4] {'dp'}, dimensions={0} | all-to-all | bytes 524288 | tf_op jit(solution)/shard_map/all_to_all | solution.py:142
  82.4 0.3 shard_map.89
  82.8 15.1 %all_to_all.22 = f32[64,4,128]{2,1,0:T(4,128)S(1)} all-to-all(f32[64,4,128]{2,1,0:T(4,128)S(1)} %bitcast.16), channel_id=1, replica_groups=mesh['dp'=64,'tensor'=4] {'dp'}, dimensions={0} | all-to-all | bytes 262144 | tf_op jit(solution)/shard_map/all_to_all | solution.py:142
  97.9 0.7 shard_map.90
  (4 shorter events, 0.0 us)
Async XLA Ops:
  0.6 0.8 copy-start.1
  1.4 0.8 copy-start.2
  2.1 0.7 copy-start.3
  2.8 30.5 %copy-start.5 = (bf16[64,8192]{1,0:T(8,128)(2,1)S(1)}, bf16[64,8192]{1,0:T(8,128)(2,1)}, u32[]{:S(2)}) copy-start(bf16[64,8192]{1,0:T(8,128)(2,1)} %param.7) | copy-start | bytes 3145732
  28.1 21.9 %all-to-all-start.1 = ((bf16[64,16,128]{2,1,0:T(8,128)(2,1)}), bf16[64,16,128]{2,1,0:T(8,128)(2,1)S(1)}, u32[]{:S(2)}, u32[]{:S(2)}) async-start(bf16[64,16,128]{2,1,0:T(8,128)(2,1)} %bitcast.2), calls=%async_computation.1 | async-start | bytes 524288 | tf_op jit(solution)/shard_map/all_to_all | solution.py:142
  33.3 16.6 %copy-start = (bf16[256,2048]{1,0:T(8,128)(2,1)S(1)}, bf16[256,2048]{1,0:T(8,128)(2,1)}, u32[]{:S(2)}) copy-start(bf16[256,2048]{1,0:T(8,128)(2,1)} %attn_ref.3) | copy-start | bytes 3145732
  33.5 11.8 %collective-permute-start.2 = (bf16[64,2048]{1,0:T(8,128)(2,1)S(1)}, bf16[64,2048]{1,0:T(8,128)(2,1)S(1)}, u32[]{:S(2)}, u32[]{:S(2)}) collective-permute-start(bf16[64,2048]{1,0:T(8,128)(2,1)S(1)} %get-tuple-element.17), channel_id=1, source_target_pairs={{0,3},{1,2},{2,1},{3,0},{4,7},{5,6},{6,5},{7,4},{8,11},{9,10},{10,... | collective-permute-start | bytes 786440 | tf_op jit(solution)/shard_map/ppermute | solution.py:146
  33.6 11.7 %collective-permute-start = (bf16[64,2048]{1,0:T(8,128)(2,1)S(1)}, bf16[64,2048]{1,0:T(8,128)(2,1)S(1)}, u32[]{:S(2)}, u32[]{:S(2)}) collective-permute-start(bf16[64,2048]{1,0:T(8,128)(2,1)S(1)} %get-tuple-element.18), channel_id=1, source_target_pairs={{0,1},{1,0},{2,3},{3,2},{4,5},{5,4},{6,7},{7,6},{8,9},{9,8},{10,11... | collective-permute-start | bytes 786440 | tf_op jit(solution)/shard_map/ppermute | solution.py:146
  35.8 14.2 %collective-permute-start.1 = (bf16[64,2048]{1,0:T(8,128)(2,1)S(1)}, bf16[64,2048]{1,0:T(8,128)(2,1)S(1)}, u32[]{:S(2)}, u32[]{:S(2)}) collective-permute-start(bf16[64,2048]{1,0:T(8,128)(2,1)S(1)} %get-tuple-element.20), channel_id=1, source_target_pairs={{0,2},{1,3},{2,0},{3,1},{4,6},{5,7},{6,4},{7,5},{8,10},{9,11},{10,... | collective-permute-start | bytes 786440 | tf_op jit(solution)/shard_map/ppermute | solution.py:146
  50.7 4.9 %collective-permute-start.5 = (f32[32,256]{1,0:T(8,128)S(1)}, f32[32,256]{1,0:T(8,128)S(1)}, u32[]{:S(2)}, u32[]{:S(2)}) collective-permute-start(f32[32,256]{1,0:T(8,128)S(1)} %get-tuple-element.10.own_ref), channel_id=1, source_target_pairs={{0,3},{1,2},{2,1},{3,0},{4,7},{5,6},{6,5},{7,4},{8,11},{9,10},{10,... | collective-permute-start | bytes 98312 | tf_op jit(solution)/shard_map/ppermute | solution.py:146
  52.1 5.4 %collective-permute-start.4 = (f32[32,256]{1,0:T(8,128)S(1)}, f32[32,256]{1,0:T(8,128)S(1)}, u32[]{:S(2)}, u32[]{:S(2)}) collective-permute-start(f32[32,256]{1,0:T(8,128)S(1)} %get-tuple-element.10.own_ref), channel_id=1, source_target_pairs={{0,2},{1,3},{2,0},{3,1},{4,6},{5,7},{6,4},{7,5},{8,10},{9,11},{10,... | collective-permute-start | bytes 98312 | tf_op jit(solution)/shard_map/ppermute | solution.py:146
  54.2 3.3 %collective-permute-start.3 = (f32[32,256]{1,0:T(8,128)S(1)}, f32[32,256]{1,0:T(8,128)S(1)}, u32[]{:S(2)}, u32[]{:S(2)}) collective-permute-start(f32[32,256]{1,0:T(8,128)S(1)} %get-tuple-element.10.own_ref), channel_id=1, source_target_pairs={{0,1},{1,0},{2,3},{3,2},{4,5},{5,4},{6,7},{7,6},{8,9},{9,8},{10,11... | collective-permute-start | bytes 98312 | tf_op jit(solution)/shard_map/ppermute | solution.py:146
  57.5 0.7 copy-start.4

commit v2 on v1

--- a/solution.py
+++ b/solution.py
@@ -17,6 +17,7 @@
 adapter_scale = 2.0
 
 VMEM = pl.BlockSpec(memory_space=pltpu.VMEM)
+ANY = pl.BlockSpec(memory_space=pl.ANY)
 SMEM = pl.BlockSpec(memory_space=pltpu.SMEM)
 PARAMS = pltpu.CompilerParams(vmem_limit_bytes=40 * 1024 * 1024)
 
@@ -25,16 +26,33 @@
     return pl.ds(first, size, stride=stride)
 
 
-def pack_tables(down_ref, up_ref, label_ref, out_ref, rows_f, out_f):
+def pack_tables(
+    down_hbm, up_hbm, label_hbm, length_hbm, out_ref, live_ref, down_ref, up_ref, label_ref, length_ref, rows_f, out_f, sems
+):
+    copies = [
+        pltpu.make_async_copy(src, dst, sems.at[n])
+        for n, (src, dst) in enumerate(
+            ((label_hbm, label_ref), (length_hbm, length_ref), (down_hbm, down_ref), (up_hbm, up_ref))
+        )
+    ]
+    for copy in copies:
+        copy.start()
+    for b in range(2):
+        out_f[rows_of(6 + b, PEERS, 8), :] = jnp.zeros((PEERS, LANES), F32)
+    copies[0].wait()
+    labels = label_ref[...]
+    for b in range(2):
+        which = jnp.maximum(labels[b:b + 1, 0:1], 0).astype(F32)
+        out_f[rows_of(4 + b, PEERS, 8), :] = jnp.broadcast_to(which, (PEERS, LANES))
+    copies[1].wait()
+    offset = lax.broadcasted_iota(jnp.int32, (2, BLOCK), 0) * BLOCK + lax.broadcasted_iota(jnp.int32, (2, BLOCK), 1)
+    live_ref[...] = jnp.where((labels >= 0) & (offset < length_ref[0]), 1.0, 0.0)
     for m, map_ref in enumerate((down_ref, up_ref)):
+        copies[2 + m].wait()
         for c in range(BANDS):
             rows_f[c * 8:(c + 1) * 8, :] = map_ref[:, c * LANES:(c + 1) * LANES].astype(F32)
         for i in range(2):
             out_f[rows_of(2 * m + i, PEERS, 8), :] = rows_f[rows_of(i, PEERS, 2), :]
-    for b in range(2):
-        which = jnp.maximum(label_ref[b * BLOCK], 0).astype(F32)
-        out_f[rows_of(4 + b, PEERS, 8), :] = jnp.full((PEERS, LANES), which, F32)
-        out_f[rows_of(6 + b, PEERS, 8), :] = jnp.zeros((PEERS, LANES), F32)
     out_ref[...] = out_f[...].astype(BF16)
 
 
@@ -71,34 +89,37 @@
         part_ref[:, block] = jnp.where((row & 2) == 0, inner, outer)
 
 
-def expand(own_ref, one_ref, two_ref, three_ref, label_ref, length_ref, maps_ref, attn_ref, grad_ref, back_ref, term_ref):
+def make_terms(own_ref, one_ref, two_ref, three_ref, live_ref, attn_ref, grad_ref, ranks_ref, term_ref):
     total = (own_ref[...] + one_ref[...]) + (two_ref[...] + three_ref[...])
-    offset = lax.broadcasted_iota(jnp.int32, (1, 2 * BLOCK), 1)
-    live = (label_ref[...] >= 0) & (offset < length_ref[0])
-    total = jnp.where(live, total, 0.0).astype(BF16)
-    row = lax.broadcasted_iota(jnp.int32, (32, BLOCK), 0)
-    row_w = lax.broadcasted_iota(jnp.int32, (32, LANES), 0)
-    over_first = (((0,), (0,)), ((), ()))
+    row = lax.broadcasted_iota(jnp.int32, (32, LANES), 0)
     terms = []
     for b in range(2):
         block = slice(b * BLOCK, (b + 1) * BLOCK)
-        ranks = total[:, block]
+        ranks = jnp.where(live_ref[b:b + 1, :] > 0, total[:, block], 0.0).astype(BF16)
+        ranks_ref[:, block] = ranks
         down = jnp.dot(ranks, attn_ref[block, :], preferred_element_type=F32)
         up = jnp.dot(ranks, grad_ref[block, :], preferred_element_type=F32)
         terms.append((down, up))
-        shifted = pltpu.roll(ranks.astype(F32), 30, 0)
-        outer = jnp.where((row & 2) == 0, shifted, 0.0).astype(BF16)
-        back = lax.dot_general(outer, maps_ref[b * 32:(b + 1) * 32, :], over_first, preferred_element_type=F32)
-        back_ref[block, :] = (adapter_scale * back).astype(BF16)
     for c in range(BANDS):
         band = slice(c * LANES, (c + 1) * LANES)
         both = [
-            adapter_scale * jnp.where((row_w & 2) == 0, up[:, band], down[:, band])
+            adapter_scale * jnp.where((row & 2) == 0, up[:, band], down[:, band])
             for down, up in terms
         ]
         for q in range(QUARTERS):
             pair = jnp.concatenate([one[q * 8:(q + 1) * 8] for one in both], axis=0)
             term_ref[c * 64 + q * 16:c * 64 + (q + 1) * 16, :] = pair.astype(BF16)
+
+
+def go_back(ranks_ref, maps_ref, back_ref):
+    row = lax.broadcasted_iota(jnp.int32, (32, BLOCK), 0)
+    over_first = (((0,), (0,)), ((), ()))
+    for b in range(2):
+        block = slice(b * BLOCK, (b + 1) * BLOCK)
+        shifted = pltpu.roll(ranks_ref[:, block].astype(F32), 30, 0)
+        outer = jnp.where((row & 2) == 0, shifted, 0.0).astype(BF16)
+        back = lax.dot_general(outer, maps_ref[b * 32:(b + 1) * 32, :], over_first, preferred_element_type=F32)
+        back_ref[block, :] = (adapter_scale * back).astype(BF16)
 
 
 def add_up(in_ref, ids_ref, out_ref, in_f, ids_f):
@@ -126,14 +147,15 @@
             map_ref[:, c * LANES:(c + 1) * LANES] = rows_f[c * 8:(c + 1) * 8, :]
 
 
-def call(kernel, outs, specs, scratch=()):
+def call(kernel, outs, specs, scratch=(), cost=None):
     return pl.pallas_call(
         kernel,
         out_shape=[jax.ShapeDtypeStruct(shape, dtype) for shape, dtype in outs],
         in_specs=specs,
         out_specs=[VMEM] * len(outs),
-        scratch_shapes=[pltpu.VMEM(shape, dtype) for shape, dtype in scratch],
+        scratch_shapes=scratch,
         compiler_params=PARAMS,
+        cost_estimate=cost,
     )
 
 
@@ -154,18 +176,27 @@
     ]
     pieces = [slices[0]] + [from_peer(slices[k], k) for k in (1, 2, 3)]
 
-    (packed,) = call(
+    packed, live = call(
         pack_tables,
-        [((8 * PEERS, LANES), BF16)],
-        [VMEM, VMEM, SMEM],
-        [((2 * PEERS, LANES), F32), ((8 * PEERS, LANES), F32)],
-    )(down_weight, up_weight, adapter_of_row)
+        [((8 * PEERS, LANES), BF16), ((2, BLOCK), F32)],
+        [ANY] * 4,
+        [
+            pltpu.VMEM((8, width), BF16),
+            pltpu.VMEM((8, width), BF16),
+            pltpu.VMEM((2, BLOCK), jnp.int32),
+            pltpu.SMEM((1,), jnp.int32),
+            pltpu.VMEM((2 * PEERS, LANES), F32),
+            pltpu.VMEM((8 * PEERS, LANES), F32),
+            pltpu.SemaphoreType.DMA((4,)),
+        ],
+    )(down_weight, up_weight, adapter_of_row.reshape(2, BLOCK), lengths)
     tables = swap(packed)
+    tables, pieces[1], pieces[3] = lax.optimization_barrier((tables, pieces[1], pieces[3]))
     (picked,) = call(
         pick_rows,
         [((16 * PEERS, LANES), BF16)],
         [VMEM],
-        [((8 * PEERS, LANES), F32), ((16 * PEERS, LANES), F32)],
+        [pltpu.VMEM((8 * PEERS, LANES), F32), pltpu.VMEM((16 * PEERS, LANES), F32)],
     )(tables)
     picked = swap(picked)
     maps, grad, part = call(
@@ -174,21 +205,30 @@
         [VMEM] * 6 + [SMEM],
     )(picked, attn, *pieces, me.astype(jnp.int32).reshape(1))
     parts = [part] + [from_peer(part, k) for k in (1, 2, 3)]
-    attention_gradient, terms = call(
-        expand,
-        [((2 * BLOCK, width), BF16), ((16 * PEERS, LANES), BF16)],
-        [VMEM] * 5 + [SMEM] + [VMEM] * 3,
-    )(*parts, adapter_of_row.reshape(1, -1), lengths, maps, attn, grad)
+    ranks, terms = call(
+        make_terms,
+        [((32, 2 * BLOCK), BF16), ((16 * PEERS, LANES), BF16)],
+        [VMEM] * 7,
+    )(*parts, live, attn, grad)
     terms = swap(terms)
+    (attention_gradient,) = call(
+        go_back,
+        [((2 * BLOCK, width), BF16)],
+        [VMEM] * 2,
+        cost=pl.CostEstimate(flops=2 * 32 * 256 * 2048, bytes_accessed=2 << 20, transcendentals=0),
+    )(ranks, maps)
     (sums,) = call(
         add_up,
         [((4 * PEERS, LANES), F32)],
         [VMEM, VMEM],
-        [((16 * PEERS, LANES), F32), ((8 * PEERS, LANES), F32)],
+        [pltpu.VMEM((16 * PEERS, LANES), F32), pltpu.VMEM((8 * PEERS, LANES), F32)],
     )(terms, tables)
     sums = swap(sums)
     grad_a, grad_b = call(
-        unpack, [((8, width), F32), ((8, width), F32)], [VMEM], [((2 * PEERS, LANES), F32)]
+        unpack,
+        [((8, width), F32), ((8, width), F32)],
+        [VMEM],
+        [pltpu.VMEM((2 * PEERS, LANES), F32)],
     )(sums)
     return attention_gradient, grad_a, grad_b
 

time: 99.5 us -> 94.7 us (0.952)
  blocking collectives: 61.3 us -> 46.5 us
  waiting for transfers between devices: 15.4 us -> 22 us
  starting transfers between devices: 12.4 us -> 17.3 us
  local copies, waits for them, and re-layouts: 2.96 us -> 1.29 us
    all_to_all x3 -> x2, blocking collectives: 61.3 us -> 46.5 us  [swap(): return lax.all_to_all(chunks, 'dp', 0, 0, tiled=True).reshape(x.shape)]
    all_to_all x1 -> x2, waiting for transfers between devices: 0.01 us -> 10.9 us  [swap(): return lax.all_to_all(chunks, 'dp', 0, 0, tiled=True).reshape(x.shape)]
    all_to_all x1 -> x2, starting transfers between devices: 5.19 us -> 10 us  [swap(): return lax.all_to_all(chunks, 'dp', 0, 0, tiled=True).reshape(x.shape)]
    ppermute x6, waiting for transfers between devices: 15.4 us -> 11.1 us  [from_peer(): return lax.ppermute(x, 'tensor', [(i, i ^ k) for i in range(4)])]
    unnamed x12 -> x8, local copies, waits for them, and re-layouts: 2.88 us -> 0.02 us
    dynamic_slice x1, local copies, waits for them, and re-layouts: 0.09 us -> 1.27 us  [per_device(): lax.dynamic_slice_in_dim(output_gradient, (me ^ k) * width, width, 1)]
    pallas_call x5 -> x6, Pallas kernels: 4.35 us -> 5.23 us  [the longest x1 1.43 us: per_device(): call(go_back, [((2 * BLOCK, width), BF16)], [VMEM] * 2, cost=pl.CostEstim...]
  transfers between devices with their start and end apart: 7 -> 8, of which waited for: 4 -> 5; matrix products, arithmetic and copies ran while one was open for 0% -> 0% of each run, Pallas kernels for 0% -> 2%
where the time goes in v2:
time: 94.7 us; the launch traced here: 94.4 us
  blocking collectives  46.5 us (49%)
  waiting for transfers between devices  22 us (23%)
  starting transfers between devices  17.3 us (18%)
  Pallas kernels  5.94 us (6%)
  between operations  1.43 us (2%)
  local copies, waits for them, and re-layouts  1.29 us (1%)
    all_to_all x2, blocking collectives, swap(): return lax.all_to_all(chunks, 'dp', 0, 0, tiled=True).reshape(x.shape)  46.5 us
    ppermute x6, waiting for transfers between devices, from_peer(): return lax.ppermute(x, 'tensor', [(i, i ^ k) for i in range(4)])  11.1 us
    all_to_all x2, waiting for transfers between devices, swap(): return lax.all_to_all(chunks, 'dp', 0, 0, tiled=True).reshape(x.shape)  10.9 us
    all_to_all x2, starting transfers between devices, swap(): return lax.all_to_all(chunks, 'dp', 0, 0, tiled=True).reshape(x.shape)  10 us
    ppermute x6, starting transfers between devices, from_peer(): return lax.ppermute(x, 'tensor', [(i, i ^ k) for i in range(4)])  7.26 us
  transfers between devices with their start and end apart: 8, of which 5 were waited for; matrix products, arithmetic and copies ran while one was open for 0% of the time, Pallas kernels for 2%

profile of v2, /device:TPU:2, one launch (start us, length us, event | category | flops | bytes accessed | tf_op | source)
XLA Modules:
  0.0 94.4 jit_solution(1076423377974861124)
XLA Ops:
  0.7 0.0 copy-start.1
  0.7 0.0 copy-start.2
  0.7 0.0 copy-start.3
  0.7 1.3 %constant_dynamic-slice_fusion = (bf16[64,2048]{1,0:T(8,128)(2,1)S(1)}, bf16[64,2048]{1,0:T(8,128)(2,1)S(1)}, bf16[64,2048]{1,0:T(8,128)(2,1)S(1)}, bf16[64,2048]{1,0:T(8,128)(2,1)S(1)}) fusion(bf16[64,8192]{1,0:T(8,128)(2,1)} %param.7, s32[]{:T(128)S(6)} %select_n.15, s32[]{:T(128)S(6)} %select_n.13, s32[]{:T(128)S(6)} %select_n.12, s32[]{:T(128)S(6)} %select_n.14), kind=kLoop, calls=%fused_computation | loop fusion | bytes 2097168 | tf_op jit(solution)/shard_map/dynamic_slice | solution.py:175
  2.0 0.0 copy-start
  2.0 1.7 %collective-permute-start.1 = (bf16[64,2048]{1,0:T(8,128)(2,1)S(1)}, bf16[64,2048]{1,0:T(8,128)(2,1)S(1)}, u32[]{:S(2)}, u32[]{:S(2)}) collective-permute-start(bf16[64,2048]{1,0:T(8,128)(2,1)S(1)} %get-tuple-element.28), channel_id=1, source_target_pairs={{0,3},{1,2},{2,1},{3,0},{4,7},{5,6},{6,5},{7,4},{8,11},{9,10},{10,... | collective-permute-start | bytes 786440 | tf_op jit(solution)/shard_map/ppermute | solution.py:168
  3.6 0.7 collective-permute-start
  5.0 0.0 copy-done.1
  5.0 0.6 shard_map.85
  5.6 23.8 %all_to_all.20 = bf16[64,8,128]{2,1,0:T(8,128)(2,1)S(1)} all-to-all(bf16[64,8,128]{2,1,0:T(8,128)(2,1)S(1)} %bitcast.16), channel_id=1, replica_groups=mesh['dp'=64,'tensor'=4] {'dp'}, dimensions={0} | all-to-all | bytes 262144 | tf_op jit(solution)/shard_map/all_to_all | solution.py:164
  29.4 0.0 collective-permute-done.1.three_ref
  29.4 0.0 collective-permute-done.one_ref
  29.4 1.0 %shard_map.86 = bf16[1024,128]{1,0:T(8,128)(2,1)} custom-call(bf16[512,128]{1,0:T(8,128)(2,1)S(1)} %bitcast.10), custom_call_target="tpu_custom_call" | custom-call | tf_op jit(solution)/shard_map/pallas_call | solution.py:195
  30.5 5.2 %all-to-all-start.1 = ((bf16[64,16,128]{2,1,0:T(8,128)(2,1)}), bf16[64,16,128]{2,1,0:T(8,128)(2,1)S(1)}, u32[]{:S(2)}, u32[]{:S(2)}) async-start(bf16[64,16,128]{2,1,0:T(8,128)(2,1)} %bitcast.3), calls=%async_computation.1 | async-start | bytes 524288 | tf_op jit(solution)/shard_map/all_to_all | solution.py:164
  35.6 1.5 %collective-permute-start.2 = (bf16[64,2048]{1,0:T(8,128)(2,1)S(1)}, bf16[64,2048]{1,0:T(8,128)(2,1)S(1)}, u32[]{:S(2)}, u32[]{:S(2)}) collective-permute-start(bf16[64,2048]{1,0:T(8,128)(2,1)S(1)} %get-tuple-element.27), channel_id=1, source_target_pairs={{0,2},{1,3},{2,0},{3,1},{4,6},{5,7},{6,4},{7,5},{8,10},{9,11},{10,... | collective-permute-start | bytes 786440 | tf_op jit(solution)/shard_map/ppermute | solution.py:168
  37.1 8.9 %collective-permute-done.2.two_ref = bf16[64,2048]{1,0:T(8,128)(2,1)S(1)} collective-permute-done((bf16[64,2048]{1,0:T(8,128)(2,1)S(1)}, bf16[64,2048]{1,0:T(8,128)(2,1)S(1)}, u32[]{:S(2)}, u32[]{:S(2)}) %collective-permute-start.2) | collective-permute-done | bytes 262176 | tf_op jit(solution)/shard_map/ppermute | solution.py:168
  46.0 1.8 %all-to-all-done.1 = bf16[64,16,128]{2,1,0:T(8,128)(2,1)S(1)} async-done(((bf16[64,16,128]{2,1,0:T(8,128)(2,1)}), bf16[64,16,128]{2,1,0:T(8,128)(2,1)S(1)}, u32[]{:S(2)}, u32[]{:S(2)}) %all-to-all-start.1) | async-done | bytes 262176 | tf_op jit(solution)/shard_map/all_to_all | solution.py:164
  47.8 0.0 copy-done
  47.8 0.7 shard_map.87
  48.5 0.1 collective-permute-start.5
  48.6 1.5 %collective-permute-start.4 = (f32[32,256]{1,0:T(8,128)S(1)}, f32[32,256]{1,0:T(8,128)S(1)}, u32[]{:S(2)}, u32[]{:S(2)}) collective-permute-start(f32[32,256]{1,0:T(8,128)S(1)} %get-tuple-element.19.own_ref), channel_id=1, source_target_pairs={{0,2},{1,3},{2,0},{3,1},{4,6},{5,7},{6,4},{7,5},{8,10},{9,11},{10,... | collective-permute-start | bytes 98312 | tf_op jit(solution)/shard_map/ppermute | solution.py:168
  50.1 1.9 %collective-permute-start.3 = (f32[32,256]{1,0:T(8,128)S(1)}, f32[32,256]{1,0:T(8,128)S(1)}, u32[]{:S(2)}, u32[]{:S(2)}) collective-permute-start(f32[32,256]{1,0:T(8,128)S(1)} %get-tuple-element.19.own_ref), channel_id=1, source_target_pairs={{0,1},{1,0},{2,3},{3,2},{4,5},{5,4},{6,7},{7,6},{8,9},{9,8},{10,11... | collective-permute-start | bytes 98312 | tf_op jit(solution)/shard_map/ppermute | solution.py:168
  52.0 1.5 %collective-permute-done.5.three_ref = f32[32,256]{1,0:T(8,128)S(1)} collective-permute-done((f32[32,256]{1,0:T(8,128)S(1)}, f32[32,256]{1,0:T(8,128)S(1)}, u32[]{:S(2)}, u32[]{:S(2)}) %collective-permute-start.5) | collective-permute-done | bytes 32800 | tf_op jit(solution)/shard_map/ppermute | solution.py:168
  53.5 0.7 collective-permute-done.4.two_ref
  54.1 0.0 collective-permute-done.3.one_ref
  54.2 0.4 shard_map.88
  54.6 22.7 %all_to_all.21 = bf16[64,16,128]{2,1,0:T(8,128)(2,1)S(1)} all-to-all(bf16[64,16,128]{2,1,0:T(8,128)(2,1)S(1)} %bitcast.15), channel_id=1, replica_groups=mesh['dp'=64,'tensor'=4] {'dp'}, dimensions={0} | all-to-all | bytes 524288 | tf_op jit(solution)/shard_map/all_to_all | solution.py:164
  77.3 1.0 %shard_map.90 = f32[256,128]{1,0:T(8,128)} custom-call(bf16[1024,128]{1,0:T(8,128)(2,1)S(1)} %bitcast.13, bf16[512,128]{1,0:T(8,128)(2,1)S(1)} %bitcast.11), custom_call_target="tpu_custom_call" | custom-call | tf_op jit(solution)/shard_map/pallas_call | solution.py:220
  78.3 4.9 %all-to-all-start.3 = ((f32[64,4,128]{2,1,0:T(4,128)}), f32[64,4,128]{2,1,0:T(4,128)S(1)}, u32[]{:S(2)}, u32[]{:S(2)}) async-start(f32[64,4,128]{2,1,0:T(4,128)} %bitcast.8), calls=%async_computation.3 | async-start | bytes 262144 | tf_op jit(solution)/shard_map/all_to_all | solution.py:164
  83.1 1.4 %shard_map.89 = bf16[256,2048]{1,0:T(8,128)(2,1)} custom-call(bf16[32,256]{1,0:T(8,128)(2,1)S(1)} %get-tuple-element.22.ranks_ref, bf16[64,2048]{1,0:T(8,128)(2,1)S(1)} %get-tuple-element.23.maps_ref), custom_call_target="tpu_custom_call" | custom-call | flops 33554432 | bytes 2097152 | tf_op jit(solution)/shard_map/pallas_call | solution.py:214
  84.6 9.2 %all-to-all-done.3 = f32[64,4,128]{2,1,0:T(4,128)S(1)} async-done(((f32[64,4,128]{2,1,0:T(4,128)}), f32[64,4,128]{2,1,0:T(4,128)S(1)}, u32[]{:S(2)}, u32[]{:S(2)}) %all-to-all-start.3) | async-done | bytes 131104 | tf_op jit(solution)/shard_map/all_to_all | solution.py:164
  93.7 0.7 shard_map.91
  (2 shorter events, 0.0 us)
Async XLA Ops:
  0.7 4.3 %copy-start.1 = (bf16[8,2048]{1,0:T(8,128)(2,1)S(1)}, bf16[8,2048]{1,0:T(8,128)(2,1)}, u32[]{:S(2)}) copy-start(bf16[8,2048]{1,0:T(8,128)(2,1)} %down_hbm.1) | copy-start | bytes 98308
  0.7 4.3 %copy-start.2 = (bf16[8,2048]{1,0:T(8,128)(2,1)S(1)}, bf16[8,2048]{1,0:T(8,128)(2,1)}, u32[]{:S(2)}) copy-start(bf16[8,2048]{1,0:T(8,128)(2,1)} %up_hbm.1) | copy-start | bytes 98308
  0.7 4.3 %copy-start.3 = (s32[256]{0:T(256)S(1)}, s32[256]{0:T(256)}, u32[]{:S(2)}) copy-start(s32[256]{0:T(256)} %param.10) | copy-start | bytes 3076
  2.0 45.8 %copy-start = (bf16[256,2048]{1,0:T(8,128)(2,1)S(1)}, bf16[256,2048]{1,0:T(8,128)(2,1)}, u32[]{:S(2)}) copy-start(bf16[256,2048]{1,0:T(8,128)(2,1)} %attn_ref.3) | copy-start | bytes 3145732
  2.0 27.4 %collective-permute-start.1 = (bf16[64,2048]{1,0:T(8,128)(2,1)S(1)}, bf16[64,2048]{1,0:T(8,128)(2,1)S(1)}, u32[]{:S(2)}, u32[]{:S(2)}) collective-permute-start(bf16[64,2048]{1,0:T(8,128)(2,1)S(1)} %get-tuple-element.28), channel_id=1, source_target_pairs={{0,3},{1,2},{2,1},{3,0},{4,7},{5,6},{6,5},{7,4},{8,11},{9,10},{10,... | collective-permute-start | bytes 786440 | tf_op jit(solution)/shard_map/ppermute | solution.py:168
  3.6 25.8 %collective-permute-start = (bf16[64,2048]{1,0:T(8,128)(2,1)S(1)}, bf16[64,2048]{1,0:T(8,128)(2,1)S(1)}, u32[]{:S(2)}, u32[]{:S(2)}) collective-permute-start(bf16[64,2048]{1,0:T(8,128)(2,1)S(1)} %get-tuple-element.29), channel_id=1, source_target_pairs={{0,1},{1,0},{2,3},{3,2},{4,5},{5,4},{6,7},{7,6},{8,9},{9,8},{10,11... | collective-permute-start | bytes 786440 | tf_op jit(solution)/shard_map/ppermute | solution.py:168
  30.5 17.4 %all-to-all-start.1 = ((bf16[64,16,128]{2,1,0:T(8,128)(2,1)}), bf16[64,16,128]{2,1,0:T(8,128)(2,1)S(1)}, u32[]{:S(2)}, u32[]{:S(2)}) async-start(bf16[64,16,128]{2,1,0:T(8,128)(2,1)} %bitcast.3), calls=%async_computation.1 | async-start | bytes 524288 | tf_op jit(solution)/shard_map/all_to_all | solution.py:164
  35.6 10.4 %collective-permute-start.2 = (bf16[64,2048]{1,0:T(8,128)(2,1)S(1)}, bf16[64,2048]{1,0:T(8,128)(2,1)S(1)}, u32[]{:S(2)}, u32[]{:S(2)}) collective-permute-start(bf16[64,2048]{1,0:T(8,128)(2,1)S(1)} %get-tuple-element.27), channel_id=1, source_target_pairs={{0,2},{1,3},{2,0},{3,1},{4,6},{5,7},{6,4},{7,5},{8,10},{9,11},{10,... | collective-permute-start | bytes 786440 | tf_op jit(solution)/shard_map/ppermute | solution.py:168
  48.5 4.9 %collective-permute-start.5 = (f32[32,256]{1,0:T(8,128)S(1)}, f32[32,256]{1,0:T(8,128)S(1)}, u32[]{:S(2)}, u32[]{:S(2)}) collective-permute-start(f32[32,256]{1,0:T(8,128)S(1)} %get-tuple-element.19.own_ref), channel_id=1, source_target_pairs={{0,3},{1,2},{2,1},{3,0},{4,7},{5,6},{6,5},{7,4},{8,11},{9,10},{10,... | collective-permute-start | bytes 98312 | tf_op jit(solution)/shard_map/ppermute | solution.py:168
  48.6 5.5 %collective-permute-start.4 = (f32[32,256]{1,0:T(8,128)S(1)}, f32[32,256]{1,0:T(8,128)S(1)}, u32[]{:S(2)}, u32[]{:S(2)}) collective-permute-start(f32[32,256]{1,0:T(8,128)S(1)} %get-tuple-element.19.own_ref), channel_id=1, source_target_pairs={{0,2},{1,3},{2,0},{3,1},{4,6},{5,7},{6,4},{7,5},{8,10},{9,11},{10,... | collective-permute-start | bytes 98312 | tf_op jit(solution)/shard_map/ppermute | solution.py:168
  50.1 4.0 %collective-permute-start.3 = (f32[32,256]{1,0:T(8,128)S(1)}, f32[32,256]{1,0:T(8,128)S(1)}, u32[]{:S(2)}, u32[]{:S(2)}) collective-permute-start(f32[32,256]{1,0:T(8,128)S(1)} %get-tuple-element.19.own_ref), channel_id=1, source_target_pairs={{0,1},{1,0},{2,3},{3,2},{4,5},{5,4},{6,7},{7,6},{8,9},{9,8},{10,11... | collective-permute-start | bytes 98312 | tf_op jit(solution)/shard_map/ppermute | solution.py:168
  78.3 15.5 %all-to-all-start.3 = ((f32[64,4,128]{2,1,0:T(4,128)}), f32[64,4,128]{2,1,0:T(4,128)S(1)}, u32[]{:S(2)}, u32[]{:S(2)}) async-start(f32[64,4,128]{2,1,0:T(4,128)} %bitcast.8), calls=%async_computation.3 | async-start | bytes 262144 | tf_op jit(solution)/shard_map/all_to_all | solution.py:164

commit v3 on v2

--- a/solution.py
+++ b/solution.py
@@ -19,7 +19,7 @@
 VMEM = pl.BlockSpec(memory_space=pltpu.VMEM)
 ANY = pl.BlockSpec(memory_space=pl.ANY)
 SMEM = pl.BlockSpec(memory_space=pltpu.SMEM)
-PARAMS = pltpu.CompilerParams(vmem_limit_bytes=40 * 1024 * 1024)
+MIB = 1024 * 1024
 
 
 def rows_of(first, size, stride):
@@ -27,14 +27,16 @@
 
 
 def pack_tables(
-    down_hbm, up_hbm, label_hbm, length_hbm, out_ref, live_ref, down_ref, up_ref, label_ref, length_ref, rows_f, out_f, sems
+    place_ref, down_hbm, up_hbm, label_hbm, length_hbm, grad_hbm,
+    out_ref, own_ref, one_ref, two_ref, three_ref,
+    down_ref, up_ref, label_ref, length_ref, rows_f, out_f, sems
 ):
-    copies = [
-        pltpu.make_async_copy(src, dst, sems.at[n])
-        for n, (src, dst) in enumerate(
-            ((label_hbm, label_ref), (length_hbm, length_ref), (down_hbm, down_ref), (up_hbm, up_ref))
-        )
-    ]
+    width = own_ref.shape[1]
+    moves = [(label_hbm, label_ref), (length_hbm, length_ref), (down_hbm, down_ref), (up_hbm, up_ref)]
+    for k, piece in ((3, three_ref), (2, two_ref), (1, one_ref), (0, own_ref)):
+        first = pl.multiple_of(lax.bitwise_xor(place_ref[0], k) * width, width)
+        moves.append((grad_hbm.at[:, pl.ds(first, width)], piece.at[pl.ds(0, 64), :]))
+    copies = [pltpu.make_async_copy(src, dst, sems.at[n]) for n, (src, dst) in enumerate(moves)]
     for copy in copies:
         copy.start()
     for b in range(2):
@@ -46,7 +48,10 @@
         out_f[rows_of(4 + b, PEERS, 8), :] = jnp.broadcast_to(which, (PEERS, LANES))
     copies[1].wait()
     offset = lax.broadcasted_iota(jnp.int32, (2, BLOCK), 0) * BLOCK + lax.broadcasted_iota(jnp.int32, (2, BLOCK), 1)
-    live_ref[...] = jnp.where((labels >= 0) & (offset < length_ref[0]), 1.0, 0.0)
+    live = jnp.where((labels >= 0) & (offset < length_ref[0]), 1.0, 0.0)
+    for b in range(2):
+        rows = jnp.broadcast_to(live[b:b + 1, :], (16, BLOCK))
+        own_ref[64:80, b * BLOCK:(b + 1) * BLOCK] = rows.astype(BF16)
     for m, map_ref in enumerate((down_ref, up_ref)):
         copies[2 + m].wait()
         for c in range(BANDS):
@@ -54,6 +59,8 @@
         for i in range(2):
             out_f[rows_of(2 * m + i, PEERS, 8), :] = rows_f[rows_of(i, PEERS, 2), :]
     out_ref[...] = out_f[...].astype(BF16)
+    for copy in copies[4:]:
+        copy.wait()
 
 
 def pick_rows(in_ref, out_ref, in_f, out_f):
@@ -74,7 +81,8 @@
     me = place_ref[0]
     for k, piece in enumerate((own_ref, one_ref, two_ref, three_ref)):
         first = pl.multiple_of(lax.bitwise_xor(me, k) * 64, 64)
-        grad_ref[pl.ds(first, 64), :] = piece[...]
+        grad_ref[pl.ds(first, 64), :] = piece[:64, :]
+    live = own_ref[64:80, :2 * BLOCK].astype(F32)[:1, :]
     for c in range(BANDS):
         rows = picked_ref[c * 64:(c + 1) * 64, :].astype(F32).reshape(QUARTERS, 2, 8, LANES)
         for b in range(2):
@@ -86,16 +94,16 @@
         block = slice(b * BLOCK, (b + 1) * BLOCK)
         inner = lax.dot_general(maps, attn_ref[block, :], over_last, preferred_element_type=F32)
         outer = lax.dot_general(maps, grad_ref[block, :], over_last, preferred_element_type=F32)
-        part_ref[:, block] = jnp.where((row & 2) == 0, inner, outer)
-
-
-def make_terms(own_ref, one_ref, two_ref, three_ref, live_ref, attn_ref, grad_ref, ranks_ref, term_ref):
+        part_ref[:, block] = jnp.where(live[:, block] > 0, jnp.where((row & 2) == 0, inner, outer), 0.0)
+
+
+def make_terms(own_ref, one_ref, two_ref, three_ref, attn_ref, grad_ref, ranks_ref, term_ref):
     total = (own_ref[...] + one_ref[...]) + (two_ref[...] + three_ref[...])
     row = lax.broadcasted_iota(jnp.int32, (32, LANES), 0)
     terms = []
     for b in range(2):
         block = slice(b * BLOCK, (b + 1) * BLOCK)
-        ranks = jnp.where(live_ref[b:b + 1, :] > 0, total[:, block], 0.0).astype(BF16)
+        ranks = total[:, block].astype(BF16)
         ranks_ref[:, block] = ranks
         down = jnp.dot(ranks, attn_ref[block, :], preferred_element_type=F32)
         up = jnp.dot(ranks, grad_ref[block, :], preferred_element_type=F32)
@@ -147,14 +155,14 @@
             map_ref[:, c * LANES:(c + 1) * LANES] = rows_f[c * 8:(c + 1) * 8, :]
 
 
-def call(kernel, outs, specs, scratch=(), cost=None):
+def call(kernel, outs, specs, scratch=(), cost=None, limit=40 * MIB):
     return pl.pallas_call(
         kernel,
         out_shape=[jax.ShapeDtypeStruct(shape, dtype) for shape, dtype in outs],
         in_specs=specs,
         out_specs=[VMEM] * len(outs),
         scratch_shapes=scratch,
-        compiler_params=PARAMS,
+        compiler_params=pltpu.CompilerParams(vmem_limit_bytes=limit),
         cost_estimate=cost,
     )
 
@@ -171,15 +179,12 @@
 def per_device(attn, output_gradient, down_weight, up_weight, adapter_of_row, lengths):
     width = attn.shape[1]
     me = lax.axis_index("tensor")
-    slices = [
-        lax.dynamic_slice_in_dim(output_gradient, (me ^ k) * width, width, 1) for k in range(4)
-    ]
-    pieces = [slices[0]] + [from_peer(slices[k], k) for k in (1, 2, 3)]
-
-    packed, live = call(
+    me = me.astype(jnp.int32).reshape(1)
+    piece = ((64, width), BF16)
+    packed, *pieces = call(
         pack_tables,
-        [((8 * PEERS, LANES), BF16), ((2, BLOCK), F32)],
-        [ANY] * 4,
+        [((8 * PEERS, LANES), BF16), ((80, width), BF16), piece, piece, piece],
+        [SMEM] + [ANY] * 5,
         [
             pltpu.VMEM((8, width), BF16),
             pltpu.VMEM((8, width), BF16),
@@ -187,11 +192,13 @@
             pltpu.SMEM((1,), jnp.int32),
             pltpu.VMEM((2 * PEERS, LANES), F32),
             pltpu.VMEM((8 * PEERS, LANES), F32),
-            pltpu.SemaphoreType.DMA((4,)),
+            pltpu.SemaphoreType.DMA((8,)),
         ],
-    )(down_weight, up_weight, adapter_of_row.reshape(2, BLOCK), lengths)
+        limit=56 * MIB,
+    )(me, down_weight, up_weight, adapter_of_row.reshape(2, BLOCK), lengths, output_gradient)
+    pieces = [pieces[0]] + [from_peer(pieces[k], k) for k in (1, 2, 3)]
     tables = swap(packed)
-    tables, pieces[1], pieces[3] = lax.optimization_barrier((tables, pieces[1], pieces[3]))
+    tables, *pieces = lax.optimization_barrier((tables, *pieces))
     (picked,) = call(
         pick_rows,
         [((16 * PEERS, LANES), BF16)],
@@ -203,13 +210,13 @@
         project,
         [((64, width), BF16), ((2 * BLOCK, width), BF16), ((32, 2 * BLOCK), F32)],
         [VMEM] * 6 + [SMEM],
-    )(picked, attn, *pieces, me.astype(jnp.int32).reshape(1))
+    )(picked, attn, *pieces, me)
     parts = [part] + [from_peer(part, k) for k in (1, 2, 3)]
     ranks, terms = call(
         make_terms,
         [((32, 2 * BLOCK), BF16), ((16 * PEERS, LANES), BF16)],
-        [VMEM] * 7,
-    )(*parts, live, attn, grad)
+        [VMEM] * 6,
+    )(*parts, attn, grad)
     terms = swap(terms)
     (attention_gradient,) = call(
         go_back,

time: 94.7 us -> 93.3 us (0.985)
  blocking collectives: 46.5 us -> 61.4 us
  waiting for transfers between devices: 22 us -> 11.3 us
  starting transfers between devices: 17.3 us -> 11.8 us
  local copies, waits for them, and re-layouts: 1.29 us -> 0.01 us
  Pallas kernels: 5.94 us -> 7.02 us
    all_to_all x2 -> x3, blocking collectives: 46.5 us -> 61.4 us  [swap(): return lax.all_to_all(chunks, 'dp', 0, 0, tiled=True).reshape(x.shape)]
    ppermute x6, waiting for transfers between devices: 11.1 us -> 2.16 us  [from_peer(): return lax.ppermute(x, 'tensor', [(i, i ^ k) for i in range(4)])]
    all_to_all x2 -> x1, starting transfers between devices: 10 us -> 4.85 us  [swap(): return lax.all_to_all(chunks, 'dp', 0, 0, tiled=True).reshape(x.shape)]
    pallas_call x1, Pallas kernels: 0.64 us -> 2.44 us  [per_device(): call(pack_tables, [((8 * PEERS, LANES), BF16), ((80, width), BF16), piece...]
    all_to_all x2 -> x1, waiting for transfers between devices: 10.9 us -> 9.17 us  [swap(): return lax.all_to_all(chunks, 'dp', 0, 0, tiled=True).reshape(x.shape)]
    dynamic_slice x1 -> x0, local copies, waits for them, and re-layouts: 1.27 us -> none  [per_device(): lax.dynamic_slice_in_dim(output_gradient, (me ^ k) * width, width, 1)]
  transfers between devices with their start and end apart: 8 -> 7, of which waited for: 5 -> 3; matrix products, arithmetic and copies ran while one was open for 0% -> 0% of each run, Pallas kernels for 2% -> 2%
where the time goes in v3:
time: 93.3 us; the launch traced here: 92.9 us
  blocking collectives  61.4 us (66%)
  starting transfers between devices  11.8 us (13%)
  waiting for transfers between devices  11.3 us (12%)
  Pallas kernels  7.02 us (8%)
  between operations  1.36 us (1%)
    all_to_all x3, blocking collectives, swap(): return lax.all_to_all(chunks, 'dp', 0, 0, tiled=True).reshape(x.shape)  61.4 us
    all_to_all x1, waiting for transfers between devices, swap(): return lax.all_to_all(chunks, 'dp', 0, 0, tiled=True).reshape(x.shape)  9.17 us
    ppermute x6, starting transfers between devices, from_peer(): return lax.ppermute(x, 'tensor', [(i, i ^ k) for i in range(4)])  6.91 us
    all_to_all x1, starting transfers between devices, swap(): return lax.all_to_all(chunks, 'dp', 0, 0, tiled=True).reshape(x.shape)  4.85 us
    pallas_call x1, Pallas kernels, per_device(): call(pack_tables, [((8 * PEERS, LANES), BF16), ((80, width), BF16), piece...  2.44 us
    ppermute x6, waiting for transfers between devices, from_peer(): return lax.ppermute(x, 'tensor', [(i, i ^ k) for i in range(4)])  2.16 us
  transfers between devices with their start and end apart: 7, of which 3 were waited for; matrix products, arithmetic and copies ran while one was open for 0% of the time, Pallas kernels for 2%

profile of v3, /device:TPU:2, one launch (start us, length us, event | category | flops | bytes accessed | tf_op | source)
XLA Modules:
  0.0 92.9 jit_solution(380771119285942242)
XLA Ops:
  1.3 0.0 copy-start
  1.3 2.4 %shard_map.85 = (bf16[512,128]{1,0:T(8,128)(2,1)}, bf16[80,2048]{1,0:T(8,128)(2,1)}, bf16[64,2048]{1,0:T(8,128)(2,1)}, bf16[64,2048]{1,0:T(8,128)(2,1)}, bf16[64,2048]{1,0:T(8,128)(2,1)}) custom-call(s32[1]{0:T(128)} %bitcast.place_ref, bf16[8,2048]{1,0:T(8,128)(2,1)} %down_hbm.1, bf16[8,2048]{1,0:T(8,128)(2,1)} %up_hbm.1, s32[2,128]{1,0:T(2,128)} %bitcast.18, ...), custom_call_target="tpu_custom_call" | custom-call | tf_op jit(solution)/shard_map/pallas_call | solution.py:184
  3.7 0.1 collective-permute-start
  3.8 2.2 %collective-permute-start.1 = (bf16[64,2048]{1,0:T(8,128)(2,1)}, bf16[64,2048]{1,0:T(8,128)(2,1)S(1)}, u32[]{:S(2)}, u32[]{:S(2)}) collective-permute-start(bf16[64,2048]{1,0:T(8,128)(2,1)} %get-tuple-element.23), channel_id=1, source_target_pairs={{0,2},{1,3},{2,0},{3,1},{4,6},{5,7},{6,4},{7,5},{8,10},{9,11},{10,... | collective-permute-start | bytes 786440 | tf_op jit(solution)/shard_map/ppermute | solution.py:176
  6.0 1.2 %collective-permute-start.2 = (bf16[64,2048]{1,0:T(8,128)(2,1)}, bf16[64,2048]{1,0:T(8,128)(2,1)S(1)}, u32[]{:S(2)}, u32[]{:S(2)}) collective-permute-start(bf16[64,2048]{1,0:T(8,128)(2,1)} %get-tuple-element.24), channel_id=1, source_target_pairs={{0,3},{1,2},{2,1},{3,0},{4,7},{5,6},{6,5},{7,4},{8,11},{9,10},{10,... | collective-permute-start | bytes 786440 | tf_op jit(solution)/shard_map/ppermute | solution.py:176
  7.2 24.3 %all_to_all.20 = bf16[64,8,128]{2,1,0:T(8,128)(2,1)S(1)} all-to-all(bf16[64,8,128]{2,1,0:T(8,128)(2,1)} %bitcast.17), channel_id=1, replica_groups=mesh['dp'=64,'tensor'=4] {'dp'}, dimensions={0} | all-to-all | bytes 262144 | tf_op jit(solution)/shard_map/all_to_all | solution.py:172
  31.5 0.0 collective-permute-done.one_ref
  31.5 0.0 collective-permute-done.1.two_ref
  31.5 0.0 collective-permute-done.2.three_ref
  31.6 0.3 shard_map.86
  31.9 0.0 copy-start.1
  31.9 17.5 %all_to_all.21 = bf16[64,16,128]{2,1,0:T(8,128)(2,1)S(1)} all-to-all(bf16[64,16,128]{2,1,0:T(8,128)(2,1)S(1)} %bitcast.13), channel_id=1, replica_groups=mesh['dp'=64,'tensor'=4] {'dp'}, dimensions={0} | all-to-all | bytes 524288 | tf_op jit(solution)/shard_map/all_to_all | solution.py:172
  49.4 0.0 copy-done
  49.4 0.0 copy-done.1
  49.4 0.7 shard_map.87
  50.2 0.1 collective-permute-start.5
  50.3 2.2 %collective-permute-start.4 = (f32[32,256]{1,0:T(8,128)S(1)}, f32[32,256]{1,0:T(8,128)S(1)}, u32[]{:S(2)}, u32[]{:S(2)}) collective-permute-start(f32[32,256]{1,0:T(8,128)S(1)} %get-tuple-element.30.own_ref), channel_id=1, source_target_pairs={{0,2},{1,3},{2,0},{3,1},{4,6},{5,7},{6,4},{7,5},{8,10},{9,11},{10,... | collective-permute-start | bytes 98312 | tf_op jit(solution)/shard_map/ppermute | solution.py:176
  52.5 1.1 %collective-permute-start.3 = (f32[32,256]{1,0:T(8,128)S(1)}, f32[32,256]{1,0:T(8,128)S(1)}, u32[]{:S(2)}, u32[]{:S(2)}) collective-permute-start(f32[32,256]{1,0:T(8,128)S(1)} %get-tuple-element.30.own_ref), channel_id=1, source_target_pairs={{0,1},{1,0},{2,3},{3,2},{4,5},{5,4},{6,7},{7,6},{8,9},{9,8},{10,11... | collective-permute-start | bytes 98312 | tf_op jit(solution)/shard_map/ppermute | solution.py:176
  53.6 1.5 %collective-permute-done.5.three_ref = f32[32,256]{1,0:T(8,128)S(1)} collective-permute-done((f32[32,256]{1,0:T(8,128)S(1)}, f32[32,256]{1,0:T(8,128)S(1)}, u32[]{:S(2)}, u32[]{:S(2)}) %collective-permute-start.5) | collective-permute-done | bytes 32800 | tf_op jit(solution)/shard_map/ppermute | solution.py:176
  55.1 0.7 collective-permute-done.4.two_ref
  55.8 0.0 collective-permute-done.3.one_ref
  55.8 0.4 shard_map.88
  56.2 19.6 %all_to_all.22 = bf16[64,16,128]{2,1,0:T(8,128)(2,1)S(1)} all-to-all(bf16[64,16,128]{2,1,0:T(8,128)(2,1)S(1)} %bitcast.16), channel_id=1, replica_groups=mesh['dp'=64,'tensor'=4] {'dp'}, dimensions={0} | all-to-all | bytes 524288 | tf_op jit(solution)/shard_map/all_to_all | solution.py:172
  75.8 1.0 %shard_map.90 = f32[256,128]{1,0:T(8,128)} custom-call(bf16[1024,128]{1,0:T(8,128)(2,1)S(1)} %bitcast.12, bf16[512,128]{1,0:T(8,128)(2,1)S(1)} %bitcast.11), custom_call_target="tpu_custom_call" | custom-call | tf_op jit(solution)/shard_map/pallas_call | solution.py:227
  76.8 4.8 %all-to-all-start.3 = ((f32[64,4,128]{2,1,0:T(4,128)}), f32[64,4,128]{2,1,0:T(4,128)S(1)}, u32[]{:S(2)}, u32[]{:S(2)}) async-start(f32[64,4,128]{2,1,0:T(4,128)} %bitcast.8), calls=%async_computation.3 | async-start | bytes 262144 | tf_op jit(solution)/shard_map/all_to_all | solution.py:172
  81.7 1.4 %shard_map.89 = bf16[256,2048]{1,0:T(8,128)(2,1)} custom-call(bf16[32,256]{1,0:T(8,128)(2,1)S(1)} %get-tuple-element.32.ranks_ref, bf16[64,2048]{1,0:T(8,128)(2,1)S(1)} %get-tuple-element.33.maps_ref), custom_call_target="tpu_custom_call" | custom-call | flops 33554432 | bytes 2097152 | tf_op jit(solution)/shard_map/pallas_call | solution.py:221
  83.1 9.2 %all-to-all-done.3 = f32[64,4,128]{2,1,0:T(4,128)S(1)} async-done(((f32[64,4,128]{2,1,0:T(4,128)}), f32[64,4,128]{2,1,0:T(4,128)S(1)}, u32[]{:S(2)}, u32[]{:S(2)}) %all-to-all-start.3) | async-done | bytes 131104 | tf_op jit(solution)/shard_map/all_to_all | solution.py:172
  92.3 0.7 shard_map.91
Async XLA Ops:
  1.3 48.2 %copy-start = (bf16[256,2048]{1,0:T(8,128)(2,1)S(1)}, bf16[256,2048]{1,0:T(8,128)(2,1)}, u32[]{:S(2)}) copy-start(bf16[256,2048]{1,0:T(8,128)(2,1)} %attn_ref.3) | copy-start | bytes 3145732
  3.7 27.8 %collective-permute-start = (bf16[64,2048]{1,0:T(8,128)(2,1)}, bf16[64,2048]{1,0:T(8,128)(2,1)S(1)}, u32[]{:S(2)}, u32[]{:S(2)}) collective-permute-start(bf16[64,2048]{1,0:T(8,128)(2,1)} %get-tuple-element.22), channel_id=1, source_target_pairs={{0,1},{1,0},{2,3},{3,2},{4,5},{5,4},{6,7},{7,6},{8,9},{9,8},{10,11... | collective-permute-start | bytes 786440 | tf_op jit(solution)/shard_map/ppermute | solution.py:176
  3.8 27.7 %collective-permute-start.1 = (bf16[64,2048]{1,0:T(8,128)(2,1)}, bf16[64,2048]{1,0:T(8,128)(2,1)S(1)}, u32[]{:S(2)}, u32[]{:S(2)}) collective-permute-start(bf16[64,2048]{1,0:T(8,128)(2,1)} %get-tuple-element.23), channel_id=1, source_target_pairs={{0,2},{1,3},{2,0},{3,1},{4,6},{5,7},{6,4},{7,5},{8,10},{9,11},{10,... | collective-permute-start | bytes 786440 | tf_op jit(solution)/shard_map/ppermute | solution.py:176
  6.0 25.5 %collective-permute-start.2 = (bf16[64,2048]{1,0:T(8,128)(2,1)}, bf16[64,2048]{1,0:T(8,128)(2,1)S(1)}, u32[]{:S(2)}, u32[]{:S(2)}) collective-permute-start(bf16[64,2048]{1,0:T(8,128)(2,1)} %get-tuple-element.24), channel_id=1, source_target_pairs={{0,3},{1,2},{2,1},{3,0},{4,7},{5,6},{6,5},{7,4},{8,11},{9,10},{10,... | collective-permute-start | bytes 786440 | tf_op jit(solution)/shard_map/ppermute | solution.py:176
  31.9 17.6 %copy-start.1 = (bf16[80,2048]{1,0:T(8,128)(2,1)S(1)}, bf16[80,2048]{1,0:T(8,128)(2,1)}, u32[]{:S(2)}) copy-start(bf16[80,2048]{1,0:T(8,128)(2,1)} %get-tuple-element.26.own_ref) | copy-start | bytes 983044
  50.2 4.9 %collective-permute-start.5 = (f32[32,256]{1,0:T(8,128)S(1)}, f32[32,256]{1,0:T(8,128)S(1)}, u32[]{:S(2)}, u32[]{:S(2)}) collective-permute-start(f32[32,256]{1,0:T(8,128)S(1)} %get-tuple-element.30.own_ref), channel_id=1, source_target_pairs={{0,3},{1,2},{2,1},{3,0},{4,7},{5,6},{6,5},{7,4},{8,11},{9,10},{10,... | collective-permute-start | bytes 98312 | tf_op jit(solution)/shard_map/ppermute | solution.py:176
  50.3 5.5 %collective-permute-start.4 = (f32[32,256]{1,0:T(8,128)S(1)}, f32[32,256]{1,0:T(8,128)S(1)}, u32[]{:S(2)}, u32[]{:S(2)}) collective-permute-start(f32[32,256]{1,0:T(8,128)S(1)} %get-tuple-element.30.own_ref), channel_id=1, source_target_pairs={{0,2},{1,3},{2,0},{3,1},{4,6},{5,7},{6,4},{7,5},{8,10},{9,11},{10,... | collective-permute-start | bytes 98312 | tf_op jit(solution)/shard_map/ppermute | solution.py:176
  52.5 3.3 %collective-permute-start.3 = (f32[32,256]{1,0:T(8,128)S(1)}, f32[32,256]{1,0:T(8,128)S(1)}, u32[]{:S(2)}, u32[]{:S(2)}) collective-permute-start(f32[32,256]{1,0:T(8,128)S(1)} %get-tuple-element.30.own_ref), channel_id=1, source_target_pairs={{0,1},{1,0},{2,3},{3,2},{4,5},{5,4},{6,7},{7,6},{8,9},{9,8},{10,11... | collective-permute-start | bytes 98312 | tf_op jit(solution)/shard_map/ppermute | solution.py:176
  76.8 15.5 %all-to-all-start.3 = ((f32[64,4,128]{2,1,0:T(4,128)}), f32[64,4,128]{2,1,0:T(4,128)S(1)}, u32[]{:S(2)}, u32[]{:S(2)}) async-start(f32[64,4,128]{2,1,0:T(4,128)} %bitcast.8), calls=%async_computation.3 | async-start | bytes 262144 | tf_op jit(solution)/shard_map/all_to_all | solution.py:172

commit v4 on v3

--- a/solution.py
+++ b/solution.py
@@ -26,16 +26,8 @@
     return pl.ds(first, size, stride=stride)
 
 
-def pack_tables(
-    place_ref, down_hbm, up_hbm, label_hbm, length_hbm, grad_hbm,
-    out_ref, own_ref, one_ref, two_ref, three_ref,
-    down_ref, up_ref, label_ref, length_ref, rows_f, out_f, sems
-):
-    width = own_ref.shape[1]
-    moves = [(label_hbm, label_ref), (length_hbm, length_ref), (down_hbm, down_ref), (up_hbm, up_ref)]
-    for k, piece in ((3, three_ref), (2, two_ref), (1, one_ref), (0, own_ref)):
-        first = pl.multiple_of(lax.bitwise_xor(place_ref[0], k) * width, width)
-        moves.append((grad_hbm.at[:, pl.ds(first, width)], piece.at[pl.ds(0, 64), :]))
+def pack_tables(down_hbm, up_hbm, label_hbm, out_ref, down_ref, up_ref, label_ref, rows_f, out_f, sems):
+    moves = ((label_hbm, label_ref), (down_hbm, down_ref), (up_hbm, up_ref))
     copies = [pltpu.make_async_copy(src, dst, sems.at[n]) for n, (src, dst) in enumerate(moves)]
     for copy in copies:
         copy.start()
@@ -46,21 +38,13 @@
     for b in range(2):
         which = jnp.maximum(labels[b:b + 1, 0:1], 0).astype(F32)
         out_f[rows_of(4 + b, PEERS, 8), :] = jnp.broadcast_to(which, (PEERS, LANES))
-    copies[1].wait()
-    offset = lax.broadcasted_iota(jnp.int32, (2, BLOCK), 0) * BLOCK + lax.broadcasted_iota(jnp.int32, (2, BLOCK), 1)
-    live = jnp.where((labels >= 0) & (offset < length_ref[0]), 1.0, 0.0)
-    for b in range(2):
-        rows = jnp.broadcast_to(live[b:b + 1, :], (16, BLOCK))
-        own_ref[64:80, b * BLOCK:(b + 1) * BLOCK] = rows.astype(BF16)
     for m, map_ref in enumerate((down_ref, up_ref)):
-        copies[2 + m].wait()
+        copies[1 + m].wait()
         for c in range(BANDS):
             rows_f[c * 8:(c + 1) * 8, :] = map_ref[:, c * LANES:(c + 1) * LANES].astype(F32)
         for i in range(2):
             out_f[rows_of(2 * m + i, PEERS, 8), :] = rows_f[rows_of(i, PEERS, 2), :]
     out_ref[...] = out_f[...].astype(BF16)
-    for copy in copies[4:]:
-        copy.wait()
 
 
 def pick_rows(in_ref, out_ref, in_f, out_f):
@@ -77,16 +61,18 @@
     out_ref[...] = out_f[...].astype(BF16)
 
 
-def project(picked_ref, attn_ref, own_ref, one_ref, two_ref, three_ref, place_ref, maps_ref, grad_ref, part_ref):
-    me = place_ref[0]
-    for k, piece in enumerate((own_ref, one_ref, two_ref, three_ref)):
-        first = pl.multiple_of(lax.bitwise_xor(me, k) * 64, 64)
-        grad_ref[pl.ds(first, 64), :] = piece[:64, :]
-    live = own_ref[64:80, :2 * BLOCK].astype(F32)[:1, :]
+def project(
+    place_ref, picked_ref, attn_ref, tokens_hbm, live_ref, maps_ref, grad_ref, part_ref, sem
+):
+    width = grad_ref.shape[1]
+    first = pl.multiple_of(place_ref[0] * width, width)
+    copy = pltpu.make_async_copy(tokens_hbm.at[:, pl.ds(first, width)], grad_ref, sem)
+    copy.start()
     for c in range(BANDS):
         rows = picked_ref[c * 64:(c + 1) * 64, :].astype(F32).reshape(QUARTERS, 2, 8, LANES)
         for b in range(2):
             maps_ref[b * 32:(b + 1) * 32, c * LANES:(c + 1) * LANES] = rows[:, b].reshape(32, LANES).astype(BF16)
+    copy.wait()
     row = lax.broadcasted_iota(jnp.int32, (32, BLOCK), 0)
     over_last = (((1,), (1,)), ((), ()))
     for b in range(2):
@@ -94,7 +80,7 @@
         block = slice(b * BLOCK, (b + 1) * BLOCK)
         inner = lax.dot_general(maps, attn_ref[block, :], over_last, preferred_element_type=F32)
         outer = lax.dot_general(maps, grad_ref[block, :], over_last, preferred_element_type=F32)
-        part_ref[:, block] = jnp.where(live[:, block] > 0, jnp.where((row & 2) == 0, inner, outer), 0.0)
+        part_ref[:, block] = jnp.where(live_ref[b:b + 1, :] > 0, jnp.where((row & 2) == 0, inner, outer), 0.0)
 
 
 def make_terms(own_ref, one_ref, two_ref, three_ref, attn_ref, grad_ref, ranks_ref, term_ref):
@@ -180,25 +166,25 @@
     width = attn.shape[1]
     me = lax.axis_index("tensor")
     me = me.astype(jnp.int32).reshape(1)
-    piece = ((64, width), BF16)
-    packed, *pieces = call(
+    labels = adapter_of_row.reshape(2, BLOCK)
+    tokens = lax.all_gather(output_gradient, "tensor", axis=0, tiled=True)
+    (packed,) = call(
         pack_tables,
-        [((8 * PEERS, LANES), BF16), ((80, width), BF16), piece, piece, piece],
-        [SMEM] + [ANY] * 5,
+        [((8 * PEERS, LANES), BF16)],
+        [ANY] * 3,
         [
             pltpu.VMEM((8, width), BF16),
             pltpu.VMEM((8, width), BF16),
             pltpu.VMEM((2, BLOCK), jnp.int32),
-            pltpu.SMEM((1,), jnp.int32),
             pltpu.VMEM((2 * PEERS, LANES), F32),
             pltpu.VMEM((8 * PEERS, LANES), F32),
-            pltpu.SemaphoreType.DMA((8,)),
+            pltpu.SemaphoreType.DMA((3,)),
         ],
         limit=56 * MIB,
-    )(me, down_weight, up_weight, adapter_of_row.reshape(2, BLOCK), lengths, output_gradient)
-    pieces = [pieces[0]] + [from_peer(pieces[k], k) for k in (1, 2, 3)]
-    tables = swap(packed)
-    tables, *pieces = lax.optimization_barrier((tables, *pieces))
+    )(down_weight, up_weight, labels)
+    live = (adapter_of_row >= 0) & (jnp.arange(2 * BLOCK, dtype=jnp.int32) < lengths[0])
+    live = live.astype(F32).reshape(2, BLOCK)
+    tables, me, live = lax.optimization_barrier((swap(packed), me, live))
     (picked,) = call(
         pick_rows,
         [((16 * PEERS, LANES), BF16)],
@@ -209,8 +195,10 @@
     maps, grad, part = call(
         project,
         [((64, width), BF16), ((2 * BLOCK, width), BF16), ((32, 2 * BLOCK), F32)],
-        [VMEM] * 6 + [SMEM],
-    )(picked, attn, *pieces, me)
+        [SMEM, VMEM, VMEM, ANY, VMEM],
+        [pltpu.SemaphoreType.DMA(())],
+        limit=52 * MIB,
+    )(me, picked, attn, tokens, live)
     parts = [part] + [from_peer(part, k) for k in (1, 2, 3)]
     ranks, terms = call(
         make_terms,

time: 93.3 us -> 115 us (1.23)
  blocking collectives: 61.4 us -> 40.2 us
  waiting for transfers between devices: 11.3 us -> 28.4 us
  between operations: 1.36 us -> 14.7 us
  starting transfers between devices: 11.8 us -> 21.6 us
  Pallas kernels: 7.02 us -> 8.64 us
    all_to_all x3 -> x2, blocking collectives: 61.4 us -> 40.2 us  [swap(): return lax.all_to_all(chunks, 'dp', 0, 0, tiled=True).reshape(x.shape)]
    all_to_all x1 -> x2, starting transfers between devices: 4.85 us -> 18.1 us  [swap(): return lax.all_to_all(chunks, 'dp', 0, 0, tiled=True).reshape(x.shape)]
    all_to_all x1 -> x2, waiting for transfers between devices: 9.17 us -> 18.4 us  [swap(): return lax.all_to_all(chunks, 'dp', 0, 0, tiled=True).reshape(x.shape)]
    all_gather x0 -> x1, waiting for transfers between devices: none -> 6 us  [per_device(): tokens = lax.all_gather(output_gradient, 'tensor', axis=0, tiled=True)]
    ppermute x6 -> x3, starting transfers between devices: 6.91 us -> 3.47 us  [from_peer(): return lax.ppermute(x, 'tensor', [(i, i ^ k) for i in range(4)])]
    pallas_call x1, Pallas kernels: 0.74 us -> 3.26 us  [per_device(): call(project, [((64, width), BF16), ((2 * BLOCK, width), BF16), ((32, 2 *...]
    ppermute x6 -> x3, waiting for transfers between devices: 2.16 us -> 3.31 us  [from_peer(): return lax.ppermute(x, 'tensor', [(i, i ^ k) for i in range(4)])]
  transfers between devices with their start and end apart: 7 -> 6, of which waited for: 3 -> 5; matrix products, arithmetic and copies ran while one was open for 0% -> 1% of each run, Pallas kernels for 2% -> 3%
where the time goes in v4:
time: 115 us; the launch traced here: 114 us
  blocking collectives  40.2 us (35%)
  waiting for transfers between devices  28.4 us (25%)
  starting transfers between devices  21.6 us (19%)
  between operations  14.7 us (13%)
  Pallas kernels  8.64 us (8%)
    all_to_all x2, blocking collectives, swap(): return lax.all_to_all(chunks, 'dp', 0, 0, tiled=True).reshape(x.shape)  40.2 us
    all_to_all x2, waiting for transfers between devices, swap(): return lax.all_to_all(chunks, 'dp', 0, 0, tiled=True).reshape(x.shape)  18.4 us
    all_to_all x2, starting transfers between devices, swap(): return lax.all_to_all(chunks, 'dp', 0, 0, tiled=True).reshape(x.shape)  18.1 us
    all_gather x1, waiting for transfers between devices, per_device(): tokens = lax.all_gather(output_gradient, 'tensor', axis=0, tiled=True)  6 us
    ppermute x3, starting transfers between devices, from_peer(): return lax.ppermute(x, 'tensor', [(i, i ^ k) for i in range(4)])  3.47 us
    ppermute x3, waiting for transfers between devices, from_peer(): return lax.ppermute(x, 'tensor', [(i, i ^ k) for i in range(4)])  3.31 us
    pallas_call x1, Pallas kernels, per_device(): call(project, [((64, width), BF16), ((2 * BLOCK, width), BF16), ((32, 2 *...  3.26 us
  transfers between devices with their start and end apart: 6, of which 5 were waited for; matrix products, arithmetic and copies ran while one was open for 1% of the time, Pallas kernels for 3%

profile of v4, /device:TPU:2, one launch (start us, length us, event | category | flops | bytes accessed | tf_op | source)
XLA Modules:
  0.0 114.2 jit_solution(5605600571285678254)
XLA Ops:
  7.2 0.0 copy-start
  7.2 0.0 all-gather.2.cloned.1.call-start
  7.2 0.7 all-gather.2.cloned.1.call-update
  7.9 1.5 %shard_map.85 = bf16[512,128]{1,0:T(8,128)(2,1)} custom-call(bf16[8,2048]{1,0:T(8,128)(2,1)} %down_hbm.1, bf16[8,2048]{1,0:T(8,128)(2,1)} %up_hbm.1, s32[2,128]{1,0:T(2,128)} %bitcast.22), custom_call_target="tpu_custom_call" | custom-call | tf_op jit(solution)/shard_map/pallas_call | solution.py:171
  9.4 13.2 %all-to-all-start = ((bf16[64,8,128]{2,1,0:T(8,128)(2,1)}), bf16[64,8,128]{2,1,0:T(8,128)(2,1)S(1)}, u32[]{:S(2)}, u32[]{:S(2)}) async-start(bf16[64,8,128]{2,1,0:T(8,128)(2,1)} %bitcast.21), calls=%async_computation | async-start | bytes 262144 | tf_op jit(solution)/shard_map/all_to_all | solution.py:158
  23.3 0.7 fusion.live_ref
  24.0 9.3 %all-to-all-done = bf16[64,8,128]{2,1,0:T(8,128)(2,1)S(1)} async-done(((bf16[64,8,128]{2,1,0:T(8,128)(2,1)}), bf16[64,8,128]{2,1,0:T(8,128)(2,1)S(1)}, u32[]{:S(2)}, u32[]{:S(2)}) %all-to-all-start) | async-done | bytes 131104 | tf_op jit(solution)/shard_map/all_to_all | solution.py:158
  33.3 0.3 shard_map.86
  33.6 16.7 %all_to_all.20 = bf16[64,16,128]{2,1,0:T(8,128)(2,1)S(1)} all-to-all(bf16[64,16,128]{2,1,0:T(8,128)(2,1)S(1)} %bitcast.18), channel_id=1, replica_groups=mesh['dp'=64,'tensor'=4] {'dp'}, dimensions={0} | all-to-all | bytes 524288 | tf_op jit(solution)/shard_map/all_to_all | solution.py:158
  50.3 6.0 %all-gather.2.cloned.1.call-done.tokens_hbm = bf16[256,8192]{1,0:T(8,128)(2,1)} async-done(((bf16[64,8192]{1,0:T(8,128)(2,1)}), bf16[256,8192]{1,0:T(8,128)(2,1)}) %all-gather.2.cloned.1.call-update) | async-done | bytes 4194320 | tf_op jit(solution)/shard_map/all_gather | solution.py:170
  56.3 3.3 %shard_map.87 = (bf16[64,2048]{1,0:T(8,128)(2,1)S(1)}, bf16[256,2048]{1,0:T(8,128)(2,1)S(1)}, f32[32,256]{1,0:T(8,128)S(1)}) custom-call(s32[1]{0:T(128)} %bitcast.3.place_ref, bf16[1024,128]{1,0:T(8,128)(2,1)S(1)} %bitcast.16, bf16[256,2048]{1,0:T(8,128)(2,1)} %attn_ref.3, bf16[256,8192]{1,0:T(8,128)(2,1)} %all-gather.2.cloned.1.call-done.tokens_hbm, ...), custom_call_target="tpu_custom_call" | custom-call | tf_op jit(solution)/shard_map/pallas_call | solution.py:195
  59.6 1.4 %collective-permute-start.2 = (f32[32,256]{1,0:T(8,128)S(1)}, f32[32,256]{1,0:T(8,128)S(1)}, u32[]{:S(2)}, u32[]{:S(2)}) collective-permute-start(f32[32,256]{1,0:T(8,128)S(1)} %get-tuple-element.16.own_ref), channel_id=1, source_target_pairs={{0,3},{1,2},{2,1},{3,0},{4,7},{5,6},{6,5},{7,4},{8,11},{9,10},{10,... | collective-permute-start | bytes 98312 | tf_op jit(solution)/shard_map/ppermute | solution.py:162
  60.9 2.1 %collective-permute-start.1 = (f32[32,256]{1,0:T(8,128)S(1)}, f32[32,256]{1,0:T(8,128)S(1)}, u32[]{:S(2)}, u32[]{:S(2)}) collective-permute-start(f32[32,256]{1,0:T(8,128)S(1)} %get-tuple-element.16.own_ref), channel_id=1, source_target_pairs={{0,2},{1,3},{2,0},{3,1},{4,6},{5,7},{6,4},{7,5},{8,10},{9,11},{10,... | collective-permute-start | bytes 98312 | tf_op jit(solution)/shard_map/ppermute | solution.py:162
  63.0 0.0 collective-permute-start
  63.1 1.5 %collective-permute-done.2.three_ref = f32[32,256]{1,0:T(8,128)S(1)} collective-permute-done((f32[32,256]{1,0:T(8,128)S(1)}, f32[32,256]{1,0:T(8,128)S(1)}, u32[]{:S(2)}, u32[]{:S(2)}) %collective-permute-start.2) | collective-permute-done | bytes 32800 | tf_op jit(solution)/shard_map/ppermute | solution.py:162
  64.5 1.8 %collective-permute-done.1.two_ref = f32[32,256]{1,0:T(8,128)S(1)} collective-permute-done((f32[32,256]{1,0:T(8,128)S(1)}, f32[32,256]{1,0:T(8,128)S(1)}, u32[]{:S(2)}, u32[]{:S(2)}) %collective-permute-start.1) | collective-permute-done | bytes 32800 | tf_op jit(solution)/shard_map/ppermute | solution.py:162
  66.4 0.0 collective-permute-done.one_ref
  66.4 0.0 copy-done
  66.4 0.4 shard_map.88
  66.8 23.5 %all_to_all.21 = bf16[64,16,128]{2,1,0:T(8,128)(2,1)S(1)} all-to-all(bf16[64,16,128]{2,1,0:T(8,128)(2,1)S(1)} %bitcast.20), channel_id=1, replica_groups=mesh['dp'=64,'tensor'=4] {'dp'}, dimensions={0} | all-to-all | bytes 524288 | tf_op jit(solution)/shard_map/all_to_all | solution.py:158
  90.3 1.0 shard_map.90
  91.3 4.8 %all-to-all-start.3 = ((f32[64,4,128]{2,1,0:T(4,128)}), f32[64,4,128]{2,1,0:T(4,128)S(1)}, u32[]{:S(2)}, u32[]{:S(2)}) async-start(f32[64,4,128]{2,1,0:T(4,128)} %bitcast.10), calls=%async_computation.3 | async-start | bytes 262144 | tf_op jit(solution)/shard_map/all_to_all | solution.py:158
  96.1 1.4 %shard_map.89 = bf16[256,2048]{1,0:T(8,128)(2,1)} custom-call(bf16[32,256]{1,0:T(8,128)(2,1)S(1)} %get-tuple-element.18.ranks_ref, bf16[64,2048]{1,0:T(8,128)(2,1)S(1)} %get-tuple-element.19.maps_ref), custom_call_target="tpu_custom_call" | custom-call | flops 33554432 | bytes 2097152 | tf_op jit(solution)/shard_map/pallas_call | solution.py:209
  97.5 9.2 %all-to-all-done.3 = f32[64,4,128]{2,1,0:T(4,128)S(1)} async-done(((f32[64,4,128]{2,1,0:T(4,128)}), f32[64,4,128]{2,1,0:T(4,128)S(1)}, u32[]{:S(2)}, u32[]{:S(2)}) %all-to-all-start.3) | async-done | bytes 131104 | tf_op jit(solution)/shard_map/all_to_all | solution.py:158
  106.7 0.7 shard_map.91
Async XLA Ops:
  7.2 59.2 %copy-start = (bf16[256,2048]{1,0:T(8,128)(2,1)S(1)}, bf16[256,2048]{1,0:T(8,128)(2,1)}, u32[]{:S(2)}) copy-start(bf16[256,2048]{1,0:T(8,128)(2,1)} %attn_ref.3) | copy-start | bytes 3145732
  7.2 49.1 %all-gather.2.cloned.1.call-start = ((), (), s32[]{:S(2)}) async-start(), calls=%async_computation.4 | async-start | bytes 5242880 | tf_op jit(solution)/shard_map/all_gather | solution.py:170
  9.4 23.8 %all-to-all-start = ((bf16[64,8,128]{2,1,0:T(8,128)(2,1)}), bf16[64,8,128]{2,1,0:T(8,128)(2,1)S(1)}, u32[]{:S(2)}, u32[]{:S(2)}) async-start(bf16[64,8,128]{2,1,0:T(8,128)(2,1)} %bitcast.21), calls=%async_computation | async-start | bytes 262144 | tf_op jit(solution)/shard_map/all_to_all | solution.py:158
  59.6 4.9 %collective-permute-start.2 = (f32[32,256]{1,0:T(8,128)S(1)}, f32[32,256]{1,0:T(8,128)S(1)}, u32[]{:S(2)}, u32[]{:S(2)}) collective-permute-start(f32[32,256]{1,0:T(8,128)S(1)} %get-tuple-element.16.own_ref), channel_id=1, source_target_pairs={{0,3},{1,2},{2,1},{3,0},{4,7},{5,6},{6,5},{7,4},{8,11},{9,10},{10,... | collective-permute-start | bytes 98312 | tf_op jit(solution)/shard_map/ppermute | solution.py:162
  60.9 5.4 %collective-permute-start.1 = (f32[32,256]{1,0:T(8,128)S(1)}, f32[32,256]{1,0:T(8,128)S(1)}, u32[]{:S(2)}, u32[]{:S(2)}) collective-permute-start(f32[32,256]{1,0:T(8,128)S(1)} %get-tuple-element.16.own_ref), channel_id=1, source_target_pairs={{0,2},{1,3},{2,0},{3,1},{4,6},{5,7},{6,4},{7,5},{8,10},{9,11},{10,... | collective-permute-start | bytes 98312 | tf_op jit(solution)/shard_map/ppermute | solution.py:162
  63.0 3.3 %collective-permute-start = (f32[32,256]{1,0:T(8,128)S(1)}, f32[32,256]{1,0:T(8,128)S(1)}, u32[]{:S(2)}, u32[]{:S(2)}) collective-permute-start(f32[32,256]{1,0:T(8,128)S(1)} %get-tuple-element.16.own_ref), channel_id=1, source_target_pairs={{0,1},{1,0},{2,3},{3,2},{4,5},{5,4},{6,7},{7,6},{8,9},{9,8},{10,11... | collective-permute-start | bytes 98312 | tf_op jit(solution)/shard_map/ppermute | solution.py:162
  91.3 15.5 %all-to-all-start.3 = ((f32[64,4,128]{2,1,0:T(4,128)}), f32[64,4,128]{2,1,0:T(4,128)S(1)}, u32[]{:S(2)}, u32[]{:S(2)}) async-start(f32[64,4,128]{2,1,0:T(4,128)} %bitcast.10), calls=%async_computation.3 | async-start | bytes 262144 | tf_op jit(solution)/shard_map/all_to_all | solution.py:158
Sparse Core Ops, SparseCore 0:
  9.8 46.4 all-gather.1

commit v5 on v4

--- a/solution.py
+++ b/solution.py
@@ -1,3 +1,5 @@
+import functools
+
 import jax
 import jax.numpy as jnp
 from jax import lax
@@ -47,6 +49,19 @@
     out_ref[...] = out_f[...].astype(BF16)
 
 
+def cut_tokens(ks, place_ref, grad_hbm, packed_hbm, *refs):
+    pieces, sems = refs[:-1], refs[-1]
+    width = pieces[0].shape[1]
+    copies = []
+    for n, (k, piece) in enumerate(zip(ks, pieces)):
+        first = pl.multiple_of(lax.bitwise_xor(place_ref[0], k) * width, width)
+        copies.append(pltpu.make_async_copy(grad_hbm.at[:, pl.ds(first, width)], piece, sems.at[n]))
+    for copy in copies:
+        copy.start()
+    for copy in copies:
+        copy.wait()
+
+
 def pick_rows(in_ref, out_ref, in_f, out_f):
     in_f[...] = in_ref[...].astype(F32)
     table = jnp.concatenate([in_f[rows_of(k, PEERS, 8), :] for k in range(4)], axis=1).astype(BF16)
@@ -61,18 +76,15 @@
     out_ref[...] = out_f[...].astype(BF16)
 
 
-def project(
-    place_ref, picked_ref, attn_ref, tokens_hbm, live_ref, maps_ref, grad_ref, part_ref, sem
-):
-    width = grad_ref.shape[1]
-    first = pl.multiple_of(place_ref[0] * width, width)
-    copy = pltpu.make_async_copy(tokens_hbm.at[:, pl.ds(first, width)], grad_ref, sem)
-    copy.start()
+def project(picked_ref, attn_ref, own_ref, one_ref, two_ref, three_ref, place_ref, live_ref, maps_ref, grad_ref, part_ref):
+    me = place_ref[0]
+    for k, piece in enumerate((own_ref, one_ref, two_ref, three_ref)):
+        first = pl.multiple_of(lax.bitwise_xor(me, k) * 64, 64)
+        grad_ref[pl.ds(first, 64), :] = piece[...]
     for c in range(BANDS):
         rows = picked_ref[c * 64:(c + 1) * 64, :].astype(F32).reshape(QUARTERS, 2, 8, LANES)
         for b in range(2):
             maps_ref[b * 32:(b + 1) * 32, c * LANES:(c + 1) * LANES] = rows[:, b].reshape(32, LANES).astype(BF16)
-    copy.wait()
     row = lax.broadcasted_iota(jnp.int32, (32, BLOCK), 0)
     over_last = (((1,), (1,)), ((), ()))
     for b in range(2):
@@ -166,8 +178,6 @@
     width = attn.shape[1]
     me = lax.axis_index("tensor")
     me = me.astype(jnp.int32).reshape(1)
-    labels = adapter_of_row.reshape(2, BLOCK)
-    tokens = lax.all_gather(output_gradient, "tensor", axis=0, tiled=True)
     (packed,) = call(
         pack_tables,
         [((8 * PEERS, LANES), BF16)],
@@ -181,10 +191,26 @@
             pltpu.SemaphoreType.DMA((3,)),
         ],
         limit=56 * MIB,
-    )(down_weight, up_weight, labels)
+    )(down_weight, up_weight, adapter_of_row.reshape(2, BLOCK))
+
+    def cut(ks, flops):
+        return call(
+            functools.partial(cut_tokens, ks),
+            [((64, width), BF16)] * len(ks),
+            [SMEM, ANY, ANY],
+            [pltpu.SemaphoreType.DMA((len(ks),))],
+            cost=pl.CostEstimate(flops=flops, bytes_accessed=len(ks) << 19, transcendentals=0),
+            limit=56 * MIB,
+        )(me, output_gradient, packed)
+
     live = (adapter_of_row >= 0) & (jnp.arange(2 * BLOCK, dtype=jnp.int32) < lengths[0])
     live = live.astype(F32).reshape(2, BLOCK)
-    tables, me, live = lax.optimization_barrier((swap(packed), me, live))
+    one, three = cut((1, 3), 1000)
+    own, two = cut((0, 2), 10 ** 10)
+    one, three = from_peer(one, 1), from_peer(three, 3)
+    tables = swap(packed)
+    tables, live, own, two, one, three = lax.optimization_barrier((tables, live, own, two, one, three))
+    pieces = [own, one, from_peer(two, 2), three]
     (picked,) = call(
         pick_rows,
         [((16 * PEERS, LANES), BF16)],
@@ -195,10 +221,8 @@
     maps, grad, part = call(
         project,
         [((64, width), BF16), ((2 * BLOCK, width), BF16), ((32, 2 * BLOCK), F32)],
-        [SMEM, VMEM, VMEM, ANY, VMEM],
-        [pltpu.SemaphoreType.DMA(())],
-        limit=52 * MIB,
-    )(me, picked, attn, tokens, live)
+        [VMEM] * 6 + [SMEM, VMEM],
+    )(picked, attn, *pieces, me, live)
     parts = [part] + [from_peer(part, k) for k in (1, 2, 3)]
     ranks, terms = call(
         make_terms,

time: 115 us -> 101 us (0.88)
  blocking collectives: 40.2 us -> 23.1 us
  starting transfers between devices: 21.6 us -> 37.1 us
  between operations: 14.7 us -> 1.38 us
  Pallas kernels: 8.64 us -> 10.6 us
    all_to_all x2 -> x1, blocking collectives: 40.2 us -> 23.1 us  [swap(): return lax.all_to_all(chunks, 'dp', 0, 0, tiled=True).reshape(x.shape)]
    all_to_all x2 -> x3, starting transfers between devices: 18.1 us -> 29.1 us  [swap(): return lax.all_to_all(chunks, 'dp', 0, 0, tiled=True).reshape(x.shape)]
    ppermute x3 -> x6, waiting for transfers between devices: 3.31 us -> 13.8 us  [from_peer(): return lax.ppermute(x, 'tensor', [(i, i ^ k) for i in range(4)])]
    all_gather x1 -> x0, waiting for transfers between devices: 6 us -> none  [per_device(): tokens = lax.all_gather(output_gradient, 'tensor', axis=0, tiled=True)]
    ppermute x3 -> x6, starting transfers between devices: 3.47 us -> 8 us  [from_peer(): return lax.ppermute(x, 'tensor', [(i, i ^ k) for i in range(4)])]
    all_to_all x2 -> x3, waiting for transfers between devices: 18.4 us -> 14.2 us  [swap(): return lax.all_to_all(chunks, 'dp', 0, 0, tiled=True).reshape(x.shape)]
    pallas_call x0 -> x2, Pallas kernels: none -> 3.76 us  [cut(): call(functools.partial(cut_tokens, ks), [((64, width), BF16)] * len(ks),...]
    pallas_call x1, Pallas kernels: 3.26 us -> 0.73 us  [per_device(): call(project, [((64, width), BF16), ((2 * BLOCK, width), BF16), ((32, 2 *...]
  transfers between devices with their start and end apart: 6 -> 9, of which waited for: 5 -> 7; matrix products, arithmetic and copies ran while one was open for 1% -> 0% of each run, Pallas kernels for 3% -> 5%
where the time goes in v5:
time: 101 us
  starting transfers between devices  37.1 us (37%)
  waiting for transfers between devices  28 us (28%)
  blocking collectives  23.1 us (23%)
  Pallas kernels  10.6 us (10%)
  between operations  1.38 us (1%)
    all_to_all x3, starting transfers between devices, swap(): return lax.all_to_all(chunks, 'dp', 0, 0, tiled=True).reshape(x.shape)  29.1 us
    all_to_all x1, blocking collectives, swap(): return lax.all_to_all(chunks, 'dp', 0, 0, tiled=True).reshape(x.shape)  23.1 us
    all_to_all x3, waiting for transfers between devices, swap(): return lax.all_to_all(chunks, 'dp', 0, 0, tiled=True).reshape(x.shape)  14.2 us
    ppermute x6, waiting for transfers between devices, from_peer(): return lax.ppermute(x, 'tensor', [(i, i ^ k) for i in range(4)])  13.8 us
    ppermute x6, starting transfers between devices, from_peer(): return lax.ppermute(x, 'tensor', [(i, i ^ k) for i in range(4)])  8 us
    pallas_call x2, Pallas kernels, cut(): call(functools.partial(cut_tokens, ks), [((64, width), BF16)] * len(ks),...  3.76 us
  transfers between devices with their start and end apart: 9, of which 7 were waited for; matrix products, arithmetic and copies ran while one was open for 0% of the time, Pallas kernels for 5%

profile of v5, /device:TPU:2, one launch (start us, length us, event | category | flops | bytes accessed | tf_op | source)
XLA Modules:
  0.0 100.9 jit_solution(7724053334601213352)
XLA Ops:
  0.6 1.5 %shard_map.85.packed_hbm = bf16[512,128]{1,0:T(8,128)(2,1)} custom-call(bf16[8,2048]{1,0:T(8,128)(2,1)} %down_hbm.1, bf16[8,2048]{1,0:T(8,128)(2,1)} %up_hbm.1, s32[2,128]{1,0:T(2,128)} %bitcast.21), custom_call_target="tpu_custom_call" | custom-call | tf_op jit(solution)/shard_map/pallas_call | solution.py:181
  2.2 13.2 %all-to-all-start = ((bf16[64,8,128]{2,1,0:T(8,128)(2,1)}), bf16[64,8,128]{2,1,0:T(8,128)(2,1)S(1)}, u32[]{:S(2)}, u32[]{:S(2)}) async-start(bf16[64,8,128]{2,1,0:T(8,128)(2,1)} %bitcast.20), calls=%async_computation | async-start | bytes 262144 | tf_op jit(solution)/shard_map/all_to_all | solution.py:170
  15.4 1.8 %shard_map.87 = (bf16[64,2048]{1,0:T(8,128)(2,1)}, bf16[64,2048]{1,0:T(8,128)(2,1)}) custom-call(s32[1]{0:T(128)} %bitcast.5.place_ref, bf16[64,8192]{1,0:T(8,128)(2,1)} %grad_hbm.3, bf16[512,128]{1,0:T(8,128)(2,1)} %shard_map.85.packed_hbm), custom_call_target="tpu_custom_call" | custom-call | flops 1000 | bytes 1048576 | tf_op jit(solution)/shard_map/pallas_call | solution.py:197
  17.2 0.1 collective-permute-start
  17.3 2.2 %collective-permute-start.1 = (bf16[64,2048]{1,0:T(8,128)(2,1)}, bf16[64,2048]{1,0:T(8,128)(2,1)S(1)}, u32[]{:S(2)}, u32[]{:S(2)}) collective-permute-start(bf16[64,2048]{1,0:T(8,128)(2,1)} %get-tuple-element.23), channel_id=1, source_target_pairs={{0,3},{1,2},{2,1},{3,0},{4,7},{5,6},{6,5},{7,4},{8,11},{9,10},{10,... | collective-permute-start | bytes 786440 | tf_op jit(solution)/shard_map/ppermute | solution.py:174
  19.6 1.9 %shard_map.86 = (bf16[64,2048]{1,0:T(8,128)(2,1)}, bf16[64,2048]{1,0:T(8,128)(2,1)}) custom-call(s32[1]{0:T(128)} %bitcast.5.place_ref, bf16[64,8192]{1,0:T(8,128)(2,1)} %grad_hbm.3, bf16[512,128]{1,0:T(8,128)(2,1)} %shard_map.85.packed_hbm), custom_call_target="tpu_custom_call" | custom-call | flops 10000000000 | bytes 1048576 | tf_op jit(solution)/shard_map/pallas_call | solution.py:197
  22.2 0.0 copy-start.2
  22.2 0.7 copy-done.2
  22.9 3.1 %all-to-all-done = bf16[64,8,128]{2,1,0:T(8,128)(2,1)S(1)} async-done(((bf16[64,8,128]{2,1,0:T(8,128)(2,1)}), bf16[64,8,128]{2,1,0:T(8,128)(2,1)S(1)}, u32[]{:S(2)}, u32[]{:S(2)}) %all-to-all-start) | async-done | bytes 131104 | tf_op jit(solution)/shard_map/all_to_all | solution.py:170
  26.0 0.0 collective-permute-done.one_ref
  26.0 1.7 %collective-permute-done.1.three_ref = bf16[64,2048]{1,0:T(8,128)(2,1)S(1)} collective-permute-done((bf16[64,2048]{1,0:T(8,128)(2,1)}, bf16[64,2048]{1,0:T(8,128)(2,1)S(1)}, u32[]{:S(2)}, u32[]{:S(2)}) %collective-permute-start.1) | collective-permute-done | bytes 262176 | tf_op jit(solution)/shard_map/ppermute | solution.py:174
  27.7 1.0 %shard_map.88 = bf16[1024,128]{1,0:T(8,128)(2,1)} custom-call(bf16[512,128]{1,0:T(8,128)(2,1)S(1)} %bitcast.14), custom_call_target="tpu_custom_call" | custom-call | tf_op jit(solution)/shard_map/pallas_call | solution.py:214
  28.7 11.0 %all-to-all-start.1 = ((bf16[64,16,128]{2,1,0:T(8,128)(2,1)}), bf16[64,16,128]{2,1,0:T(8,128)(2,1)S(1)}, u32[]{:S(2)}, u32[]{:S(2)}) async-start(bf16[64,16,128]{2,1,0:T(8,128)(2,1)} %bitcast.6), calls=%async_computation.1 | async-start | bytes 524288 | tf_op jit(solution)/shard_map/all_to_all | solution.py:170
  39.7 0.0 copy-done.3
  39.7 2.2 %collective-permute-start.2 = (bf16[64,2048]{1,0:T(8,128)(2,1)S(1)}, bf16[64,2048]{1,0:T(8,128)(2,1)S(1)}, u32[]{:S(2)}, u32[]{:S(2)}) collective-permute-start(bf16[64,2048]{1,0:T(8,128)(2,1)S(1)} %copy-done.3), channel_id=1, source_target_pairs={{0,2},{1,3},{2,0},{3,1},{4,6},{5,7},{6,4},{7,5},{8,10},{9,11},{10,... | collective-permute-start | bytes 786440 | tf_op jit(solution)/shard_map/ppermute | solution.py:174
  41.9 9.7 %collective-permute-done.2.two_ref = bf16[64,2048]{1,0:T(8,128)(2,1)S(1)} collective-permute-done((bf16[64,2048]{1,0:T(8,128)(2,1)S(1)}, bf16[64,2048]{1,0:T(8,128)(2,1)S(1)}, u32[]{:S(2)}, u32[]{:S(2)}) %collective-permute-start.2) | collective-permute-done | bytes 262176 | tf_op jit(solution)/shard_map/ppermute | solution.py:174
  51.6 1.9 %all-to-all-done.1 = bf16[64,16,128]{2,1,0:T(8,128)(2,1)S(1)} async-done(((bf16[64,16,128]{2,1,0:T(8,128)(2,1)}), bf16[64,16,128]{2,1,0:T(8,128)(2,1)S(1)}, u32[]{:S(2)}, u32[]{:S(2)}) %all-to-all-start.1) | async-done | bytes 262176 | tf_op jit(solution)/shard_map/all_to_all | solution.py:170
  53.5 0.0 copy-done
  53.5 0.7 shard_map.89
  54.3 0.4 collective-permute-start.5
  54.7 1.9 %collective-permute-start.4 = (f32[32,256]{1,0:T(8,128)S(1)}, f32[32,256]{1,0:T(8,128)S(1)}, u32[]{:S(2)}, u32[]{:S(2)}) collective-permute-start(f32[32,256]{1,0:T(8,128)S(1)} %get-tuple-element.30.own_ref), channel_id=1, source_target_pairs={{0,2},{1,3},{2,0},{3,1},{4,6},{5,7},{6,4},{7,5},{8,10},{9,11},{10,... | collective-permute-start | bytes 98312 | tf_op jit(solution)/shard_map/ppermute | solution.py:174
  56.6 1.1 %collective-permute-start.3 = (f32[32,256]{1,0:T(8,128)S(1)}, f32[32,256]{1,0:T(8,128)S(1)}, u32[]{:S(2)}, u32[]{:S(2)}) collective-permute-start(f32[32,256]{1,0:T(8,128)S(1)} %get-tuple-element.30.own_ref), channel_id=1, source_target_pairs={{0,1},{1,0},{2,3},{3,2},{4,5},{5,4},{6,7},{7,6},{8,9},{9,8},{10,11... | collective-permute-start | bytes 98312 | tf_op jit(solution)/shard_map/ppermute | solution.py:174
  57.7 1.5 %collective-permute-done.5.three_ref = f32[32,256]{1,0:T(8,128)S(1)} collective-permute-done((f32[32,256]{1,0:T(8,128)S(1)}, f32[32,256]{1,0:T(8,128)S(1)}, u32[]{:S(2)}, u32[]{:S(2)}) %collective-permute-start.5) | collective-permute-done | bytes 32800 | tf_op jit(solution)/shard_map/ppermute | solution.py:174
  59.2 0.9 collective-permute-done.4.two_ref
  60.1 0.0 collective-permute-done.3.one_ref
  60.1 0.4 shard_map.90
  60.6 23.1 %all_to_all.20 = bf16[64,16,128]{2,1,0:T(8,128)(2,1)S(1)} all-to-all(bf16[64,16,128]{2,1,0:T(8,128)(2,1)S(1)} %bitcast.19), channel_id=1, replica_groups=mesh['dp'=64,'tensor'=4] {'dp'}, dimensions={0} | all-to-all | bytes 524288 | tf_op jit(solution)/shard_map/all_to_all | solution.py:170
  83.7 1.0 shard_map.92
  84.7 4.9 %all-to-all-start.3 = ((f32[64,4,128]{2,1,0:T(4,128)}), f32[64,4,128]{2,1,0:T(4,128)S(1)}, u32[]{:S(2)}, u32[]{:S(2)}) async-start(f32[64,4,128]{2,1,0:T(4,128)} %bitcast.10), calls=%async_computation.3 | async-start | bytes 262144 | tf_op jit(solution)/shard_map/all_to_all | solution.py:170
  89.6 1.4 %shard_map.91 = bf16[256,2048]{1,0:T(8,128)(2,1)} custom-call(bf16[32,256]{1,0:T(8,128)(2,1)S(1)} %get-tuple-element.32.ranks_ref, bf16[64,2048]{1,0:T(8,128)(2,1)S(1)} %get-tuple-element.33.maps_ref), custom_call_target="tpu_custom_call" | custom-call | flops 33554432 | bytes 2097152 | tf_op jit(solution)/shard_map/pallas_call | solution.py:233
  91.0 9.2 %all-to-all-done.3 = f32[64,4,128]{2,1,0:T(4,128)S(1)} async-done(((f32[64,4,128]{2,1,0:T(4,128)}), f32[64,4,128]{2,1,0:T(4,128)S(1)}, u32[]{:S(2)}, u32[]{:S(2)}) %all-to-all-start.3) | async-done | bytes 131104 | tf_op jit(solution)/shard_map/all_to_all | solution.py:170
  100.2 0.7 shard_map.93
  (5 shorter events, 0.0 us)
Async XLA Ops:
  2.2 23.8 %all-to-all-start = ((bf16[64,8,128]{2,1,0:T(8,128)(2,1)}), bf16[64,8,128]{2,1,0:T(8,128)(2,1)S(1)}, u32[]{:S(2)}, u32[]{:S(2)}) async-start(bf16[64,8,128]{2,1,0:T(8,128)(2,1)} %bitcast.20), calls=%async_computation | async-start | bytes 262144 | tf_op jit(solution)/shard_map/all_to_all | solution.py:170
  17.2 8.8 %collective-permute-start = (bf16[64,2048]{1,0:T(8,128)(2,1)}, bf16[64,2048]{1,0:T(8,128)(2,1)S(1)}, u32[]{:S(2)}, u32[]{:S(2)}) collective-permute-start(bf16[64,2048]{1,0:T(8,128)(2,1)} %get-tuple-element.22), channel_id=1, source_target_pairs={{0,1},{1,0},{2,3},{3,2},{4,5},{5,4},{6,7},{7,6},{8,9},{9,8},{10,11... | collective-permute-start | bytes 786440 | tf_op jit(solution)/shard_map/ppermute | solution.py:174
  17.3 10.3 %collective-permute-start.1 = (bf16[64,2048]{1,0:T(8,128)(2,1)}, bf16[64,2048]{1,0:T(8,128)(2,1)S(1)}, u32[]{:S(2)}, u32[]{:S(2)}) collective-permute-start(bf16[64,2048]{1,0:T(8,128)(2,1)} %get-tuple-element.23), channel_id=1, source_target_pairs={{0,3},{1,2},{2,1},{3,0},{4,7},{5,6},{6,5},{7,4},{8,11},{9,10},{10,... | collective-permute-start | bytes 786440 | tf_op jit(solution)/shard_map/ppermute | solution.py:174
  19.6 34.0 %copy-start = (bf16[256,2048]{1,0:T(8,128)(2,1)S(1)}, bf16[256,2048]{1,0:T(8,128)(2,1)}, u32[]{:S(2)}) copy-start(bf16[256,2048]{1,0:T(8,128)(2,1)} %attn_ref.3) | copy-start | bytes 3145732
  22.2 0.7 copy-start.2
  28.7 11.0 %copy-start.3 = (bf16[64,2048]{1,0:T(8,128)(2,1)S(1)}, bf16[64,2048]{1,0:T(8,128)(2,1)}, u32[]{:S(2)}) copy-start(bf16[64,2048]{1,0:T(8,128)(2,1)} %get-tuple-element.27) | copy-start | bytes 786436
  28.7 24.8 %copy-start.1 = (bf16[64,2048]{1,0:T(8,128)(2,1)S(1)}, bf16[64,2048]{1,0:T(8,128)(2,1)}, u32[]{:S(2)}) copy-start(bf16[64,2048]{1,0:T(8,128)(2,1)} %get-tuple-element.25.own_ref) | copy-start | bytes 786436
  28.7 24.8 %all-to-all-start.1 = ((bf16[64,16,128]{2,1,0:T(8,128)(2,1)}), bf16[64,16,128]{2,1,0:T(8,128)(2,1)S(1)}, u32[]{:S(2)}, u32[]{:S(2)}) async-start(bf16[64,16,128]{2,1,0:T(8,128)(2,1)} %bitcast.6), calls=%async_computation.1 | async-start | bytes 524288 | tf_op jit(solution)/shard_map/all_to_all | solution.py:170
  39.7 11.9 %collective-permute-start.2 = (bf16[64,2048]{1,0:T(8,128)(2,1)S(1)}, bf16[64,2048]{1,0:T(8,128)(2,1)S(1)}, u32[]{:S(2)}, u32[]{:S(2)}) collective-permute-start(bf16[64,2048]{1,0:T(8,128)(2,1)S(1)} %copy-done.3), channel_id=1, source_target_pairs={{0,2},{1,3},{2,0},{3,1},{4,6},{5,7},{6,4},{7,5},{8,10},{9,11},{10,... | collective-permute-start | bytes 786440 | tf_op jit(solution)/shard_map/ppermute | solution.py:174
  54.3 4.9 %collective-permute-start.5 = (f32[32,256]{1,0:T(8,128)S(1)}, f32[32,256]{1,0:T(8,128)S(1)}, u32[]{:S(2)}, u32[]{:S(2)}) collective-permute-start(f32[32,256]{1,0:T(8,128)S(1)} %get-tuple-element.30.own_ref), channel_id=1, source_target_pairs={{0,3},{1,2},{2,1},{3,0},{4,7},{5,6},{6,5},{7,4},{8,11},{9,10},{10,... | collective-permute-start | bytes 98312 | tf_op jit(solution)/shard_map/ppermute | solution.py:174
  54.7 5.4 %collective-permute-start.4 = (f32[32,256]{1,0:T(8,128)S(1)}, f32[32,256]{1,0:T(8,128)S(1)}, u32[]{:S(2)}, u32[]{:S(2)}) collective-permute-start(f32[32,256]{1,0:T(8,128)S(1)} %get-tuple-element.30.own_ref), channel_id=1, source_target_pairs={{0,2},{1,3},{2,0},{3,1},{4,6},{5,7},{6,4},{7,5},{8,10},{9,11},{10,... | collective-permute-start | bytes 98312 | tf_op jit(solution)/shard_map/ppermute | solution.py:174
  56.6 3.5 %collective-permute-start.3 = (f32[32,256]{1,0:T(8,128)S(1)}, f32[32,256]{1,0:T(8,128)S(1)}, u32[]{:S(2)}, u32[]{:S(2)}) collective-permute-start(f32[32,256]{1,0:T(8,128)S(1)} %get-tuple-element.30.own_ref), channel_id=1, source_target_pairs={{0,1},{1,0},{2,3},{3,2},{4,5},{5,4},{6,7},{7,6},{8,9},{9,8},{10,11... | collective-permute-start | bytes 98312 | tf_op jit(solution)/shard_map/ppermute | solution.py:174
  84.7 15.5 %all-to-all-start.3 = ((f32[64,4,128]{2,1,0:T(4,128)}), f32[64,4,128]{2,1,0:T(4,128)S(1)}, u32[]{:S(2)}, u32[]{:S(2)}) async-start(f32[64,4,128]{2,1,0:T(4,128)} %bitcast.10), calls=%async_computation.3 | async-start | bytes 262144 | tf_op jit(solution)/shard_map/all_to_all | solution.py:170

commit v6 on v4

--- a/solution.py
+++ b/solution.py
@@ -26,8 +26,15 @@
     return pl.ds(first, size, stride=stride)
 
 
-def pack_tables(down_hbm, up_hbm, label_hbm, out_ref, down_ref, up_ref, label_ref, rows_f, out_f, sems):
-    moves = ((label_hbm, label_ref), (down_hbm, down_ref), (up_hbm, up_ref))
+def pack_tables(
+    place_ref, down_hbm, up_hbm, label_hbm, grad_hbm,
+    out_ref, near_ref, far_ref, down_ref, up_ref, label_ref, rows_f, out_f, sems
+):
+    width = near_ref.shape[1]
+    moves = [(label_hbm, label_ref), (down_hbm, down_ref), (up_hbm, up_ref)]
+    for k, piece in ((1, near_ref), (2, far_ref.at[pl.ds(0, 64), :]), (3, far_ref.at[pl.ds(64, 64), :])):
+        first = pl.multiple_of(lax.bitwise_xor(place_ref[0], k) * width, width)
+        moves.append((grad_hbm.at[:, pl.ds(first, width)], piece))
     copies = [pltpu.make_async_copy(src, dst, sems.at[n]) for n, (src, dst) in enumerate(moves)]
     for copy in copies:
         copy.start()
@@ -45,6 +52,8 @@
         for i in range(2):
             out_f[rows_of(2 * m + i, PEERS, 8), :] = rows_f[rows_of(i, PEERS, 2), :]
     out_ref[...] = out_f[...].astype(BF16)
+    for copy in copies[3:]:
+        copy.wait()
 
 
 def pick_rows(in_ref, out_ref, in_f, out_f):
@@ -61,13 +70,15 @@
     out_ref[...] = out_f[...].astype(BF16)
 
 
-def project(
-    place_ref, picked_ref, attn_ref, tokens_hbm, live_ref, maps_ref, grad_ref, part_ref, sem
-):
+def project(place_ref, picked_ref, attn_ref, tokens_hbm, one_ref, two_ref, three_ref, maps_ref, grad_ref, part_ref, sem):
+    me = place_ref[0]
     width = grad_ref.shape[1]
-    first = pl.multiple_of(place_ref[0] * width, width)
-    copy = pltpu.make_async_copy(tokens_hbm.at[:, pl.ds(first, width)], grad_ref, sem)
+    own = tokens_hbm.at[:, pl.ds(pl.multiple_of(me * width, width), width)]
+    copy = pltpu.make_async_copy(own, grad_ref.at[pl.ds(pl.multiple_of(me * 64, 64), 64), :], sem)
     copy.start()
+    for k, piece in ((1, one_ref), (2, two_ref), (3, three_ref)):
+        first = pl.multiple_of(lax.bitwise_xor(me, k) * 64, 64)
+        grad_ref[pl.ds(first, 64), :] = piece[:64, :]
     for c in range(BANDS):
         rows = picked_ref[c * 64:(c + 1) * 64, :].astype(F32).reshape(QUARTERS, 2, 8, LANES)
         for b in range(2):
@@ -80,16 +91,16 @@
         block = slice(b * BLOCK, (b + 1) * BLOCK)
         inner = lax.dot_general(maps, attn_ref[block, :], over_last, preferred_element_type=F32)
         outer = lax.dot_general(maps, grad_ref[block, :], over_last, preferred_element_type=F32)
-        part_ref[:, block] = jnp.where(live_ref[b:b + 1, :] > 0, jnp.where((row & 2) == 0, inner, outer), 0.0)
-
-
-def make_terms(own_ref, one_ref, two_ref, three_ref, attn_ref, grad_ref, ranks_ref, term_ref):
+        part_ref[:, block] = jnp.where((row & 2) == 0, inner, outer)
+
+
+def make_terms(own_ref, one_ref, two_ref, three_ref, live_ref, attn_ref, grad_ref, ranks_ref, term_ref):
     total = (own_ref[...] + one_ref[...]) + (two_ref[...] + three_ref[...])
     row = lax.broadcasted_iota(jnp.int32, (32, LANES), 0)
     terms = []
     for b in range(2):
         block = slice(b * BLOCK, (b + 1) * BLOCK)
-        ranks = total[:, block].astype(BF16)
+        ranks = jnp.where(live_ref[b:b + 1, :] > 0, total[:, block], 0.0).astype(BF16)
         ranks_ref[:, block] = ranks
         down = jnp.dot(ranks, attn_ref[block, :], preferred_element_type=F32)
         up = jnp.dot(ranks, grad_ref[block, :], preferred_element_type=F32)
@@ -166,25 +177,26 @@
     width = attn.shape[1]
     me = lax.axis_index("tensor")
     me = me.astype(jnp.int32).reshape(1)
-    labels = adapter_of_row.reshape(2, BLOCK)
-    tokens = lax.all_gather(output_gradient, "tensor", axis=0, tiled=True)
-    (packed,) = call(
+    packed, near, far = call(
         pack_tables,
-        [((8 * PEERS, LANES), BF16)],
-        [ANY] * 3,
+        [((8 * PEERS, LANES), BF16), ((64, width), BF16), ((128, width), BF16)],
+        [SMEM] + [ANY] * 4,
         [
             pltpu.VMEM((8, width), BF16),
             pltpu.VMEM((8, width), BF16),
             pltpu.VMEM((2, BLOCK), jnp.int32),
             pltpu.VMEM((2 * PEERS, LANES), F32),
             pltpu.VMEM((8 * PEERS, LANES), F32),
-            pltpu.SemaphoreType.DMA((3,)),
+            pltpu.SemaphoreType.DMA((6,)),
         ],
         limit=56 * MIB,
-    )(down_weight, up_weight, labels)
+    )(me, down_weight, up_weight, adapter_of_row.reshape(2, BLOCK), output_gradient)
     live = (adapter_of_row >= 0) & (jnp.arange(2 * BLOCK, dtype=jnp.int32) < lengths[0])
     live = live.astype(F32).reshape(2, BLOCK)
-    tables, me, live = lax.optimization_barrier((swap(packed), me, live))
+    near, far = from_peer(near, 1), from_peer(far, 2)
+    tables = swap(packed)
+    tables, near, far = lax.optimization_barrier((tables, near, far))
+    pieces = [near, far, from_peer(far[64:], 1)]
     (picked,) = call(
         pick_rows,
         [((16 * PEERS, LANES), BF16)],
@@ -195,16 +207,15 @@
     maps, grad, part = call(
         project,
         [((64, width), BF16), ((2 * BLOCK, width), BF16), ((32, 2 * BLOCK), F32)],
-        [SMEM, VMEM, VMEM, ANY, VMEM],
+        [SMEM, VMEM, VMEM, ANY, VMEM, VMEM, VMEM],
         [pltpu.SemaphoreType.DMA(())],
-        limit=52 * MIB,
-    )(me, picked, attn, tokens, live)
+    )(me, picked, attn, output_gradient, *pieces)
     parts = [part] + [from_peer(part, k) for k in (1, 2, 3)]
     ranks, terms = call(
         make_terms,
         [((32, 2 * BLOCK), BF16), ((16 * PEERS, LANES), BF16)],
-        [VMEM] * 6,
-    )(*parts, attn, grad)
+        [VMEM] * 7,
+    )(*parts, live, attn, grad)
     terms = swap(terms)
     (attention_gradient,) = call(
         go_back,

time: 115 us -> 92.5 us (0.80)
  between operations: 14.7 us -> 1.41 us
  starting transfers between devices: 21.6 us -> 15.9 us
  waiting for transfers between devices: 28.4 us -> 23.9 us
  blocking collectives: 40.2 us -> 43.2 us
    all_to_all x2, starting transfers between devices: 18.1 us -> 10.1 us  [swap(): return lax.all_to_all(chunks, 'dp', 0, 0, tiled=True).reshape(x.shape)]
    all_gather x1 -> x0, waiting for transfers between devices: 6 us -> none  [per_device(): tokens = lax.all_gather(output_gradient, 'tensor', axis=0, tiled=True)]
    all_to_all x2, blocking collectives: 40.2 us -> 43.2 us  [swap(): return lax.all_to_all(chunks, 'dp', 0, 0, tiled=True).reshape(x.shape)]
    pallas_call x1, Pallas kernels: 3.26 us -> 0.94 us  [per_device(): call(project, [((64, width), BF16), ((2 * BLOCK, width), BF16), ((32, 2 *...]
    ppermute x3 -> x6, starting transfers between devices: 3.47 us -> 5.77 us  [from_peer(): return lax.ppermute(x, 'tensor', [(i, i ^ k) for i in range(4)])]
    all_to_all x2, waiting for transfers between devices: 18.4 us -> 20 us  [swap(): return lax.all_to_all(chunks, 'dp', 0, 0, tiled=True).reshape(x.shape)]
    ppermute x3 -> x6, waiting for transfers between devices: 3.31 us -> 3.86 us  [from_peer(): return lax.ppermute(x, 'tensor', [(i, i ^ k) for i in range(4)])]
  transfers between devices with their start and end apart: 6 -> 8, of which waited for: 5 -> 5; matrix products, arithmetic and copies ran while one was open for 1% -> 0% of each run, Pallas kernels for 3% -> 2%
where the time goes in v6:
time: 92.5 us; the launch traced here: 92.2 us
  blocking collectives  43.2 us (47%)
  waiting for transfers between devices  23.9 us (26%)
  starting transfers between devices  15.9 us (17%)
  Pallas kernels  7.76 us (8%)
  between operations  1.41 us (2%)
    all_to_all x2, blocking collectives, swap(): return lax.all_to_all(chunks, 'dp', 0, 0, tiled=True).reshape(x.shape)  43.2 us
    all_to_all x2, waiting for transfers between devices, swap(): return lax.all_to_all(chunks, 'dp', 0, 0, tiled=True).reshape(x.shape)  20 us
    all_to_all x2, starting transfers between devices, swap(): return lax.all_to_all(chunks, 'dp', 0, 0, tiled=True).reshape(x.shape)  10.1 us
    ppermute x6, starting transfers between devices, from_peer(): return lax.ppermute(x, 'tensor', [(i, i ^ k) for i in range(4)])  5.77 us
    ppermute x6, waiting for transfers between devices, from_peer(): return lax.ppermute(x, 'tensor', [(i, i ^ k) for i in range(4)])  3.86 us
    pallas_call x1, Pallas kernels, per_device(): call(pack_tables, [((8 * PEERS, LANES), BF16), ((64, width), BF16), ((128...  2.24 us
  transfers between devices with their start and end apart: 8, of which 5 were waited for; matrix products, arithmetic and copies ran while one was open for 0% of the time, Pallas kernels for 2%

profile of v6, /device:TPU:2, one launch (start us, length us, event | category | flops | bytes accessed | tf_op | source)
XLA Modules:
  0.0 92.2 jit_solution(7936172862039020934)
XLA Ops:
  0.6 0.0 copy-start.1
  0.6 2.2 %shard_map.85 = (bf16[512,128]{1,0:T(8,128)(2,1)}, bf16[64,2048]{1,0:T(8,128)(2,1)}, bf16[128,2048]{1,0:T(8,128)(2,1)}) custom-call(s32[1]{0:T(128)} %bitcast.place_ref, bf16[8,2048]{1,0:T(8,128)(2,1)} %down_hbm.1, bf16[8,2048]{1,0:T(8,128)(2,1)} %up_hbm.1, s32[2,128]{1,0:T(2,128)} %bitcast.21, bf16[64,8192]{1,0:T(8,128)(2,1)} %tokens_hbm.1), custom_call_target="tpu_custom_call" | custom-call | tf_op jit(solution)/shard_map/pallas_call | solution.py:180
  2.9 0.0 copy-start
  2.9 2.2 %collective-permute-start.1 = (bf16[128,2048]{1,0:T(8,128)(2,1)}, bf16[128,2048]{1,0:T(8,128)(2,1)S(1)}, u32[]{:S(2)}, u32[]{:S(2)}) collective-permute-start(bf16[128,2048]{1,0:T(8,128)(2,1)} %get-tuple-element.18), channel_id=1, source_target_pairs={{0,2},{1,3},{2,0},{3,1},{4,6},{5,7},{6,4},{7,5},{8,10},{9,11},{10,... | collective-permute-start | bytes 1572872 | tf_op jit(solution)/shard_map/ppermute | solution.py:173
  5.1 0.0 collective-permute-start
  5.1 24.5 %all_to_all.20 = bf16[64,8,128]{2,1,0:T(8,128)(2,1)S(1)} all-to-all(bf16[64,8,128]{2,1,0:T(8,128)(2,1)} %bitcast.20), channel_id=1, replica_groups=mesh['dp'=64,'tensor'=4] {'dp'}, dimensions={0} | all-to-all | bytes 262144 | tf_op jit(solution)/shard_map/all_to_all | solution.py:169
  29.6 0.0 collective-permute-done.one_ref
  29.6 0.0 collective-permute-done.1.two_ref
  29.6 1.0 %shard_map.86 = bf16[1024,128]{1,0:T(8,128)(2,1)} custom-call(bf16[512,128]{1,0:T(8,128)(2,1)S(1)} %bitcast.14), custom_call_target="tpu_custom_call" | custom-call | tf_op jit(solution)/shard_map/pallas_call | solution.py:200
  30.6 5.1 %all-to-all-start.1 = ((bf16[64,16,128]{2,1,0:T(8,128)(2,1)}), bf16[64,16,128]{2,1,0:T(8,128)(2,1)S(1)}, u32[]{:S(2)}, u32[]{:S(2)}) async-start(bf16[64,16,128]{2,1,0:T(8,128)(2,1)} %bitcast.4), calls=%async_computation.1 | async-start | bytes 524288 | tf_op jit(solution)/shard_map/all_to_all | solution.py:169
  35.8 0.1 collective-permute-start.2
  36.6 0.9 collective-permute-done.2.three_ref
  37.4 10.8 %all-to-all-done.1 = bf16[64,16,128]{2,1,0:T(8,128)(2,1)S(1)} async-done(((bf16[64,16,128]{2,1,0:T(8,128)(2,1)}), bf16[64,16,128]{2,1,0:T(8,128)(2,1)S(1)}, u32[]{:S(2)}, u32[]{:S(2)}) %all-to-all-start.1) | async-done | bytes 262176 | tf_op jit(solution)/shard_map/all_to_all | solution.py:169
  48.3 0.0 copy-done.1
  48.3 0.9 %shard_map.87 = (bf16[64,2048]{1,0:T(8,128)(2,1)S(1)}, bf16[256,2048]{1,0:T(8,128)(2,1)S(1)}, f32[32,256]{1,0:T(8,128)S(1)}) custom-call(s32[1]{0:T(128)} %bitcast.place_ref, bf16[1024,128]{1,0:T(8,128)(2,1)S(1)} %bitcast.16, bf16[256,2048]{1,0:T(8,128)(2,1)S(1)} %copy-done.1, bf16[64,8192]{1,0:T(8,128)(2,1)S(1)} %copy-done, ...), custom_call_target="tpu_custom_call" | custom-call | tf_op jit(solution)/shard_map/pallas_call | solution.py:207
  49.2 0.0 copy-start.2
  49.3 0.0 copy-start.4
  49.3 0.1 collective-permute-start.3
  49.4 1.5 %collective-permute-start.4 = (f32[32,256]{1,0:T(8,128)S(1)}, f32[32,256]{1,0:T(8,128)S(1)}, u32[]{:S(2)}, u32[]{:S(2)}) collective-permute-start(f32[32,256]{1,0:T(8,128)S(1)} %get-tuple-element.22.own_ref), channel_id=1, source_target_pairs={{0,2},{1,3},{2,0},{3,1},{4,6},{5,7},{6,4},{7,5},{8,10},{9,11},{10,... | collective-permute-start | bytes 98312 | tf_op jit(solution)/shard_map/ppermute | solution.py:173
  50.9 1.9 %collective-permute-start.5 = (f32[32,256]{1,0:T(8,128)S(1)}, f32[32,256]{1,0:T(8,128)S(1)}, u32[]{:S(2)}, u32[]{:S(2)}) collective-permute-start(f32[32,256]{1,0:T(8,128)S(1)} %get-tuple-element.22.own_ref), channel_id=1, source_target_pairs={{0,3},{1,2},{2,1},{3,0},{4,7},{5,6},{6,5},{7,4},{8,11},{9,10},{10,... | collective-permute-start | bytes 98312 | tf_op jit(solution)/shard_map/ppermute | solution.py:173
  52.7 0.0 collective-permute-done.3.one_ref
  52.7 2.1 %collective-permute-done.4.two_ref = f32[32,256]{1,0:T(8,128)S(1)} collective-permute-done((f32[32,256]{1,0:T(8,128)S(1)}, f32[32,256]{1,0:T(8,128)S(1)}, u32[]{:S(2)}, u32[]{:S(2)}) %collective-permute-start.4) | collective-permute-done | bytes 32800 | tf_op jit(solution)/shard_map/ppermute | solution.py:173
  54.9 0.9 collective-permute-done.5.three_ref
  55.7 0.4 shard_map.88
  56.2 0.0 copy-done.2
  56.2 18.7 %all_to_all.21 = bf16[64,16,128]{2,1,0:T(8,128)(2,1)S(1)} all-to-all(bf16[64,16,128]{2,1,0:T(8,128)(2,1)S(1)} %bitcast.19), channel_id=1, replica_groups=mesh['dp'=64,'tensor'=4] {'dp'}, dimensions={0} | all-to-all | bytes 524288 | tf_op jit(solution)/shard_map/all_to_all | solution.py:169
  74.9 1.0 %shard_map.90 = f32[256,128]{1,0:T(8,128)} custom-call(bf16[1024,128]{1,0:T(8,128)(2,1)S(1)} %bitcast.17, bf16[512,128]{1,0:T(8,128)(2,1)S(1)} %bitcast.15), custom_call_target="tpu_custom_call" | custom-call | tf_op jit(solution)/shard_map/pallas_call | solution.py:226
  75.9 5.0 %all-to-all-start.3 = ((f32[64,4,128]{2,1,0:T(4,128)}), f32[64,4,128]{2,1,0:T(4,128)S(1)}, u32[]{:S(2)}, u32[]{:S(2)}) async-start(f32[64,4,128]{2,1,0:T(4,128)} %bitcast.10), calls=%async_computation.3 | async-start | bytes 262144 | tf_op jit(solution)/shard_map/all_to_all | solution.py:169
  80.9 0.0 copy-done.3
  80.9 1.4 %shard_map.89 = bf16[256,2048]{1,0:T(8,128)(2,1)} custom-call(bf16[32,256]{1,0:T(8,128)(2,1)S(1)} %get-tuple-element.24.ranks_ref, bf16[64,2048]{1,0:T(8,128)(2,1)S(1)} %copy-done.3), custom_call_target="tpu_custom_call" | custom-call | flops 33554432 | bytes 2097152 | tf_op jit(solution)/shard_map/pallas_call | solution.py:220
  82.3 9.2 %all-to-all-done.3 = f32[64,4,128]{2,1,0:T(4,128)S(1)} async-done(((f32[64,4,128]{2,1,0:T(4,128)}), f32[64,4,128]{2,1,0:T(4,128)S(1)}, u32[]{:S(2)}, u32[]{:S(2)}) %all-to-all-start.3) | async-done | bytes 131104 | tf_op jit(solution)/shard_map/all_to_all | solution.py:169
  91.5 0.7 shard_map.91
  (5 shorter events, 0.0 us)
Async XLA Ops:
  0.6 47.7 %copy-start.1 = (bf16[256,2048]{1,0:T(8,128)(2,1)S(1)}, bf16[256,2048]{1,0:T(8,128)(2,1)}, u32[]{:S(2)}) copy-start(bf16[256,2048]{1,0:T(8,128)(2,1)} %attn_ref.3) | copy-start | bytes 3145732
  2.9 45.4 %copy-start = (bf16[64,8192]{1,0:T(8,128)(2,1)S(1)}, bf16[64,8192]{1,0:T(8,128)(2,1)}, u32[]{:S(2)}) copy-start(bf16[64,8192]{1,0:T(8,128)(2,1)} %tokens_hbm.1) | copy-start | bytes 3145732
  2.9 26.7 %collective-permute-start.1 = (bf16[128,2048]{1,0:T(8,128)(2,1)}, bf16[128,2048]{1,0:T(8,128)(2,1)S(1)}, u32[]{:S(2)}, u32[]{:S(2)}) collective-permute-start(bf16[128,2048]{1,0:T(8,128)(2,1)} %get-tuple-element.18), channel_id=1, source_target_pairs={{0,2},{1,3},{2,0},{3,1},{4,6},{5,7},{6,4},{7,5},{8,10},{9,11},{10,... | collective-permute-start | bytes 1572872 | tf_op jit(solution)/shard_map/ppermute | solution.py:173
  5.1 24.5 %collective-permute-start = (bf16[64,2048]{1,0:T(8,128)(2,1)}, bf16[64,2048]{1,0:T(8,128)(2,1)S(1)}, u32[]{:S(2)}, u32[]{:S(2)}) collective-permute-start(bf16[64,2048]{1,0:T(8,128)(2,1)} %get-tuple-element.17), channel_id=1, source_target_pairs={{0,1},{1,0},{2,3},{3,2},{4,5},{5,4},{6,7},{7,6},{8,9},{9,8},{10,11... | collective-permute-start | bytes 786440 | tf_op jit(solution)/shard_map/ppermute | solution.py:173
  30.6 17.6 %all-to-all-start.1 = ((bf16[64,16,128]{2,1,0:T(8,128)(2,1)}), bf16[64,16,128]{2,1,0:T(8,128)(2,1)S(1)}, u32[]{:S(2)}, u32[]{:S(2)}) async-start(bf16[64,16,128]{2,1,0:T(8,128)(2,1)} %bitcast.4), calls=%async_computation.1 | async-start | bytes 524288 | tf_op jit(solution)/shard_map/all_to_all | solution.py:169
  35.8 1.6 %collective-permute-start.2 = (bf16[64,2048]{1,0:T(8,128)(2,1)S(1)}, bf16[64,2048]{1,0:T(8,128)(2,1)S(1)}, u32[]{:S(2)}, u32[]{:S(2)}) collective-permute-start(bf16[64,2048]{1,0:T(8,128)(2,1)S(1)} %slice.3), channel_id=1, source_target_pairs={{0,1},{1,0},{2,3},{3,2},{4,5},{5,4},{6,7},{7,6},{8,9},{9,8},{10,11... | collective-permute-start | bytes 786440 | tf_op jit(solution)/shard_map/ppermute | solution.py:173
  49.2 6.9 %copy-start.2 = (bf16[64,2048]{1,0:T(8,128)(2,1)}, bf16[64,2048]{1,0:T(8,128)(2,1)S(1)}, u32[]{:S(2)}) copy-start(bf16[64,2048]{1,0:T(8,128)(2,1)S(1)} %get-tuple-element.25.maps_ref) | copy-start | bytes 786436
  49.3 3.5 %copy-start.4 = (s32[256]{0:T(256)S(1)}, s32[256]{0:T(256)}, u32[]{:S(2)}) copy-start(s32[256]{0:T(256)} %param.10) | copy-start | bytes 3076
  49.3 3.5 %collective-permute-start.3 = (f32[32,256]{1,0:T(8,128)S(1)}, f32[32,256]{1,0:T(8,128)S(1)}, u32[]{:S(2)}, u32[]{:S(2)}) collective-permute-start(f32[32,256]{1,0:T(8,128)S(1)} %get-tuple-element.22.own_ref), channel_id=1, source_target_pairs={{0,1},{1,0},{2,3},{3,2},{4,5},{5,4},{6,7},{7,6},{8,9},{9,8},{10,11... | collective-permute-start | bytes 98312 | tf_op jit(solution)/shard_map/ppermute | solution.py:173
  49.4 5.5 %collective-permute-start.4 = (f32[32,256]{1,0:T(8,128)S(1)}, f32[32,256]{1,0:T(8,128)S(1)}, u32[]{:S(2)}, u32[]{:S(2)}) collective-permute-start(f32[32,256]{1,0:T(8,128)S(1)} %get-tuple-element.22.own_ref), channel_id=1, source_target_pairs={{0,2},{1,3},{2,0},{3,1},{4,6},{5,7},{6,4},{7,5},{8,10},{9,11},{10,... | collective-permute-start | bytes 98312 | tf_op jit(solution)/shard_map/ppermute | solution.py:173
  50.9 4.9 %collective-permute-start.5 = (f32[32,256]{1,0:T(8,128)S(1)}, f32[32,256]{1,0:T(8,128)S(1)}, u32[]{:S(2)}, u32[]{:S(2)}) collective-permute-start(f32[32,256]{1,0:T(8,128)S(1)} %get-tuple-element.22.own_ref), channel_id=1, source_target_pairs={{0,3},{1,2},{2,1},{3,0},{4,7},{5,6},{6,5},{7,4},{8,11},{9,10},{10,... | collective-permute-start | bytes 98312 | tf_op jit(solution)/shard_map/ppermute | solution.py:173
  75.9 5.0 %copy-start.3 = (bf16[64,2048]{1,0:T(8,128)(2,1)S(1)}, bf16[64,2048]{1,0:T(8,128)(2,1)}, u32[]{:S(2)}) copy-start(bf16[64,2048]{1,0:T(8,128)(2,1)} %copy-done.2) | copy-start | bytes 786436
  75.9 15.6 %all-to-all-start.3 = ((f32[64,4,128]{2,1,0:T(4,128)}), f32[64,4,128]{2,1,0:T(4,128)S(1)}, u32[]{:S(2)}, u32[]{:S(2)}) async-start(f32[64,4,128]{2,1,0:T(4,128)} %bitcast.10), calls=%async_computation.3 | async-start | bytes 262144 | tf_op jit(solution)/shard_map/all_to_all | solution.py:169

commit v7 on v6

--- a/solution.py
+++ b/solution.py
@@ -83,15 +83,23 @@
         rows = picked_ref[c * 64:(c + 1) * 64, :].astype(F32).reshape(QUARTERS, 2, 8, LANES)
         for b in range(2):
             maps_ref[b * 32:(b + 1) * 32, c * LANES:(c + 1) * LANES] = rows[:, b].reshape(32, LANES).astype(BF16)
-    copy.wait()
     row = lax.broadcasted_iota(jnp.int32, (32, BLOCK), 0)
     over_last = (((1,), (1,)), ((), ()))
+    inners = [
+        lax.dot_general(
+            maps_ref[b * 32:(b + 1) * 32, :],
+            attn_ref[b * BLOCK:(b + 1) * BLOCK, :],
+            over_last,
+            preferred_element_type=F32,
+        )
+        for b in range(2)
+    ]
+    copy.wait()
     for b in range(2):
         maps = maps_ref[b * 32:(b + 1) * 32, :]
         block = slice(b * BLOCK, (b + 1) * BLOCK)
-        inner = lax.dot_general(maps, attn_ref[block, :], over_last, preferred_element_type=F32)
         outer = lax.dot_general(maps, grad_ref[block, :], over_last, preferred_element_type=F32)
-        part_ref[:, block] = jnp.where((row & 2) == 0, inner, outer)
+        part_ref[:, block] = jnp.where((row & 2) == 0, inners[b], outer)
 
 
 def make_terms(own_ref, one_ref, two_ref, three_ref, live_ref, attn_ref, grad_ref, ranks_ref, term_ref):
@@ -152,12 +160,12 @@
             map_ref[:, c * LANES:(c + 1) * LANES] = rows_f[c * 8:(c + 1) * 8, :]
 
 
-def call(kernel, outs, specs, scratch=(), cost=None, limit=40 * MIB):
+def call(kernel, outs, specs, scratch=(), cost=None, limit=40 * MIB, places=None):
     return pl.pallas_call(
         kernel,
         out_shape=[jax.ShapeDtypeStruct(shape, dtype) for shape, dtype in outs],
         in_specs=specs,
-        out_specs=[VMEM] * len(outs),
+        out_specs=places or [VMEM] * len(outs),
         scratch_shapes=scratch,
         compiler_params=pltpu.CompilerParams(vmem_limit_bytes=limit),
         cost_estimate=cost,
@@ -190,13 +198,15 @@
             pltpu.SemaphoreType.DMA((6,)),
         ],
         limit=56 * MIB,
+        places=[VMEM, ANY, ANY],
     )(me, down_weight, up_weight, adapter_of_row.reshape(2, BLOCK), output_gradient)
     live = (adapter_of_row >= 0) & (jnp.arange(2 * BLOCK, dtype=jnp.int32) < lengths[0])
     live = live.astype(F32).reshape(2, BLOCK)
     near, far = from_peer(near, 1), from_peer(far, 2)
     tables = swap(packed)
     tables, near, far = lax.optimization_barrier((tables, near, far))
-    pieces = [near, far, from_peer(far[64:], 1)]
+    odd, live = lax.optimization_barrier((from_peer(far[64:], 1), live))
+    pieces = [near, far, odd]
     (picked,) = call(
         pick_rows,
         [((16 * PEERS, LANES), BF16)],

time: 92.5 us -> 115 us (1.24)
  Pallas kernels: 7.76 us -> 31.2 us
  waiting for transfers between devices: 23.9 us -> 22.4 us
    pallas_call x1, Pallas kernels: 2.24 us -> 25.6 us  [per_device(): call(pack_tables, [((8 * PEERS, LANES), BF16), ((64, width), BF16), ((128...]
    ppermute x6, waiting for transfers between devices: 3.86 us -> 2.35 us  [from_peer(): return lax.ppermute(x, 'tensor', [(i, i ^ k) for i in range(4)])]
  transfers between devices with their start and end apart: 8 -> 8, of which waited for: 5 -> 5; matrix products, arithmetic and copies ran while one was open for 0% -> 0% of each run, Pallas kernels for 2% -> 1%
where the time goes in v7:
time: 115 us
  blocking collectives  43.3 us (38%)
  Pallas kernels  31.2 us (27%)
  waiting for transfers between devices  22.4 us (19%)
  starting transfers between devices  15.8 us (14%)
  between operations  1.4 us (1%)
    all_to_all x2, blocking collectives, swap(): return lax.all_to_all(chunks, 'dp', 0, 0, tiled=True).reshape(x.shape)  43.3 us
    pallas_call x1, Pallas kernels, per_device(): call(pack_tables, [((8 * PEERS, LANES), BF16), ((64, width), BF16), ((128...  25.6 us
    all_to_all x2, waiting for transfers between devices, swap(): return lax.all_to_all(chunks, 'dp', 0, 0, tiled=True).reshape(x.shape)  20 us
    all_to_all x2, starting transfers between devices, swap(): return lax.all_to_all(chunks, 'dp', 0, 0, tiled=True).reshape(x.shape)  10.1 us
    ppermute x6, starting transfers between devices, from_peer(): return lax.ppermute(x, 'tensor', [(i, i ^ k) for i in range(4)])  5.75 us
    ppermute x6, waiting for transfers between devices, from_peer(): return lax.ppermute(x, 'tensor', [(i, i ^ k) for i in range(4)])  2.35 us
  transfers between devices with their start and end apart: 8, of which 5 were waited for; matrix products, arithmetic and copies ran while one was open for 0% of the time, Pallas kernels for 1%

profile of v7, /device:TPU:2, one launch (start us, length us, event | category | flops | bytes accessed | tf_op | source)
XLA Modules:
  0.0 114.8 jit_solution(2755612890665659948)
XLA Ops:
  0.6 0.0 copy-start.1
  0.6 25.6 %shard_map.85 = (bf16[512,128]{1,0:T(8,128)(2,1)}, bf16[64,2048]{1,0:T(8,128)(2,1)}, bf16[128,2048]{1,0:T(8,128)(2,1)}) custom-call(s32[1]{0:T(128)} %bitcast.place_ref, bf16[8,2048]{1,0:T(8,128)(2,1)} %down_hbm.1, bf16[8,2048]{1,0:T(8,128)(2,1)} %up_hbm.1, s32[2,128]{1,0:T(2,128)} %bitcast.21, bf16[64,8192]{1,0:T(8,128)(2,1)} %tokens_hbm.1), custom_call_target="tpu_custom_call" | custom-call | tf_op jit(solution)/shard_map/pallas_call | solution.py:188
  26.3 0.0 copy-start
  26.3 2.2 %collective-permute-start.1 = (bf16[128,2048]{1,0:T(8,128)(2,1)}, bf16[128,2048]{1,0:T(8,128)(2,1)S(1)}, u32[]{:S(2)}, u32[]{:S(2)}) collective-permute-start(bf16[128,2048]{1,0:T(8,128)(2,1)} %get-tuple-element.20), channel_id=1, source_target_pairs={{0,2},{1,3},{2,0},{3,1},{4,6},{5,7},{6,4},{7,5},{8,10},{9,11},{10,... | collective-permute-start | bytes 1572872 | tf_op jit(solution)/shard_map/ppermute | solution.py:181
  28.5 0.0 collective-permute-start
  28.5 24.5 %all_to_all.20 = bf16[64,8,128]{2,1,0:T(8,128)(2,1)S(1)} all-to-all(bf16[64,8,128]{2,1,0:T(8,128)(2,1)} %bitcast.20), channel_id=1, replica_groups=mesh['dp'=64,'tensor'=4] {'dp'}, dimensions={0} | all-to-all | bytes 262144 | tf_op jit(solution)/shard_map/all_to_all | solution.py:177
  53.0 0.0 collective-permute-done.one_ref
  53.0 0.0 collective-permute-done.1.two_ref
  53.0 1.0 shard_map.86
  54.0 5.1 %all-to-all-start.1 = ((bf16[64,16,128]{2,1,0:T(8,128)(2,1)}), bf16[64,16,128]{2,1,0:T(8,128)(2,1)S(1)}, u32[]{:S(2)}, u32[]{:S(2)}) async-start(bf16[64,16,128]{2,1,0:T(8,128)(2,1)} %bitcast.4), calls=%async_computation.1 | async-start | bytes 524288 | tf_op jit(solution)/shard_map/all_to_all | solution.py:177
  59.2 0.1 collective-permute-start.2
  60.0 0.0 copy-start.4
  60.0 0.7 copy-done.4
  60.6 0.2 collective-permute-done.2.three_ref
  60.8 10.8 %all-to-all-done.1 = bf16[64,16,128]{2,1,0:T(8,128)(2,1)S(1)} async-done(((bf16[64,16,128]{2,1,0:T(8,128)(2,1)}), bf16[64,16,128]{2,1,0:T(8,128)(2,1)S(1)}, u32[]{:S(2)}, u32[]{:S(2)}) %all-to-all-start.1) | async-done | bytes 262176 | tf_op jit(solution)/shard_map/all_to_all | solution.py:177
  71.7 0.0 copy-done.1
  71.7 0.0 copy-done
  71.7 1.0 shard_map.87
  72.7 0.0 copy-start.2
  72.7 0.1 collective-permute-start.5
  72.8 1.5 %collective-permute-start.4 = (f32[32,256]{1,0:T(8,128)S(1)}, f32[32,256]{1,0:T(8,128)S(1)}, u32[]{:S(2)}, u32[]{:S(2)}) collective-permute-start(f32[32,256]{1,0:T(8,128)S(1)} %get-tuple-element.25.own_ref), channel_id=1, source_target_pairs={{0,2},{1,3},{2,0},{3,1},{4,6},{5,7},{6,4},{7,5},{8,10},{9,11},{10,... | collective-permute-start | bytes 98312 | tf_op jit(solution)/shard_map/ppermute | solution.py:181
  74.3 1.9 %collective-permute-start.3 = (f32[32,256]{1,0:T(8,128)S(1)}, f32[32,256]{1,0:T(8,128)S(1)}, u32[]{:S(2)}, u32[]{:S(2)}) collective-permute-start(f32[32,256]{1,0:T(8,128)S(1)} %get-tuple-element.25.own_ref), channel_id=1, source_target_pairs={{0,1},{1,0},{2,3},{3,2},{4,5},{5,4},{6,7},{7,6},{8,9},{9,8},{10,11... | collective-permute-start | bytes 98312 | tf_op jit(solution)/shard_map/ppermute | solution.py:181
  76.2 1.5 %collective-permute-done.5.three_ref = f32[32,256]{1,0:T(8,128)S(1)} collective-permute-done((f32[32,256]{1,0:T(8,128)S(1)}, f32[32,256]{1,0:T(8,128)S(1)}, u32[]{:S(2)}, u32[]{:S(2)}) %collective-permute-start.5) | collective-permute-done | bytes 32800 | tf_op jit(solution)/shard_map/ppermute | solution.py:181
  77.6 0.7 collective-permute-done.4.two_ref
  78.3 0.0 collective-permute-done.3.one_ref
  78.3 0.4 shard_map.88
  78.8 18.8 %all_to_all.21 = bf16[64,16,128]{2,1,0:T(8,128)(2,1)S(1)} all-to-all(bf16[64,16,128]{2,1,0:T(8,128)(2,1)S(1)} %bitcast.19), channel_id=1, replica_groups=mesh['dp'=64,'tensor'=4] {'dp'}, dimensions={0} | all-to-all | bytes 524288 | tf_op jit(solution)/shard_map/all_to_all | solution.py:177
  97.6 1.0 shard_map.90
  98.6 4.9 %all-to-all-start.3 = ((f32[64,4,128]{2,1,0:T(4,128)}), f32[64,4,128]{2,1,0:T(4,128)S(1)}, u32[]{:S(2)}, u32[]{:S(2)}) async-start(f32[64,4,128]{2,1,0:T(4,128)} %bitcast.10), calls=%async_computation.3 | async-start | bytes 262144 | tf_op jit(solution)/shard_map/all_to_all | solution.py:177
  103.6 1.4 %shard_map.89 = bf16[256,2048]{1,0:T(8,128)(2,1)} custom-call(bf16[32,256]{1,0:T(8,128)(2,1)S(1)} %get-tuple-element.28.ranks_ref, bf16[64,2048]{1,0:T(8,128)(2,1)S(1)} %copy-done.3), custom_call_target="tpu_custom_call" | custom-call | flops 33554432 | bytes 2097152 | tf_op jit(solution)/shard_map/pallas_call | solution.py:230
  105.0 9.2 %all-to-all-done.3 = f32[64,4,128]{2,1,0:T(4,128)S(1)} async-done(((f32[64,4,128]{2,1,0:T(4,128)}), f32[64,4,128]{2,1,0:T(4,128)S(1)}, u32[]{:S(2)}, u32[]{:S(2)}) %all-to-all-start.3) | async-done | bytes 131104 | tf_op jit(solution)/shard_map/all_to_all | solution.py:177
  114.1 0.7 shard_map.91
  (5 shorter events, 0.0 us)
Async XLA Ops:
  0.6 71.0 %copy-start.1 = (bf16[256,2048]{1,0:T(8,128)(2,1)S(1)}, bf16[256,2048]{1,0:T(8,128)(2,1)}, u32[]{:S(2)}) copy-start(bf16[256,2048]{1,0:T(8,128)(2,1)} %attn_ref.3) | copy-start | bytes 3145732
  26.3 45.4 %copy-start = (bf16[64,8192]{1,0:T(8,128)(2,1)S(1)}, bf16[64,8192]{1,0:T(8,128)(2,1)}, u32[]{:S(2)}) copy-start(bf16[64,8192]{1,0:T(8,128)(2,1)} %tokens_hbm.1) | copy-start | bytes 3145732
  26.3 26.7 %collective-permute-start.1 = (bf16[128,2048]{1,0:T(8,128)(2,1)}, bf16[128,2048]{1,0:T(8,128)(2,1)S(1)}, u32[]{:S(2)}, u32[]{:S(2)}) collective-permute-start(bf16[128,2048]{1,0:T(8,128)(2,1)} %get-tuple-element.20), channel_id=1, source_target_pairs={{0,2},{1,3},{2,0},{3,1},{4,6},{5,7},{6,4},{7,5},{8,10},{9,11},{10,... | collective-permute-start | bytes 1572872 | tf_op jit(solution)/shard_map/ppermute | solution.py:181
  28.5 24.5 %collective-permute-start = (bf16[64,2048]{1,0:T(8,128)(2,1)}, bf16[64,2048]{1,0:T(8,128)(2,1)S(1)}, u32[]{:S(2)}, u32[]{:S(2)}) collective-permute-start(bf16[64,2048]{1,0:T(8,128)(2,1)} %get-tuple-element.19), channel_id=1, source_target_pairs={{0,1},{1,0},{2,3},{3,2},{4,5},{5,4},{6,7},{7,6},{8,9},{9,8},{10,11... | collective-permute-start | bytes 786440 | tf_op jit(solution)/shard_map/ppermute | solution.py:181
  54.0 17.6 %all-to-all-start.1 = ((bf16[64,16,128]{2,1,0:T(8,128)(2,1)}), bf16[64,16,128]{2,1,0:T(8,128)(2,1)S(1)}, u32[]{:S(2)}, u32[]{:S(2)}) async-start(bf16[64,16,128]{2,1,0:T(8,128)(2,1)} %bitcast.4), calls=%async_computation.1 | async-start | bytes 524288 | tf_op jit(solution)/shard_map/all_to_all | solution.py:177
  59.2 1.6 %collective-permute-start.2 = (bf16[64,2048]{1,0:T(8,128)(2,1)S(1)}, bf16[64,2048]{1,0:T(8,128)(2,1)S(1)}, u32[]{:S(2)}, u32[]{:S(2)}) collective-permute-start(bf16[64,2048]{1,0:T(8,128)(2,1)S(1)} %slice.3), channel_id=1, source_target_pairs={{0,1},{1,0},{2,3},{3,2},{4,5},{5,4},{6,7},{7,6},{8,9},{9,8},{10,11... | collective-permute-start | bytes 786440 | tf_op jit(solution)/shard_map/ppermute | solution.py:181
  60.0 0.7 copy-start.4
  72.7 6.1 %copy-start.2 = (bf16[64,2048]{1,0:T(8,128)(2,1)}, bf16[64,2048]{1,0:T(8,128)(2,1)S(1)}, u32[]{:S(2)}) copy-start(bf16[64,2048]{1,0:T(8,128)(2,1)S(1)} %get-tuple-element.29.maps_ref) | copy-start | bytes 786436
  72.7 4.9 %collective-permute-start.5 = (f32[32,256]{1,0:T(8,128)S(1)}, f32[32,256]{1,0:T(8,128)S(1)}, u32[]{:S(2)}, u32[]{:S(2)}) collective-permute-start(f32[32,256]{1,0:T(8,128)S(1)} %get-tuple-element.25.own_ref), channel_id=1, source_target_pairs={{0,3},{1,2},{2,1},{3,0},{4,7},{5,6},{6,5},{7,4},{8,11},{9,10},{10,... | collective-permute-start | bytes 98312 | tf_op jit(solution)/shard_map/ppermute | solution.py:181
  72.8 5.5 %collective-permute-start.4 = (f32[32,256]{1,0:T(8,128)S(1)}, f32[32,256]{1,0:T(8,128)S(1)}, u32[]{:S(2)}, u32[]{:S(2)}) collective-permute-start(f32[32,256]{1,0:T(8,128)S(1)} %get-tuple-element.25.own_ref), channel_id=1, source_target_pairs={{0,2},{1,3},{2,0},{3,1},{4,6},{5,7},{6,4},{7,5},{8,10},{9,11},{10,... | collective-permute-start | bytes 98312 | tf_op jit(solution)/shard_map/ppermute | solution.py:181
  74.3 4.0 %collective-permute-start.3 = (f32[32,256]{1,0:T(8,128)S(1)}, f32[32,256]{1,0:T(8,128)S(1)}, u32[]{:S(2)}, u32[]{:S(2)}) collective-permute-start(f32[32,256]{1,0:T(8,128)S(1)} %get-tuple-element.25.own_ref), channel_id=1, source_target_pairs={{0,1},{1,0},{2,3},{3,2},{4,5},{5,4},{6,7},{7,6},{8,9},{9,8},{10,11... | collective-permute-start | bytes 98312 | tf_op jit(solution)/shard_map/ppermute | solution.py:181
  98.6 4.9 %copy-start.3 = (bf16[64,2048]{1,0:T(8,128)(2,1)S(1)}, bf16[64,2048]{1,0:T(8,128)(2,1)}, u32[]{:S(2)}) copy-start(bf16[64,2048]{1,0:T(8,128)(2,1)} %copy-done.2) | copy-start | bytes 786436
  98.6 15.5 %all-to-all-start.3 = ((f32[64,4,128]{2,1,0:T(4,128)}), f32[64,4,128]{2,1,0:T(4,128)S(1)}, u32[]{:S(2)}, u32[]{:S(2)}) async-start(f32[64,4,128]{2,1,0:T(4,128)} %bitcast.10), calls=%async_computation.3 | async-start | bytes 262144 | tf_op jit(solution)/shard_map/all_to_all | solution.py:177

commit v8 on v6

--- a/solution.py
+++ b/solution.py
@@ -28,13 +28,15 @@
 
 def pack_tables(
     place_ref, down_hbm, up_hbm, label_hbm, grad_hbm,
-    out_ref, near_ref, far_ref, down_ref, up_ref, label_ref, rows_f, out_f, sems
+    out_ref, near_hbm, far_hbm, down_ref, up_ref, label_ref, rows_f, out_f, cut_ref, sems
 ):
-    width = near_ref.shape[1]
+    width = down_ref.shape[1]
     moves = [(label_hbm, label_ref), (down_hbm, down_ref), (up_hbm, up_ref)]
-    for k, piece in ((1, near_ref), (2, far_ref.at[pl.ds(0, 64), :]), (3, far_ref.at[pl.ds(64, 64), :])):
-        first = pl.multiple_of(lax.bitwise_xor(place_ref[0], k) * width, width)
-        moves.append((grad_hbm.at[:, pl.ds(first, width)], piece))
+    slots = [cut_ref.at[pl.ds(n * 64, 64), :] for n in range(3)]
+    for n in range(3):
+        first = pl.multiple_of(lax.bitwise_xor(place_ref[0], (2, 3, 1)[n]) * width, width)
+        moves.append((grad_hbm.at[:, pl.ds(first, width)], slots[n]))
+    ends = (far_hbm.at[pl.ds(0, 64), :], far_hbm.at[pl.ds(64, 64), :], near_hbm)
     copies = [pltpu.make_async_copy(src, dst, sems.at[n]) for n, (src, dst) in enumerate(moves)]
     for copy in copies:
         copy.start()
@@ -51,9 +53,13 @@
             rows_f[c * 8:(c + 1) * 8, :] = map_ref[:, c * LANES:(c + 1) * LANES].astype(F32)
         for i in range(2):
             out_f[rows_of(2 * m + i, PEERS, 8), :] = rows_f[rows_of(i, PEERS, 2), :]
+    backs = [pltpu.make_async_copy(slots[n], ends[n], sems.at[6 + n]) for n in range(3)]
+    for copy, back in zip(copies[3:], backs):
+        copy.wait()
+        back.start()
     out_ref[...] = out_f[...].astype(BF16)
-    for copy in copies[3:]:
-        copy.wait()
+    for back in backs:
+        back.wait()
 
 
 def pick_rows(in_ref, out_ref, in_f, out_f):
@@ -70,12 +76,11 @@
     out_ref[...] = out_f[...].astype(BF16)
 
 
-def project(place_ref, picked_ref, attn_ref, tokens_hbm, one_ref, two_ref, three_ref, maps_ref, grad_ref, part_ref, sem):
+def project(place_ref, picked_ref, attn_ref, tokens_ref, one_ref, two_ref, three_ref, maps_ref, grad_ref, part_ref):
     me = place_ref[0]
     width = grad_ref.shape[1]
-    own = tokens_hbm.at[:, pl.ds(pl.multiple_of(me * width, width), width)]
-    copy = pltpu.make_async_copy(own, grad_ref.at[pl.ds(pl.multiple_of(me * 64, 64), 64), :], sem)
-    copy.start()
+    own = tokens_ref[:, pl.ds(pl.multiple_of(me * width, width), width)]
+    grad_ref[pl.ds(pl.multiple_of(me * 64, 64), 64), :] = own
     for k, piece in ((1, one_ref), (2, two_ref), (3, three_ref)):
         first = pl.multiple_of(lax.bitwise_xor(me, k) * 64, 64)
         grad_ref[pl.ds(first, 64), :] = piece[:64, :]
@@ -83,7 +88,6 @@
         rows = picked_ref[c * 64:(c + 1) * 64, :].astype(F32).reshape(QUARTERS, 2, 8, LANES)
         for b in range(2):
             maps_ref[b * 32:(b + 1) * 32, c * LANES:(c + 1) * LANES] = rows[:, b].reshape(32, LANES).astype(BF16)
-    copy.wait()
     row = lax.broadcasted_iota(jnp.int32, (32, BLOCK), 0)
     over_last = (((1,), (1,)), ((), ()))
     for b in range(2):
@@ -152,12 +156,12 @@
             map_ref[:, c * LANES:(c + 1) * LANES] = rows_f[c * 8:(c + 1) * 8, :]
 
 
-def call(kernel, outs, specs, scratch=(), cost=None, limit=40 * MIB):
+def call(kernel, outs, specs, scratch=(), cost=None, limit=40 * MIB, places=None):
     return pl.pallas_call(
         kernel,
         out_shape=[jax.ShapeDtypeStruct(shape, dtype) for shape, dtype in outs],
         in_specs=specs,
-        out_specs=[VMEM] * len(outs),
+        out_specs=places or [VMEM] * len(outs),
         scratch_shapes=scratch,
         compiler_params=pltpu.CompilerParams(vmem_limit_bytes=limit),
         cost_estimate=cost,
@@ -187,16 +191,19 @@
             pltpu.VMEM((2, BLOCK), jnp.int32),
             pltpu.VMEM((2 * PEERS, LANES), F32),
             pltpu.VMEM((8 * PEERS, LANES), F32),
-            pltpu.SemaphoreType.DMA((6,)),
+            pltpu.VMEM((192, width), BF16),
+            pltpu.SemaphoreType.DMA((9,)),
         ],
         limit=56 * MIB,
+        places=[VMEM, ANY, ANY],
     )(me, down_weight, up_weight, adapter_of_row.reshape(2, BLOCK), output_gradient)
     live = (adapter_of_row >= 0) & (jnp.arange(2 * BLOCK, dtype=jnp.int32) < lengths[0])
     live = live.astype(F32).reshape(2, BLOCK)
     near, far = from_peer(near, 1), from_peer(far, 2)
     tables = swap(packed)
     tables, near, far = lax.optimization_barrier((tables, near, far))
-    pieces = [near, far, from_peer(far[64:], 1)]
+    odd, live = lax.optimization_barrier((from_peer(far[64:], 1), live))
+    pieces = [near, far, odd]
     (picked,) = call(
         pick_rows,
         [((16 * PEERS, LANES), BF16)],
@@ -207,8 +214,7 @@
     maps, grad, part = call(
         project,
         [((64, width), BF16), ((2 * BLOCK, width), BF16), ((32, 2 * BLOCK), F32)],
-        [SMEM, VMEM, VMEM, ANY, VMEM, VMEM, VMEM],
-        [pltpu.SemaphoreType.DMA(())],
+        [SMEM] + [VMEM] * 6,
     )(me, picked, attn, output_gradient, *pieces)
     parts = [part] + [from_peer(part, k) for k in (1, 2, 3)]
     ranks, terms = call(
@@ -223,6 +229,7 @@
         [VMEM] * 2,
         cost=pl.CostEstimate(flops=2 * 32 * 256 * 2048, bytes_accessed=2 << 20, transcendentals=0),
     )(ranks, maps)
+    terms, attention_gradient = lax.optimization_barrier((terms, attention_gradient))
     (sums,) = call(
         add_up,
         [((4 * PEERS, LANES), F32)],

time: 92.5 us -> 92.8 us (level)
  blocking collectives: 43.2 us -> 39.9 us
  waiting for transfers between devices: 23.9 us -> 26.4 us
    all_to_all x2, waiting for transfers between devices: 20 us -> 24.1 us  [swap(): return lax.all_to_all(chunks, 'dp', 0, 0, tiled=True).reshape(x.shape)]
    all_to_all x2, blocking collectives: 43.2 us -> 39.9 us  [swap(): return lax.all_to_all(chunks, 'dp', 0, 0, tiled=True).reshape(x.shape)]
    ppermute x6, waiting for transfers between devices: 3.86 us -> 2.35 us  [from_peer(): return lax.ppermute(x, 'tensor', [(i, i ^ k) for i in range(4)])]
where the time goes in v8:
time: 92.8 us; the launch traced here: 92.4 us
  blocking collectives  39.9 us (43%)
  waiting for transfers between devices  26.4 us (28%)
  starting transfers between devices  15.9 us (17%)
  Pallas kernels  8.05 us (9%)
  between operations  1.41 us (2%)
    all_to_all x2, blocking collectives, swap(): return lax.all_to_all(chunks, 'dp', 0, 0, tiled=True).reshape(x.shape)  39.9 us
    all_to_all x2, waiting for transfers between devices, swap(): return lax.all_to_all(chunks, 'dp', 0, 0, tiled=True).reshape(x.shape)  24.1 us
    all_to_all x2, starting transfers between devices, swap(): return lax.all_to_all(chunks, 'dp', 0, 0, tiled=True).reshape(x.shape)  10.1 us
    ppermute x6, starting transfers between devices, from_peer(): return lax.ppermute(x, 'tensor', [(i, i ^ k) for i in range(4)])  5.75 us
    pallas_call x1, Pallas kernels, per_device(): call(pack_tables, [((8 * PEERS, LANES), BF16), ((64, width), BF16), ((128...  2.71 us
    ppermute x6, waiting for transfers between devices, from_peer(): return lax.ppermute(x, 'tensor', [(i, i ^ k) for i in range(4)])  2.35 us
  transfers between devices with their start and end apart: 8, of which 5 were waited for; matrix products, arithmetic and copies ran while one was open for 0% of the time, Pallas kernels for 2%

profile of v8, /device:TPU:2, one launch (start us, length us, event | category | flops | bytes accessed | tf_op | source)
XLA Modules:
  0.0 92.4 jit_solution(4601092675636381593)
XLA Ops:
  0.6 0.0 copy-start.1
  0.6 2.7 %shard_map.85 = (bf16[512,128]{1,0:T(8,128)(2,1)}, bf16[64,2048]{1,0:T(8,128)(2,1)}, bf16[128,2048]{1,0:T(8,128)(2,1)}) custom-call(s32[1]{0:T(128)} %bitcast.place_ref, bf16[8,2048]{1,0:T(8,128)(2,1)} %down_hbm.1, bf16[8,2048]{1,0:T(8,128)(2,1)} %up_hbm.1, s32[2,128]{1,0:T(2,128)} %bitcast.21, bf16[64,8192]{1,0:T(8,128)(2,1)} %tokens_ref.1), custom_call_target="tpu_custom_call" | custom-call | tf_op jit(solution)/shard_map/pallas_call | solution.py:184
  3.4 0.0 copy-start
  3.4 2.2 %collective-permute-start.1 = (bf16[128,2048]{1,0:T(8,128)(2,1)}, bf16[128,2048]{1,0:T(8,128)(2,1)S(1)}, u32[]{:S(2)}, u32[]{:S(2)}) collective-permute-start(bf16[128,2048]{1,0:T(8,128)(2,1)} %get-tuple-element.22), channel_id=1, source_target_pairs={{0,2},{1,3},{2,0},{3,1},{4,6},{5,7},{6,4},{7,5},{8,10},{9,11},{10,... | collective-permute-start | bytes 1572872 | tf_op jit(solution)/shard_map/ppermute | solution.py:177
  5.6 0.0 collective-permute-start
  5.6 24.5 %all_to_all.20 = bf16[64,8,128]{2,1,0:T(8,128)(2,1)S(1)} all-to-all(bf16[64,8,128]{2,1,0:T(8,128)(2,1)} %bitcast.20), channel_id=1, replica_groups=mesh['dp'=64,'tensor'=4] {'dp'}, dimensions={0} | all-to-all | bytes 262144 | tf_op jit(solution)/shard_map/all_to_all | solution.py:173
  30.1 0.0 collective-permute-done.one_ref
  30.1 0.0 collective-permute-done.1.two_ref
  30.1 1.0 %shard_map.86 = bf16[1024,128]{1,0:T(8,128)(2,1)} custom-call(bf16[512,128]{1,0:T(8,128)(2,1)S(1)} %bitcast.14), custom_call_target="tpu_custom_call" | custom-call | tf_op jit(solution)/shard_map/pallas_call | solution.py:207
  31.1 5.1 %all-to-all-start.1 = ((bf16[64,16,128]{2,1,0:T(8,128)(2,1)}), bf16[64,16,128]{2,1,0:T(8,128)(2,1)S(1)}, u32[]{:S(2)}, u32[]{:S(2)}) async-start(bf16[64,16,128]{2,1,0:T(8,128)(2,1)} %bitcast.4), calls=%async_computation.1 | async-start | bytes 524288 | tf_op jit(solution)/shard_map/all_to_all | solution.py:173
  36.3 0.1 collective-permute-start.2
  37.0 0.0 copy-start.4
  37.0 0.7 copy-done.4
  37.7 0.2 collective-permute-done.2.three_ref
  37.9 10.8 %all-to-all-done.1 = bf16[64,16,128]{2,1,0:T(8,128)(2,1)S(1)} async-done(((bf16[64,16,128]{2,1,0:T(8,128)(2,1)}), bf16[64,16,128]{2,1,0:T(8,128)(2,1)S(1)}, u32[]{:S(2)}, u32[]{:S(2)}) %all-to-all-start.1) | async-done | bytes 262176 | tf_op jit(solution)/shard_map/all_to_all | solution.py:173
  48.8 0.0 copy-done.1
  48.8 0.0 copy-done
  48.8 0.7 shard_map.87
  49.5 0.0 copy-start.2
  49.5 0.1 collective-permute-start.5
  49.6 1.5 %collective-permute-start.4 = (f32[32,256]{1,0:T(8,128)S(1)}, f32[32,256]{1,0:T(8,128)S(1)}, u32[]{:S(2)}, u32[]{:S(2)}) collective-permute-start(f32[32,256]{1,0:T(8,128)S(1)} %get-tuple-element.27.own_ref), channel_id=1, source_target_pairs={{0,2},{1,3},{2,0},{3,1},{4,6},{5,7},{6,4},{7,5},{8,10},{9,11},{10,... | collective-permute-start | bytes 98312 | tf_op jit(solution)/shard_map/ppermute | solution.py:177
  51.1 1.9 %collective-permute-start.3 = (f32[32,256]{1,0:T(8,128)S(1)}, f32[32,256]{1,0:T(8,128)S(1)}, u32[]{:S(2)}, u32[]{:S(2)}) collective-permute-start(f32[32,256]{1,0:T(8,128)S(1)} %get-tuple-element.27.own_ref), channel_id=1, source_target_pairs={{0,1},{1,0},{2,3},{3,2},{4,5},{5,4},{6,7},{7,6},{8,9},{9,8},{10,11... | collective-permute-start | bytes 98312 | tf_op jit(solution)/shard_map/ppermute | solution.py:177
  53.0 1.5 %collective-permute-done.5.three_ref = f32[32,256]{1,0:T(8,128)S(1)} collective-permute-done((f32[32,256]{1,0:T(8,128)S(1)}, f32[32,256]{1,0:T(8,128)S(1)}, u32[]{:S(2)}, u32[]{:S(2)}) %collective-permute-start.5) | collective-permute-done | bytes 32800 | tf_op jit(solution)/shard_map/ppermute | solution.py:177
  54.4 0.7 collective-permute-done.4.two_ref
  55.1 0.0 collective-permute-done.3.one_ref
  55.1 1.1 %shard_map.88 = (bf16[32,256]{1,0:T(8,128)(2,1)S(1)}, bf16[1024,128]{1,0:T(8,128)(2,1)}) custom-call(f32[32,256]{1,0:T(8,128)S(1)} %get-tuple-element.27.own_ref, f32[32,256]{1,0:T(8,128)S(1)} %collective-permute-done.3.one_ref, f32[32,256]{1,0:T(8,128)S(1)} %collective-permute-done.4.two_ref, f32[32,256]{1,0:T(8,128)S(1)} %collective-permute-done.5.three_ref, ...), custom_call_target="tpu_custom_call" | custom-call | tf_op jit(solution)/shard_map/pallas_call | solution.py:220
  56.3 5.0 %all-to-all-start.2 = ((bf16[64,16,128]{2,1,0:T(8,128)(2,1)}), bf16[64,16,128]{2,1,0:T(8,128)(2,1)S(1)}, u32[]{:S(2)}, u32[]{:S(2)}) async-start(bf16[64,16,128]{2,1,0:T(8,128)(2,1)} %bitcast.8), calls=%async_computation.2 | async-start | bytes 524288 | tf_op jit(solution)/shard_map/all_to_all | solution.py:173
  61.3 1.4 %shard_map.89 = bf16[256,2048]{1,0:T(8,128)(2,1)} custom-call(bf16[32,256]{1,0:T(8,128)(2,1)S(1)} %get-tuple-element.31.ranks_ref, bf16[64,2048]{1,0:T(8,128)(2,1)S(1)} %copy-done.3), custom_call_target="tpu_custom_call" | custom-call | flops 33554432 | bytes 2097152 | tf_op jit(solution)/shard_map/pallas_call | solution.py:226
  62.7 13.2 %all-to-all-done.2 = bf16[64,16,128]{2,1,0:T(8,128)(2,1)S(1)} async-done(((bf16[64,16,128]{2,1,0:T(8,128)(2,1)}), bf16[64,16,128]{2,1,0:T(8,128)(2,1)S(1)}, u32[]{:S(2)}, u32[]{:S(2)}) %all-to-all-start.2) | async-done | bytes 262176 | tf_op jit(solution)/shard_map/all_to_all | solution.py:173
  75.9 0.3 shard_map.90
  76.3 15.4 %all_to_all.21 = f32[64,4,128]{2,1,0:T(4,128)S(1)} all-to-all(f32[64,4,128]{2,1,0:T(4,128)S(1)} %bitcast.19), channel_id=1, replica_groups=mesh['dp'=64,'tensor'=4] {'dp'}, dimensions={0} | all-to-all | bytes 262144 | tf_op jit(solution)/shard_map/all_to_all | solution.py:173
  91.7 0.7 shard_map.91
  (5 shorter events, 0.0 us)
Async XLA Ops:
  0.6 48.1 %copy-start.1 = (bf16[256,2048]{1,0:T(8,128)(2,1)S(1)}, bf16[256,2048]{1,0:T(8,128)(2,1)}, u32[]{:S(2)}) copy-start(bf16[256,2048]{1,0:T(8,128)(2,1)} %attn_ref.3) | copy-start | bytes 3145732
  3.4 45.4 %copy-start = (bf16[64,8192]{1,0:T(8,128)(2,1)S(1)}, bf16[64,8192]{1,0:T(8,128)(2,1)}, u32[]{:S(2)}) copy-start(bf16[64,8192]{1,0:T(8,128)(2,1)} %tokens_ref.1) | copy-start | bytes 3145732
  3.4 26.7 %collective-permute-start.1 = (bf16[128,2048]{1,0:T(8,128)(2,1)}, bf16[128,2048]{1,0:T(8,128)(2,1)S(1)}, u32[]{:S(2)}, u32[]{:S(2)}) collective-permute-start(bf16[128,2048]{1,0:T(8,128)(2,1)} %get-tuple-element.22), channel_id=1, source_target_pairs={{0,2},{1,3},{2,0},{3,1},{4,6},{5,7},{6,4},{7,5},{8,10},{9,11},{10,... | collective-permute-start | bytes 1572872 | tf_op jit(solution)/shard_map/ppermute | solution.py:177
  5.6 24.5 %collective-permute-start = (bf16[64,2048]{1,0:T(8,128)(2,1)}, bf16[64,2048]{1,0:T(8,128)(2,1)S(1)}, u32[]{:S(2)}, u32[]{:S(2)}) collective-permute-start(bf16[64,2048]{1,0:T(8,128)(2,1)} %get-tuple-element.21), channel_id=1, source_target_pairs={{0,1},{1,0},{2,3},{3,2},{4,5},{5,4},{6,7},{7,6},{8,9},{9,8},{10,11... | collective-permute-start | bytes 786440 | tf_op jit(solution)/shard_map/ppermute | solution.py:177
  31.1 17.6 %all-to-all-start.1 = ((bf16[64,16,128]{2,1,0:T(8,128)(2,1)}), bf16[64,16,128]{2,1,0:T(8,128)(2,1)S(1)}, u32[]{:S(2)}, u32[]{:S(2)}) async-start(bf16[64,16,128]{2,1,0:T(8,128)(2,1)} %bitcast.4), calls=%async_computation.1 | async-start | bytes 524288 | tf_op jit(solution)/shard_map/all_to_all | solution.py:173
  36.3 1.6 %collective-permute-start.2 = (bf16[64,2048]{1,0:T(8,128)(2,1)S(1)}, bf16[64,2048]{1,0:T(8,128)(2,1)S(1)}, u32[]{:S(2)}, u32[]{:S(2)}) collective-permute-start(bf16[64,2048]{1,0:T(8,128)(2,1)S(1)} %slice.3), channel_id=1, source_target_pairs={{0,1},{1,0},{2,3},{3,2},{4,5},{5,4},{6,7},{7,6},{8,9},{9,8},{10,11... | collective-permute-start | bytes 786440 | tf_op jit(solution)/shard_map/ppermute | solution.py:177
  37.0 0.7 copy-start.4
  49.5 6.8 %copy-start.2 = (bf16[64,2048]{1,0:T(8,128)(2,1)}, bf16[64,2048]{1,0:T(8,128)(2,1)S(1)}, u32[]{:S(2)}) copy-start(bf16[64,2048]{1,0:T(8,128)(2,1)S(1)} %get-tuple-element.32.maps_ref) | copy-start | bytes 786436
  49.5 4.9 %collective-permute-start.5 = (f32[32,256]{1,0:T(8,128)S(1)}, f32[32,256]{1,0:T(8,128)S(1)}, u32[]{:S(2)}, u32[]{:S(2)}) collective-permute-start(f32[32,256]{1,0:T(8,128)S(1)} %get-tuple-element.27.own_ref), channel_id=1, source_target_pairs={{0,3},{1,2},{2,1},{3,0},{4,7},{5,6},{6,5},{7,4},{8,11},{9,10},{10,... | collective-permute-start | bytes 98312 | tf_op jit(solution)/shard_map/ppermute | solution.py:177
  49.6 5.5 %collective-permute-start.4 = (f32[32,256]{1,0:T(8,128)S(1)}, f32[32,256]{1,0:T(8,128)S(1)}, u32[]{:S(2)}, u32[]{:S(2)}) collective-permute-start(f32[32,256]{1,0:T(8,128)S(1)} %get-tuple-element.27.own_ref), channel_id=1, source_target_pairs={{0,2},{1,3},{2,0},{3,1},{4,6},{5,7},{6,4},{7,5},{8,10},{9,11},{10,... | collective-permute-start | bytes 98312 | tf_op jit(solution)/shard_map/ppermute | solution.py:177
  51.1 4.0 %collective-permute-start.3 = (f32[32,256]{1,0:T(8,128)S(1)}, f32[32,256]{1,0:T(8,128)S(1)}, u32[]{:S(2)}, u32[]{:S(2)}) collective-permute-start(f32[32,256]{1,0:T(8,128)S(1)} %get-tuple-element.27.own_ref), channel_id=1, source_target_pairs={{0,1},{1,0},{2,3},{3,2},{4,5},{5,4},{6,7},{7,6},{8,9},{9,8},{10,11... | collective-permute-start | bytes 98312 | tf_op jit(solution)/shard_map/ppermute | solution.py:177
  56.3 5.0 %copy-start.3 = (bf16[64,2048]{1,0:T(8,128)(2,1)S(1)}, bf16[64,2048]{1,0:T(8,128)(2,1)}, u32[]{:S(2)}) copy-start(bf16[64,2048]{1,0:T(8,128)(2,1)} %copy-done.2) | copy-start | bytes 786436
  56.3 19.7 %all-to-all-start.2 = ((bf16[64,16,128]{2,1,0:T(8,128)(2,1)}), bf16[64,16,128]{2,1,0:T(8,128)(2,1)S(1)}, u32[]{:S(2)}, u32[]{:S(2)}) async-start(bf16[64,16,128]{2,1,0:T(8,128)(2,1)} %bitcast.8), calls=%async_computation.2 | async-start | bytes 524288 | tf_op jit(solution)/shard_map/all_to_all | solution.py:173

commit v9 on v6

--- a/solution.py
+++ b/solution.py
@@ -26,15 +26,8 @@
     return pl.ds(first, size, stride=stride)
 
 
-def pack_tables(
-    place_ref, down_hbm, up_hbm, label_hbm, grad_hbm,
-    out_ref, near_ref, far_ref, down_ref, up_ref, label_ref, rows_f, out_f, sems
-):
-    width = near_ref.shape[1]
-    moves = [(label_hbm, label_ref), (down_hbm, down_ref), (up_hbm, up_ref)]
-    for k, piece in ((1, near_ref), (2, far_ref.at[pl.ds(0, 64), :]), (3, far_ref.at[pl.ds(64, 64), :])):
-        first = pl.multiple_of(lax.bitwise_xor(place_ref[0], k) * width, width)
-        moves.append((grad_hbm.at[:, pl.ds(first, width)], piece))
+def pack_tables(down_hbm, up_hbm, label_hbm, out_ref, down_ref, up_ref, label_ref, rows_f, out_f, sems):
+    moves = ((label_hbm, label_ref), (down_hbm, down_ref), (up_hbm, up_ref))
     copies = [pltpu.make_async_copy(src, dst, sems.at[n]) for n, (src, dst) in enumerate(moves)]
     for copy in copies:
         copy.start()
@@ -52,7 +45,17 @@
         for i in range(2):
             out_f[rows_of(2 * m + i, PEERS, 8), :] = rows_f[rows_of(i, PEERS, 2), :]
     out_ref[...] = out_f[...].astype(BF16)
-    for copy in copies[3:]:
+
+
+def cut_tokens(place_ref, grad_hbm, packed_hbm, near_ref, far_ref, sems):
+    width = near_ref.shape[1]
+    copies = []
+    for k, piece in ((2, far_ref.at[pl.ds(0, 64), :]), (3, far_ref.at[pl.ds(64, 64), :]), (1, near_ref)):
+        first = pl.multiple_of(lax.bitwise_xor(place_ref[0], k) * width, width)
+        copies.append(pltpu.make_async_copy(grad_hbm.at[:, pl.ds(first, width)], piece, sems.at[k - 1]))
+    for copy in copies:
+        copy.start()
+    for copy in copies:
         copy.wait()
 
 
@@ -70,12 +73,11 @@
     out_ref[...] = out_f[...].astype(BF16)
 
 
-def project(place_ref, picked_ref, attn_ref, tokens_hbm, one_ref, two_ref, three_ref, maps_ref, grad_ref, part_ref, sem):
+def project(place_ref, picked_ref, attn_ref, tokens_ref, one_ref, two_ref, three_ref, maps_ref, grad_ref, part_ref):
     me = place_ref[0]
     width = grad_ref.shape[1]
-    own = tokens_hbm.at[:, pl.ds(pl.multiple_of(me * width, width), width)]
-    copy = pltpu.make_async_copy(own, grad_ref.at[pl.ds(pl.multiple_of(me * 64, 64), 64), :], sem)
-    copy.start()
+    own = tokens_ref[:, pl.ds(pl.multiple_of(me * width, width), width)]
+    grad_ref[pl.ds(pl.multiple_of(me * 64, 64), 64), :] = own
     for k, piece in ((1, one_ref), (2, two_ref), (3, three_ref)):
         first = pl.multiple_of(lax.bitwise_xor(me, k) * 64, 64)
         grad_ref[pl.ds(first, 64), :] = piece[:64, :]
@@ -83,7 +85,6 @@
         rows = picked_ref[c * 64:(c + 1) * 64, :].astype(F32).reshape(QUARTERS, 2, 8, LANES)
         for b in range(2):
             maps_ref[b * 32:(b + 1) * 32, c * LANES:(c + 1) * LANES] = rows[:, b].reshape(32, LANES).astype(BF16)
-    copy.wait()
     row = lax.broadcasted_iota(jnp.int32, (32, BLOCK), 0)
     over_last = (((1,), (1,)), ((), ()))
     for b in range(2):
@@ -177,26 +178,34 @@
     width = attn.shape[1]
     me = lax.axis_index("tensor")
     me = me.astype(jnp.int32).reshape(1)
-    packed, near, far = call(
+    (packed,) = call(
         pack_tables,
-        [((8 * PEERS, LANES), BF16), ((64, width), BF16), ((128, width), BF16)],
-        [SMEM] + [ANY] * 4,
+        [((8 * PEERS, LANES), BF16)],
+        [ANY] * 3,
         [
             pltpu.VMEM((8, width), BF16),
             pltpu.VMEM((8, width), BF16),
             pltpu.VMEM((2, BLOCK), jnp.int32),
             pltpu.VMEM((2 * PEERS, LANES), F32),
             pltpu.VMEM((8 * PEERS, LANES), F32),
-            pltpu.SemaphoreType.DMA((6,)),
+            pltpu.SemaphoreType.DMA((3,)),
         ],
         limit=56 * MIB,
-    )(me, down_weight, up_weight, adapter_of_row.reshape(2, BLOCK), output_gradient)
+    )(down_weight, up_weight, adapter_of_row.reshape(2, BLOCK))
+    near, far = call(
+        cut_tokens,
+        [((64, width), BF16), ((128, width), BF16)],
+        [SMEM, ANY, ANY],
+        [pltpu.SemaphoreType.DMA((3,))],
+        limit=56 * MIB,
+    )(me, output_gradient, packed)
     live = (adapter_of_row >= 0) & (jnp.arange(2 * BLOCK, dtype=jnp.int32) < lengths[0])
     live = live.astype(F32).reshape(2, BLOCK)
-    near, far = from_peer(near, 1), from_peer(far, 2)
     tables = swap(packed)
     tables, near, far = lax.optimization_barrier((tables, near, far))
-    pieces = [near, far, from_peer(far[64:], 1)]
+    near, far = from_peer(near, 1), from_peer(far, 2)
+    odd, live = lax.optimization_barrier((from_peer(far[64:], 1), live))
+    pieces = [near, far, odd]
     (picked,) = call(
         pick_rows,
         [((16 * PEERS, LANES), BF16)],
@@ -207,8 +216,7 @@
     maps, grad, part = call(
         project,
         [((64, width), BF16), ((2 * BLOCK, width), BF16), ((32, 2 * BLOCK), F32)],
-        [SMEM, VMEM, VMEM, ANY, VMEM, VMEM, VMEM],
-        [pltpu.SemaphoreType.DMA(())],
+        [SMEM] + [VMEM] * 6,
     )(me, picked, attn, output_gradient, *pieces)
     parts = [part] + [from_peer(part, k) for k in (1, 2, 3)]
     ranks, terms = call(

time: 92.5 us -> 89.8 us (0.971)
  blocking collectives: 43.2 us -> 18.4 us
  starting transfers between devices: 15.9 us -> 30.1 us
  waiting for transfers between devices: 23.9 us -> 29.7 us
  Pallas kernels: 7.76 us -> 8.93 us
    all_to_all x2 -> x1, blocking collectives: 43.2 us -> 18.4 us  [swap(): return lax.all_to_all(chunks, 'dp', 0, 0, tiled=True).reshape(x.shape)]
    all_to_all x2 -> x3, starting transfers between devices: 10.1 us -> 24 us  [swap(): return lax.all_to_all(chunks, 'dp', 0, 0, tiled=True).reshape(x.shape)]
    ppermute x6, waiting for transfers between devices: 3.86 us -> 10 us  [from_peer(): return lax.ppermute(x, 'tensor', [(i, i ^ k) for i in range(4)])]
    pallas_call x1 -> x2, Pallas kernels: 2.24 us -> 3.68 us  [the longest x1 2.16 us: per_device(): call(cut_tokens, [((64, width), BF16), ((128, width), BF16)], [SMEM, ANY,...]
    all_to_all x2 -> x3, waiting for transfers between devices: 20 us -> 19.7 us  [swap(): return lax.all_to_all(chunks, 'dp', 0, 0, tiled=True).reshape(x.shape)]
  transfers between devices with their start and end apart: 8 -> 9, of which waited for: 5 -> 7; matrix products, arithmetic and copies ran while one was open for 0% -> 0% of each run, Pallas kernels for 2% -> 5%
where the time goes in v9:
time: 89.8 us; the launch traced here: 89.3 us
  starting transfers between devices  30.1 us (34%)
  waiting for transfers between devices  29.7 us (33%)
  blocking collectives  18.4 us (20%)
  Pallas kernels  8.93 us (10%)
  between operations  1.45 us (2%)
    all_to_all x3, starting transfers between devices, swap(): return lax.all_to_all(chunks, 'dp', 0, 0, tiled=True).reshape(x.shape)  24 us
    all_to_all x3, waiting for transfers between devices, swap(): return lax.all_to_all(chunks, 'dp', 0, 0, tiled=True).reshape(x.shape)  19.7 us
    all_to_all x1, blocking collectives, swap(): return lax.all_to_all(chunks, 'dp', 0, 0, tiled=True).reshape(x.shape)  18.4 us
    ppermute x6, waiting for transfers between devices, from_peer(): return lax.ppermute(x, 'tensor', [(i, i ^ k) for i in range(4)])  10 us
    ppermute x6, starting transfers between devices, from_peer(): return lax.ppermute(x, 'tensor', [(i, i ^ k) for i in range(4)])  6.15 us
    pallas_call x1, Pallas kernels, per_device(): call(cut_tokens, [((64, width), BF16), ((128, width), BF16)], [SMEM, ANY,...  2.16 us
  transfers between devices with their start and end apart: 9, of which 7 were waited for; matrix products, arithmetic and copies ran while one was open for 0% of the time, Pallas kernels for 5%

profile of v9, /device:TPU:2, one launch (start us, length us, event | category | flops | bytes accessed | tf_op | source)
XLA Modules:
  0.0 89.3 jit_solution(14732950549557993754)
XLA Ops:
  0.6 1.5 %shard_map.85.packed_hbm = bf16[512,128]{1,0:T(8,128)(2,1)} custom-call(bf16[8,2048]{1,0:T(8,128)(2,1)} %down_hbm.1, bf16[8,2048]{1,0:T(8,128)(2,1)} %up_hbm.1, s32[2,128]{1,0:T(2,128)} %bitcast.21), custom_call_target="tpu_custom_call" | custom-call | tf_op jit(solution)/shard_map/pallas_call | solution.py:181
  2.2 13.2 %all-to-all-start = ((bf16[64,8,128]{2,1,0:T(8,128)(2,1)}), bf16[64,8,128]{2,1,0:T(8,128)(2,1)S(1)}, u32[]{:S(2)}, u32[]{:S(2)}) async-start(bf16[64,8,128]{2,1,0:T(8,128)(2,1)} %bitcast.20), calls=%async_computation | async-start | bytes 262144 | tf_op jit(solution)/shard_map/all_to_all | solution.py:170
  15.4 0.0 copy-start
  15.4 0.0 copy-start.1
  15.4 2.2 %shard_map.86 = (bf16[64,2048]{1,0:T(8,128)(2,1)}, bf16[128,2048]{1,0:T(8,128)(2,1)}) custom-call(s32[1]{0:T(128)} %bitcast.place_ref, bf16[64,8192]{1,0:T(8,128)(2,1)} %tokens_ref.1, bf16[512,128]{1,0:T(8,128)(2,1)} %shard_map.85.packed_hbm), custom_call_target="tpu_custom_call" | custom-call | tf_op jit(solution)/shard_map/pallas_call | solution.py:195
  17.6 8.4 %all-to-all-done = bf16[64,8,128]{2,1,0:T(8,128)(2,1)S(1)} async-done(((bf16[64,8,128]{2,1,0:T(8,128)(2,1)}), bf16[64,8,128]{2,1,0:T(8,128)(2,1)S(1)}, u32[]{:S(2)}, u32[]{:S(2)}) %all-to-all-start) | async-done | bytes 131104 | tf_op jit(solution)/shard_map/all_to_all | solution.py:170
  26.0 2.1 %collective-permute-start.1 = (bf16[128,2048]{1,0:T(8,128)(2,1)}, bf16[128,2048]{1,0:T(8,128)(2,1)S(1)}, u32[]{:S(2)}, u32[]{:S(2)}) collective-permute-start(bf16[128,2048]{1,0:T(8,128)(2,1)} %get-tuple-element.21), channel_id=1, source_target_pairs={{0,2},{1,3},{2,0},{3,1},{4,6},{5,7},{6,4},{7,5},{8,10},{9,11},{10,... | collective-permute-start | bytes 1572872 | tf_op jit(solution)/shard_map/ppermute | solution.py:174
  28.1 1.0 %shard_map.87 = bf16[1024,128]{1,0:T(8,128)(2,1)} custom-call(bf16[512,128]{1,0:T(8,128)(2,1)S(1)} %bitcast.14), custom_call_target="tpu_custom_call" | custom-call | tf_op jit(solution)/shard_map/pallas_call | solution.py:209
  29.1 5.8 %all-to-all-start.1 = ((bf16[64,16,128]{2,1,0:T(8,128)(2,1)}), bf16[64,16,128]{2,1,0:T(8,128)(2,1)S(1)}, u32[]{:S(2)}, u32[]{:S(2)}) async-start(bf16[64,16,128]{2,1,0:T(8,128)(2,1)} %bitcast.4), calls=%async_computation.1 | async-start | bytes 524288 | tf_op jit(solution)/shard_map/all_to_all | solution.py:170
  34.9 7.8 %collective-permute-done.1.two_ref = bf16[128,2048]{1,0:T(8,128)(2,1)S(1)} collective-permute-done((bf16[128,2048]{1,0:T(8,128)(2,1)}, bf16[128,2048]{1,0:T(8,128)(2,1)S(1)}, u32[]{:S(2)}, u32[]{:S(2)}) %collective-permute-start.1) | collective-permute-done | bytes 524320 | tf_op jit(solution)/shard_map/ppermute | solution.py:174
  42.7 0.1 collective-permute-start.2
  42.8 0.5 collective-permute-start
  44.0 0.0 copy-start.4
  44.0 0.7 copy-done.4
  44.6 0.0 collective-permute-done.2.three_ref
  44.7 0.1 collective-permute-done.one_ref
  44.7 2.1 %all-to-all-done.1 = bf16[64,16,128]{2,1,0:T(8,128)(2,1)S(1)} async-done(((bf16[64,16,128]{2,1,0:T(8,128)(2,1)}), bf16[64,16,128]{2,1,0:T(8,128)(2,1)S(1)}, u32[]{:S(2)}, u32[]{:S(2)}) %all-to-all-start.1) | async-done | bytes 262176 | tf_op jit(solution)/shard_map/all_to_all | solution.py:170
  46.8 0.7 shard_map.88
  47.6 0.0 copy-start.2
  47.6 0.1 collective-permute-start.5
  47.7 1.2 %collective-permute-start.4 = (f32[32,256]{1,0:T(8,128)S(1)}, f32[32,256]{1,0:T(8,128)S(1)}, u32[]{:S(2)}, u32[]{:S(2)}) collective-permute-start(f32[32,256]{1,0:T(8,128)S(1)} %get-tuple-element.23.own_ref), channel_id=1, source_target_pairs={{0,2},{1,3},{2,0},{3,1},{4,6},{5,7},{6,4},{7,5},{8,10},{9,11},{10,... | collective-permute-start | bytes 98312 | tf_op jit(solution)/shard_map/ppermute | solution.py:174
  48.8 2.2 %collective-permute-start.3 = (f32[32,256]{1,0:T(8,128)S(1)}, f32[32,256]{1,0:T(8,128)S(1)}, u32[]{:S(2)}, u32[]{:S(2)}) collective-permute-start(f32[32,256]{1,0:T(8,128)S(1)} %get-tuple-element.23.own_ref), channel_id=1, source_target_pairs={{0,1},{1,0},{2,3},{3,2},{4,5},{5,4},{6,7},{7,6},{8,9},{9,8},{10,11... | collective-permute-start | bytes 98312 | tf_op jit(solution)/shard_map/ppermute | solution.py:174
  51.0 1.5 %collective-permute-done.5.three_ref = f32[32,256]{1,0:T(8,128)S(1)} collective-permute-done((f32[32,256]{1,0:T(8,128)S(1)}, f32[32,256]{1,0:T(8,128)S(1)}, u32[]{:S(2)}, u32[]{:S(2)}) %collective-permute-start.5) | collective-permute-done | bytes 32800 | tf_op jit(solution)/shard_map/ppermute | solution.py:174
  52.5 0.7 collective-permute-done.4.two_ref
  53.2 0.0 collective-permute-done.3.one_ref
  53.2 0.4 shard_map.89
  53.6 18.4 %all_to_all.20 = bf16[64,16,128]{2,1,0:T(8,128)(2,1)S(1)} all-to-all(bf16[64,16,128]{2,1,0:T(8,128)(2,1)S(1)} %bitcast.19), channel_id=1, replica_groups=mesh['dp'=64,'tensor'=4] {'dp'}, dimensions={0} | all-to-all | bytes 524288 | tf_op jit(solution)/shard_map/all_to_all | solution.py:170
  72.1 1.0 %shard_map.91 = f32[256,128]{1,0:T(8,128)} custom-call(bf16[1024,128]{1,0:T(8,128)(2,1)S(1)} %bitcast.17, bf16[512,128]{1,0:T(8,128)(2,1)S(1)} %bitcast.15), custom_call_target="tpu_custom_call" | custom-call | tf_op jit(solution)/shard_map/pallas_call | solution.py:234
  73.0 5.0 %all-to-all-start.3 = ((f32[64,4,128]{2,1,0:T(4,128)}), f32[64,4,128]{2,1,0:T(4,128)S(1)}, u32[]{:S(2)}, u32[]{:S(2)}) async-start(f32[64,4,128]{2,1,0:T(4,128)} %bitcast.10), calls=%async_computation.3 | async-start | bytes 262144 | tf_op jit(solution)/shard_map/all_to_all | solution.py:170
  78.1 1.4 %shard_map.90 = bf16[256,2048]{1,0:T(8,128)(2,1)} custom-call(bf16[32,256]{1,0:T(8,128)(2,1)S(1)} %get-tuple-element.26.ranks_ref, bf16[64,2048]{1,0:T(8,128)(2,1)S(1)} %copy-done.3), custom_call_target="tpu_custom_call" | custom-call | flops 33554432 | bytes 2097152 | tf_op jit(solution)/shard_map/pallas_call | solution.py:228
  79.5 9.2 %all-to-all-done.3 = f32[64,4,128]{2,1,0:T(4,128)S(1)} async-done(((f32[64,4,128]{2,1,0:T(4,128)}), f32[64,4,128]{2,1,0:T(4,128)S(1)}, u32[]{:S(2)}, u32[]{:S(2)}) %all-to-all-start.3) | async-done | bytes 131104 | tf_op jit(solution)/shard_map/all_to_all | solution.py:170
  88.7 0.7 shard_map.92
  (9 shorter events, 0.0 us)
Async XLA Ops:
  2.2 23.8 %all-to-all-start = ((bf16[64,8,128]{2,1,0:T(8,128)(2,1)}), bf16[64,8,128]{2,1,0:T(8,128)(2,1)S(1)}, u32[]{:S(2)}, u32[]{:S(2)}) async-start(bf16[64,8,128]{2,1,0:T(8,128)(2,1)} %bitcast.20), calls=%async_computation | async-start | bytes 262144 | tf_op jit(solution)/shard_map/all_to_all | solution.py:170
  15.4 31.4 %copy-start = (bf16[64,8192]{1,0:T(8,128)(2,1)S(1)}, bf16[64,8192]{1,0:T(8,128)(2,1)}, u32[]{:S(2)}) copy-start(bf16[64,8192]{1,0:T(8,128)(2,1)} %tokens_ref.1) | copy-start | bytes 3145732
  15.4 31.4 %copy-start.1 = (bf16[256,2048]{1,0:T(8,128)(2,1)S(1)}, bf16[256,2048]{1,0:T(8,128)(2,1)}, u32[]{:S(2)}) copy-start(bf16[256,2048]{1,0:T(8,128)(2,1)} %attn_ref.3) | copy-start | bytes 3145732
  26.0 16.7 %collective-permute-start.1 = (bf16[128,2048]{1,0:T(8,128)(2,1)}, bf16[128,2048]{1,0:T(8,128)(2,1)S(1)}, u32[]{:S(2)}, u32[]{:S(2)}) collective-permute-start(bf16[128,2048]{1,0:T(8,128)(2,1)} %get-tuple-element.21), channel_id=1, source_target_pairs={{0,2},{1,3},{2,0},{3,1},{4,6},{5,7},{6,4},{7,5},{8,10},{9,11},{10,... | collective-permute-start | bytes 1572872 | tf_op jit(solution)/shard_map/ppermute | solution.py:174
  29.1 17.7 %all-to-all-start.1 = ((bf16[64,16,128]{2,1,0:T(8,128)(2,1)}), bf16[64,16,128]{2,1,0:T(8,128)(2,1)S(1)}, u32[]{:S(2)}, u32[]{:S(2)}) async-start(bf16[64,16,128]{2,1,0:T(8,128)(2,1)} %bitcast.4), calls=%async_computation.1 | async-start | bytes 524288 | tf_op jit(solution)/shard_map/all_to_all | solution.py:170
  34.9 7.9 %copy-start.5 = (bf16[64,2048]{1,0:T(8,128)(2,1)S(1)}, bf16[64,2048]{1,0:T(8,128)(2,1)}, u32[]{:S(2)}) copy-start(bf16[64,2048]{1,0:T(8,128)(2,1)} %get-tuple-element.20) | copy-start | bytes 786436
  42.7 1.9 %collective-permute-start.2 = (bf16[64,2048]{1,0:T(8,128)(2,1)S(1)}, bf16[64,2048]{1,0:T(8,128)(2,1)S(1)}, u32[]{:S(2)}, u32[]{:S(2)}) collective-permute-start(bf16[64,2048]{1,0:T(8,128)(2,1)S(1)} %slice.4), channel_id=1, source_target_pairs={{0,1},{1,0},{2,3},{3,2},{4,5},{5,4},{6,7},{7,6},{8,9},{9,8},{10,11... | collective-permute-start | bytes 786440 | tf_op jit(solution)/shard_map/ppermute | solution.py:174
  42.8 1.9 %collective-permute-start = (bf16[64,2048]{1,0:T(8,128)(2,1)S(1)}, bf16[64,2048]{1,0:T(8,128)(2,1)S(1)}, u32[]{:S(2)}, u32[]{:S(2)}) collective-permute-start(bf16[64,2048]{1,0:T(8,128)(2,1)S(1)} %copy-done.5), channel_id=1, source_target_pairs={{0,1},{1,0},{2,3},{3,2},{4,5},{5,4},{6,7},{7,6},{8,9},{9,8},{10,11... | collective-permute-start | bytes 786440 | tf_op jit(solution)/shard_map/ppermute | solution.py:174
  44.0 0.7 copy-start.4
  47.6 6.1 %copy-start.2 = (bf16[64,2048]{1,0:T(8,128)(2,1)}, bf16[64,2048]{1,0:T(8,128)(2,1)S(1)}, u32[]{:S(2)}) copy-start(bf16[64,2048]{1,0:T(8,128)(2,1)S(1)} %get-tuple-element.27.maps_ref) | copy-start | bytes 786436
  47.6 4.9 %collective-permute-start.5 = (f32[32,256]{1,0:T(8,128)S(1)}, f32[32,256]{1,0:T(8,128)S(1)}, u32[]{:S(2)}, u32[]{:S(2)}) collective-permute-start(f32[32,256]{1,0:T(8,128)S(1)} %get-tuple-element.23.own_ref), channel_id=1, source_target_pairs={{0,3},{1,2},{2,1},{3,0},{4,7},{5,6},{6,5},{7,4},{8,11},{9,10},{10,... | collective-permute-start | bytes 98312 | tf_op jit(solution)/shard_map/ppermute | solution.py:174
  47.7 5.5 %collective-permute-start.4 = (f32[32,256]{1,0:T(8,128)S(1)}, f32[32,256]{1,0:T(8,128)S(1)}, u32[]{:S(2)}, u32[]{:S(2)}) collective-permute-start(f32[32,256]{1,0:T(8,128)S(1)} %get-tuple-element.23.own_ref), channel_id=1, source_target_pairs={{0,2},{1,3},{2,0},{3,1},{4,6},{5,7},{6,4},{7,5},{8,10},{9,11},{10,... | collective-permute-start | bytes 98312 | tf_op jit(solution)/shard_map/ppermute | solution.py:174
  48.8 4.4 %collective-permute-start.3 = (f32[32,256]{1,0:T(8,128)S(1)}, f32[32,256]{1,0:T(8,128)S(1)}, u32[]{:S(2)}, u32[]{:S(2)}) collective-permute-start(f32[32,256]{1,0:T(8,128)S(1)} %get-tuple-element.23.own_ref), channel_id=1, source_target_pairs={{0,1},{1,0},{2,3},{3,2},{4,5},{5,4},{6,7},{7,6},{8,9},{9,8},{10,11... | collective-permute-start | bytes 98312 | tf_op jit(solution)/shard_map/ppermute | solution.py:174
  73.0 5.0 %copy-start.3 = (bf16[64,2048]{1,0:T(8,128)(2,1)S(1)}, bf16[64,2048]{1,0:T(8,128)(2,1)}, u32[]{:S(2)}) copy-start(bf16[64,2048]{1,0:T(8,128)(2,1)} %copy-done.2) | copy-start | bytes 786436
  73.0 15.6 %all-to-all-start.3 = ((f32[64,4,128]{2,1,0:T(4,128)}), f32[64,4,128]{2,1,0:T(4,128)S(1)}, u32[]{:S(2)}, u32[]{:S(2)}) async-start(f32[64,4,128]{2,1,0:T(4,128)} %bitcast.10), calls=%async_computation.3 | async-start | bytes 262144 | tf_op jit(solution)/shard_map/all_to_all | solution.py:170

commit v10 on v9

--- a/solution.py
+++ b/solution.py
@@ -1,3 +1,5 @@
+import functools
+
 import jax
 import jax.numpy as jnp
 from jax import lax
@@ -47,12 +49,13 @@
     out_ref[...] = out_f[...].astype(BF16)
 
 
-def cut_tokens(place_ref, grad_hbm, packed_hbm, near_ref, far_ref, sems):
-    width = near_ref.shape[1]
+def cut_tokens(ks, place_ref, grad_hbm, packed_hbm, out_ref, sems):
+    width = out_ref.shape[1]
     copies = []
-    for k, piece in ((2, far_ref.at[pl.ds(0, 64), :]), (3, far_ref.at[pl.ds(64, 64), :]), (1, near_ref)):
+    for n, k in enumerate(ks):
         first = pl.multiple_of(lax.bitwise_xor(place_ref[0], k) * width, width)
-        copies.append(pltpu.make_async_copy(grad_hbm.at[:, pl.ds(first, width)], piece, sems.at[k - 1]))
+        piece = out_ref.at[pl.ds(n * 64, 64), :]
+        copies.append(pltpu.make_async_copy(grad_hbm.at[:, pl.ds(first, width)], piece, sems.at[n]))
     for copy in copies:
         copy.start()
     for copy in copies:
@@ -192,17 +195,22 @@
         ],
         limit=56 * MIB,
     )(down_weight, up_weight, adapter_of_row.reshape(2, BLOCK))
-    near, far = call(
-        cut_tokens,
-        [((64, width), BF16), ((128, width), BF16)],
-        [SMEM, ANY, ANY],
-        [pltpu.SemaphoreType.DMA((3,))],
-        limit=56 * MIB,
-    )(me, output_gradient, packed)
+
+    def cut(ks, flops):
+        return call(
+            functools.partial(cut_tokens, ks),
+            [((64 * len(ks), width), BF16)],
+            [SMEM, ANY, ANY],
+            [pltpu.SemaphoreType.DMA((len(ks),))],
+            cost=pl.CostEstimate(flops=flops, bytes_accessed=len(ks) << 19, transcendentals=0),
+            limit=56 * MIB,
+        )(me, output_gradient, packed)[0]
+
+    far, near = cut((2, 3), 1000), cut((1,), 10 ** 10)
     live = (adapter_of_row >= 0) & (jnp.arange(2 * BLOCK, dtype=jnp.int32) < lengths[0])
     live = live.astype(F32).reshape(2, BLOCK)
     tables = swap(packed)
-    tables, near, far = lax.optimization_barrier((tables, near, far))
+    tables, near = lax.optimization_barrier((tables, near))
     near, far = from_peer(near, 1), from_peer(far, 2)
     odd, live = lax.optimization_barrier((from_peer(far[64:], 1), live))
     pieces = [near, far, odd]

time: 89.8 us -> 89.4 us (level)
  waiting for transfers between devices: 29.7 us -> 26.3 us
  Pallas kernels: 8.93 us -> 10.4 us
    ppermute x6, waiting for transfers between devices: 10 us -> 2.35 us  [from_peer(): return lax.ppermute(x, 'tensor', [(i, i ^ k) for i in range(4)])]
    all_to_all x3, waiting for transfers between devices: 19.7 us -> 23.9 us  [swap(): return lax.all_to_all(chunks, 'dp', 0, 0, tiled=True).reshape(x.shape)]
    pallas_call x1 -> x2, Pallas kernels: 2.16 us -> 3.59 us  [cut(): call(functools.partial(cut_tokens, ks), [((64 * len(ks), width), BF16)],...]
  transfers between devices with their start and end apart: 9 -> 9, of which waited for: 7 -> 6; matrix products, arithmetic and copies ran while one was open for 0% -> 0% of each run, Pallas kernels for 5% -> 7%
where the time goes in v10:
time: 89.4 us; the launch traced here: 88.9 us
  starting transfers between devices  30.4 us (34%)
  waiting for transfers between devices  26.3 us (29%)
  blocking collectives  18.8 us (21%)
  Pallas kernels  10.4 us (12%)
  local copies, waits for them, and re-layouts  1.52 us (2%)
  between operations  1.46 us (2%)
    all_to_all x3, starting transfers between devices, swap(): return lax.all_to_all(chunks, 'dp', 0, 0, tiled=True).reshape(x.shape)  24.7 us
    all_to_all x3, waiting for transfers between devices, swap(): return lax.all_to_all(chunks, 'dp', 0, 0, tiled=True).reshape(x.shape)  23.9 us
    all_to_all x1, blocking collectives, swap(): return lax.all_to_all(chunks, 'dp', 0, 0, tiled=True).reshape(x.shape)  18.8 us
    ppermute x6, starting transfers between devices, from_peer(): return lax.ppermute(x, 'tensor', [(i, i ^ k) for i in range(4)])  5.75 us
    pallas_call x2, Pallas kernels, cut(): call(functools.partial(cut_tokens, ks), [((64 * len(ks), width), BF16)],...  3.59 us
    ppermute x6, waiting for transfers between devices, from_peer(): return lax.ppermute(x, 'tensor', [(i, i ^ k) for i in range(4)])  2.35 us
  transfers between devices with their start and end apart: 9, of which 6 were waited for; matrix products, arithmetic and copies ran while one was open for 0% of the time, Pallas kernels for 7%

profile of v10, /device:TPU:2, one launch (start us, length us, event | category | flops | bytes accessed | tf_op | source)
XLA Modules:
  0.0 88.9 jit_solution(16394190318017182175)
XLA Ops:
  0.6 1.5 %shard_map.85.packed_hbm = bf16[512,128]{1,0:T(8,128)(2,1)} custom-call(bf16[8,2048]{1,0:T(8,128)(2,1)} %down_hbm.1, bf16[8,2048]{1,0:T(8,128)(2,1)} %up_hbm.1, s32[2,128]{1,0:T(2,128)} %bitcast.21), custom_call_target="tpu_custom_call" | custom-call | tf_op jit(solution)/shard_map/pallas_call | solution.py:184
  2.2 13.2 %all-to-all-start = ((bf16[64,8,128]{2,1,0:T(8,128)(2,1)}), bf16[64,8,128]{2,1,0:T(8,128)(2,1)S(1)}, u32[]{:S(2)}, u32[]{:S(2)}) async-start(bf16[64,8,128]{2,1,0:T(8,128)(2,1)} %bitcast.20), calls=%async_computation | async-start | bytes 262144 | tf_op jit(solution)/shard_map/all_to_all | solution.py:173
  15.4 1.8 %shard_map.88 = bf16[128,2048]{1,0:T(8,128)(2,1)} custom-call(s32[1]{0:T(128)} %bitcast.place_ref, bf16[64,8192]{1,0:T(8,128)(2,1)} %tokens_ref.1, bf16[512,128]{1,0:T(8,128)(2,1)} %shard_map.85.packed_hbm), custom_call_target="tpu_custom_call" | custom-call | flops 1000 | bytes 1048576 | tf_op jit(solution)/shard_map/pallas_call | solution.py:200
  17.2 2.2 %collective-permute-start.1 = (bf16[128,2048]{1,0:T(8,128)(2,1)}, bf16[128,2048]{1,0:T(8,128)(2,1)S(1)}, u32[]{:S(2)}, u32[]{:S(2)}) collective-permute-start(bf16[128,2048]{1,0:T(8,128)(2,1)} %shard_map.88), channel_id=1, source_target_pairs={{0,2},{1,3},{2,0},{3,1},{4,6},{5,7},{6,4},{7,5},{8,10},{9,11},{10,... | collective-permute-start | bytes 1572872 | tf_op jit(solution)/shard_map/ppermute | solution.py:177
  19.5 1.7 %shard_map.86 = bf16[64,2048]{1,0:T(8,128)(2,1)} custom-call(s32[1]{0:T(128)} %bitcast.place_ref, bf16[64,8192]{1,0:T(8,128)(2,1)} %tokens_ref.1, bf16[512,128]{1,0:T(8,128)(2,1)} %shard_map.85.packed_hbm), custom_call_target="tpu_custom_call" | custom-call | flops 10000000000 | bytes 524288 | tf_op jit(solution)/shard_map/pallas_call | solution.py:200
  21.2 0.0 copy-start
  21.2 4.8 %all-to-all-done = bf16[64,8,128]{2,1,0:T(8,128)(2,1)S(1)} async-done(((bf16[64,8,128]{2,1,0:T(8,128)(2,1)}), bf16[64,8,128]{2,1,0:T(8,128)(2,1)S(1)}, u32[]{:S(2)}, u32[]{:S(2)}) %all-to-all-start) | async-done | bytes 131104 | tf_op jit(solution)/shard_map/all_to_all | solution.py:173
  26.0 1.0 %shard_map.87 = bf16[1024,128]{1,0:T(8,128)(2,1)} custom-call(bf16[512,128]{1,0:T(8,128)(2,1)S(1)} %bitcast.14), custom_call_target="tpu_custom_call" | custom-call | tf_op jit(solution)/shard_map/pallas_call | solution.py:217
  27.0 6.5 %all-to-all-start.1 = ((bf16[64,16,128]{2,1,0:T(8,128)(2,1)}), bf16[64,16,128]{2,1,0:T(8,128)(2,1)S(1)}, u32[]{:S(2)}, u32[]{:S(2)}) async-start(bf16[64,16,128]{2,1,0:T(8,128)(2,1)} %bitcast.4), calls=%async_computation.1 | async-start | bytes 524288 | tf_op jit(solution)/shard_map/all_to_all | solution.py:173
  33.6 0.0 collective-permute-done.1.two_ref
  33.6 0.1 collective-permute-start.2
  33.7 0.8 copy-done.5
  34.5 0.0 collective-permute-start
  35.2 0.0 copy-start.4
  35.2 0.7 copy-done.4
  35.9 0.0 collective-permute-done.2.three_ref
  35.9 0.2 collective-permute-done.one_ref
  36.1 10.0 %all-to-all-done.1 = bf16[64,16,128]{2,1,0:T(8,128)(2,1)S(1)} async-done(((bf16[64,16,128]{2,1,0:T(8,128)(2,1)}), bf16[64,16,128]{2,1,0:T(8,128)(2,1)S(1)}, u32[]{:S(2)}, u32[]{:S(2)}) %all-to-all-start.1) | async-done | bytes 262176 | tf_op jit(solution)/shard_map/all_to_all | solution.py:173
  46.1 0.7 shard_map.89
  46.8 0.0 copy-start.2
  46.8 0.1 collective-permute-start.5
  46.9 1.5 %collective-permute-start.4 = (f32[32,256]{1,0:T(8,128)S(1)}, f32[32,256]{1,0:T(8,128)S(1)}, u32[]{:S(2)}, u32[]{:S(2)}) collective-permute-start(f32[32,256]{1,0:T(8,128)S(1)} %get-tuple-element.17.own_ref), channel_id=1, source_target_pairs={{0,2},{1,3},{2,0},{3,1},{4,6},{5,7},{6,4},{7,5},{8,10},{9,11},{10,... | collective-permute-start | bytes 98312 | tf_op jit(solution)/shard_map/ppermute | solution.py:177
  48.4 1.9 %collective-permute-start.3 = (f32[32,256]{1,0:T(8,128)S(1)}, f32[32,256]{1,0:T(8,128)S(1)}, u32[]{:S(2)}, u32[]{:S(2)}) collective-permute-start(f32[32,256]{1,0:T(8,128)S(1)} %get-tuple-element.17.own_ref), channel_id=1, source_target_pairs={{0,1},{1,0},{2,3},{3,2},{4,5},{5,4},{6,7},{7,6},{8,9},{9,8},{10,11... | collective-permute-start | bytes 98312 | tf_op jit(solution)/shard_map/ppermute | solution.py:177
  50.3 1.5 %collective-permute-done.5.three_ref = f32[32,256]{1,0:T(8,128)S(1)} collective-permute-done((f32[32,256]{1,0:T(8,128)S(1)}, f32[32,256]{1,0:T(8,128)S(1)}, u32[]{:S(2)}, u32[]{:S(2)}) %collective-permute-start.5) | collective-permute-done | bytes 32800 | tf_op jit(solution)/shard_map/ppermute | solution.py:177
  51.7 0.7 collective-permute-done.4.two_ref
  52.4 0.4 shard_map.90
  52.9 18.8 %all_to_all.20 = bf16[64,16,128]{2,1,0:T(8,128)(2,1)S(1)} all-to-all(bf16[64,16,128]{2,1,0:T(8,128)(2,1)S(1)} %bitcast.19), channel_id=1, replica_groups=mesh['dp'=64,'tensor'=4] {'dp'}, dimensions={0} | all-to-all | bytes 524288 | tf_op jit(solution)/shard_map/all_to_all | solution.py:173
  71.7 1.0 %shard_map.92 = f32[256,128]{1,0:T(8,128)} custom-call(bf16[1024,128]{1,0:T(8,128)(2,1)S(1)} %bitcast.17, bf16[512,128]{1,0:T(8,128)(2,1)S(1)} %bitcast.15), custom_call_target="tpu_custom_call" | custom-call | tf_op jit(solution)/shard_map/pallas_call | solution.py:242
  72.7 4.9 %all-to-all-start.3 = ((f32[64,4,128]{2,1,0:T(4,128)}), f32[64,4,128]{2,1,0:T(4,128)S(1)}, u32[]{:S(2)}, u32[]{:S(2)}) async-start(f32[64,4,128]{2,1,0:T(4,128)} %bitcast.10), calls=%async_computation.3 | async-start | bytes 262144 | tf_op jit(solution)/shard_map/all_to_all | solution.py:173
  77.6 1.4 %shard_map.91 = bf16[256,2048]{1,0:T(8,128)(2,1)} custom-call(bf16[32,256]{1,0:T(8,128)(2,1)S(1)} %get-tuple-element.20.ranks_ref, bf16[64,2048]{1,0:T(8,128)(2,1)S(1)} %copy-done.3), custom_call_target="tpu_custom_call" | custom-call | flops 33554432 | bytes 2097152 | tf_op jit(solution)/shard_map/pallas_call | solution.py:236
  79.1 9.2 %all-to-all-done.3 = f32[64,4,128]{2,1,0:T(4,128)S(1)} async-done(((f32[64,4,128]{2,1,0:T(4,128)}), f32[64,4,128]{2,1,0:T(4,128)S(1)}, u32[]{:S(2)}, u32[]{:S(2)}) %all-to-all-start.3) | async-done | bytes 131104 | tf_op jit(solution)/shard_map/all_to_all | solution.py:173
  88.2 0.7 shard_map.93
  (10 shorter events, 0.0 us)
Async XLA Ops:
  2.2 23.8 %all-to-all-start = ((bf16[64,8,128]{2,1,0:T(8,128)(2,1)}), bf16[64,8,128]{2,1,0:T(8,128)(2,1)S(1)}, u32[]{:S(2)}, u32[]{:S(2)}) async-start(bf16[64,8,128]{2,1,0:T(8,128)(2,1)} %bitcast.20), calls=%async_computation | async-start | bytes 262144 | tf_op jit(solution)/shard_map/all_to_all | solution.py:173
  17.2 16.3 %collective-permute-start.1 = (bf16[128,2048]{1,0:T(8,128)(2,1)}, bf16[128,2048]{1,0:T(8,128)(2,1)S(1)}, u32[]{:S(2)}, u32[]{:S(2)}) collective-permute-start(bf16[128,2048]{1,0:T(8,128)(2,1)} %shard_map.88), channel_id=1, source_target_pairs={{0,2},{1,3},{2,0},{3,1},{4,6},{5,7},{6,4},{7,5},{8,10},{9,11},{10,... | collective-permute-start | bytes 1572872 | tf_op jit(solution)/shard_map/ppermute | solution.py:177
  19.5 26.6 %copy-start.1 = (bf16[256,2048]{1,0:T(8,128)(2,1)S(1)}, bf16[256,2048]{1,0:T(8,128)(2,1)}, u32[]{:S(2)}) copy-start(bf16[256,2048]{1,0:T(8,128)(2,1)} %attn_ref.3) | copy-start | bytes 3145732
  21.2 24.9 %copy-start = (bf16[64,8192]{1,0:T(8,128)(2,1)S(1)}, bf16[64,8192]{1,0:T(8,128)(2,1)}, u32[]{:S(2)}) copy-start(bf16[64,8192]{1,0:T(8,128)(2,1)} %tokens_ref.1) | copy-start | bytes 3145732
  27.0 19.0 %all-to-all-start.1 = ((bf16[64,16,128]{2,1,0:T(8,128)(2,1)}), bf16[64,16,128]{2,1,0:T(8,128)(2,1)S(1)}, u32[]{:S(2)}, u32[]{:S(2)}) async-start(bf16[64,16,128]{2,1,0:T(8,128)(2,1)} %bitcast.4), calls=%async_computation.1 | async-start | bytes 524288 | tf_op jit(solution)/shard_map/all_to_all | solution.py:173
  33.6 1.0 %copy-start.5 = (bf16[64,2048]{1,0:T(8,128)(2,1)S(1)}, bf16[64,2048]{1,0:T(8,128)(2,1)}, u32[]{:S(2)}) copy-start(bf16[64,2048]{1,0:T(8,128)(2,1)} %shard_map.86) | copy-start | bytes 786436
  33.6 2.2 %collective-permute-start.2 = (bf16[64,2048]{1,0:T(8,128)(2,1)S(1)}, bf16[64,2048]{1,0:T(8,128)(2,1)S(1)}, u32[]{:S(2)}, u32[]{:S(2)}) collective-permute-start(bf16[64,2048]{1,0:T(8,128)(2,1)S(1)} %slice.4), channel_id=1, source_target_pairs={{0,1},{1,0},{2,3},{3,2},{4,5},{5,4},{6,7},{7,6},{8,9},{9,8},{10,11... | collective-permute-start | bytes 786440 | tf_op jit(solution)/shard_map/ppermute | solution.py:177
  34.5 1.5 %collective-permute-start = (bf16[64,2048]{1,0:T(8,128)(2,1)S(1)}, bf16[64,2048]{1,0:T(8,128)(2,1)S(1)}, u32[]{:S(2)}, u32[]{:S(2)}) collective-permute-start(bf16[64,2048]{1,0:T(8,128)(2,1)S(1)} %copy-done.5), channel_id=1, source_target_pairs={{0,1},{1,0},{2,3},{3,2},{4,5},{5,4},{6,7},{7,6},{8,9},{9,8},{10,11... | collective-permute-start | bytes 786440 | tf_op jit(solution)/shard_map/ppermute | solution.py:177
  35.2 0.7 copy-start.4
  46.8 6.0 %copy-start.2 = (bf16[64,2048]{1,0:T(8,128)(2,1)}, bf16[64,2048]{1,0:T(8,128)(2,1)S(1)}, u32[]{:S(2)}) copy-start(bf16[64,2048]{1,0:T(8,128)(2,1)S(1)} %get-tuple-element.21.maps_ref) | copy-start | bytes 786436
  46.8 4.9 %collective-permute-start.5 = (f32[32,256]{1,0:T(8,128)S(1)}, f32[32,256]{1,0:T(8,128)S(1)}, u32[]{:S(2)}, u32[]{:S(2)}) collective-permute-start(f32[32,256]{1,0:T(8,128)S(1)} %get-tuple-element.17.own_ref), channel_id=1, source_target_pairs={{0,3},{1,2},{2,1},{3,0},{4,7},{5,6},{6,5},{7,4},{8,11},{9,10},{10,... | collective-permute-start | bytes 98312 | tf_op jit(solution)/shard_map/ppermute | solution.py:177
  46.9 5.5 %collective-permute-start.4 = (f32[32,256]{1,0:T(8,128)S(1)}, f32[32,256]{1,0:T(8,128)S(1)}, u32[]{:S(2)}, u32[]{:S(2)}) collective-permute-start(f32[32,256]{1,0:T(8,128)S(1)} %get-tuple-element.17.own_ref), channel_id=1, source_target_pairs={{0,2},{1,3},{2,0},{3,1},{4,6},{5,7},{6,4},{7,5},{8,10},{9,11},{10,... | collective-permute-start | bytes 98312 | tf_op jit(solution)/shard_map/ppermute | solution.py:177
  48.4 4.0 %collective-permute-start.3 = (f32[32,256]{1,0:T(8,128)S(1)}, f32[32,256]{1,0:T(8,128)S(1)}, u32[]{:S(2)}, u32[]{:S(2)}) collective-permute-start(f32[32,256]{1,0:T(8,128)S(1)} %get-tuple-element.17.own_ref), channel_id=1, source_target_pairs={{0,1},{1,0},{2,3},{3,2},{4,5},{5,4},{6,7},{7,6},{8,9},{9,8},{10,11... | collective-permute-start | bytes 98312 | tf_op jit(solution)/shard_map/ppermute | solution.py:177
  72.7 4.9 %copy-start.3 = (bf16[64,2048]{1,0:T(8,128)(2,1)S(1)}, bf16[64,2048]{1,0:T(8,128)(2,1)}, u32[]{:S(2)}) copy-start(bf16[64,2048]{1,0:T(8,128)(2,1)} %copy-done.2) | copy-start | bytes 786436
  72.7 15.5 %all-to-all-start.3 = ((f32[64,4,128]{2,1,0:T(4,128)}), f32[64,4,128]{2,1,0:T(4,128)S(1)}, u32[]{:S(2)}, u32[]{:S(2)}) async-start(f32[64,4,128]{2,1,0:T(4,128)} %bitcast.10), calls=%async_computation.3 | async-start | bytes 262144 | tf_op jit(solution)/shard_map/all_to_all | solution.py:173

commit v11 on v10

--- a/solution.py
+++ b/solution.py
@@ -226,7 +226,8 @@
         [((64, width), BF16), ((2 * BLOCK, width), BF16), ((32, 2 * BLOCK), F32)],
         [SMEM] + [VMEM] * 6,
     )(me, picked, attn, output_gradient, *pieces)
-    parts = [part] + [from_peer(part, k) for k in (1, 2, 3)]
+    across, beside = from_peer(part, 2), from_peer(part, 1)
+    parts = [part, beside, across, from_peer(across, 1)]
     ranks, terms = call(
         make_terms,
         [((32, 2 * BLOCK), BF16), ((16 * PEERS, LANES), BF16)],

time: 89.4 us -> 89.9 us (level)
  waiting for transfers between devices: 26.3 us -> 29.3 us
  starting transfers between devices: 30.4 us -> 28.6 us
    ppermute x6, waiting for transfers between devices: 2.35 us -> 5.41 us  [from_peer(): return lax.ppermute(x, 'tensor', [(i, i ^ k) for i in range(4)])]
    ppermute x6, starting transfers between devices: 5.75 us -> 3.8 us  [from_peer(): return lax.ppermute(x, 'tensor', [(i, i ^ k) for i in range(4)])]
where the time goes in v11:
time: 89.9 us; the launch traced here: 89.5 us
  waiting for transfers between devices  29.3 us (33%)
  starting transfers between devices  28.6 us (32%)
  blocking collectives  18.2 us (20%)
  Pallas kernels  10.4 us (12%)
  local copies, waits for them, and re-layouts  1.52 us (2%)
  between operations  1.45 us (2%)
    all_to_all x3, starting transfers between devices, swap(): return lax.all_to_all(chunks, 'dp', 0, 0, tiled=True).reshape(x.shape)  24.8 us
    all_to_all x3, waiting for transfers between devices, swap(): return lax.all_to_all(chunks, 'dp', 0, 0, tiled=True).reshape(x.shape)  23.9 us
    all_to_all x1, blocking collectives, swap(): return lax.all_to_all(chunks, 'dp', 0, 0, tiled=True).reshape(x.shape)  18.2 us
    ppermute x6, waiting for transfers between devices, from_peer(): return lax.ppermute(x, 'tensor', [(i, i ^ k) for i in range(4)])  5.41 us
    ppermute x6, starting transfers between devices, from_peer(): return lax.ppermute(x, 'tensor', [(i, i ^ k) for i in range(4)])  3.8 us
    pallas_call x2, Pallas kernels, cut(): call(functools.partial(cut_tokens, ks), [((64 * len(ks), width), BF16)],...  3.59 us
  transfers between devices with their start and end apart: 9, of which 6 were waited for; matrix products, arithmetic and copies ran while one was open for 0% of the time, Pallas kernels for 7%

profile of v11, /device:TPU:2, one launch (start us, length us, event | category | flops | bytes accessed | tf_op | source)
XLA Modules:
  0.0 89.5 jit_solution(16906688111744496531)
XLA Ops:
  0.6 1.5 %shard_map.85.packed_hbm = bf16[512,128]{1,0:T(8,128)(2,1)} custom-call(bf16[8,2048]{1,0:T(8,128)(2,1)} %down_hbm.1, bf16[8,2048]{1,0:T(8,128)(2,1)} %up_hbm.1, s32[2,128]{1,0:T(2,128)} %bitcast.21), custom_call_target="tpu_custom_call" | custom-call | tf_op jit(solution)/shard_map/pallas_call | solution.py:184
  2.2 13.2 %all-to-all-start = ((bf16[64,8,128]{2,1,0:T(8,128)(2,1)}), bf16[64,8,128]{2,1,0:T(8,128)(2,1)S(1)}, u32[]{:S(2)}, u32[]{:S(2)}) async-start(bf16[64,8,128]{2,1,0:T(8,128)(2,1)} %bitcast.20), calls=%async_computation | async-start | bytes 262144 | tf_op jit(solution)/shard_map/all_to_all | solution.py:173
  15.4 1.8 %shard_map.88 = bf16[128,2048]{1,0:T(8,128)(2,1)} custom-call(s32[1]{0:T(128)} %bitcast.place_ref, bf16[64,8192]{1,0:T(8,128)(2,1)} %tokens_ref.1, bf16[512,128]{1,0:T(8,128)(2,1)} %shard_map.85.packed_hbm), custom_call_target="tpu_custom_call" | custom-call | flops 1000 | bytes 1048576 | tf_op jit(solution)/shard_map/pallas_call | solution.py:200
  17.2 2.2 %collective-permute-start.1 = (bf16[128,2048]{1,0:T(8,128)(2,1)}, bf16[128,2048]{1,0:T(8,128)(2,1)S(1)}, u32[]{:S(2)}, u32[]{:S(2)}) collective-permute-start(bf16[128,2048]{1,0:T(8,128)(2,1)} %shard_map.88), channel_id=1, source_target_pairs={{0,2},{1,3},{2,0},{3,1},{4,6},{5,7},{6,4},{7,5},{8,10},{9,11},{10,... | collective-permute-start | bytes 1572872 | tf_op jit(solution)/shard_map/ppermute | solution.py:177
  19.5 1.7 %shard_map.86 = bf16[64,2048]{1,0:T(8,128)(2,1)} custom-call(s32[1]{0:T(128)} %bitcast.place_ref, bf16[64,8192]{1,0:T(8,128)(2,1)} %tokens_ref.1, bf16[512,128]{1,0:T(8,128)(2,1)} %shard_map.85.packed_hbm), custom_call_target="tpu_custom_call" | custom-call | flops 10000000000 | bytes 524288 | tf_op jit(solution)/shard_map/pallas_call | solution.py:200
  21.2 0.0 copy-start
  21.2 4.8 %all-to-all-done = bf16[64,8,128]{2,1,0:T(8,128)(2,1)S(1)} async-done(((bf16[64,8,128]{2,1,0:T(8,128)(2,1)}), bf16[64,8,128]{2,1,0:T(8,128)(2,1)S(1)}, u32[]{:S(2)}, u32[]{:S(2)}) %all-to-all-start) | async-done | bytes 131104 | tf_op jit(solution)/shard_map/all_to_all | solution.py:173
  26.0 1.0 %shard_map.87 = bf16[1024,128]{1,0:T(8,128)(2,1)} custom-call(bf16[512,128]{1,0:T(8,128)(2,1)S(1)} %bitcast.14), custom_call_target="tpu_custom_call" | custom-call | tf_op jit(solution)/shard_map/pallas_call | solution.py:217
  27.0 6.5 %all-to-all-start.1 = ((bf16[64,16,128]{2,1,0:T(8,128)(2,1)}), bf16[64,16,128]{2,1,0:T(8,128)(2,1)S(1)}, u32[]{:S(2)}, u32[]{:S(2)}) async-start(bf16[64,16,128]{2,1,0:T(8,128)(2,1)} %bitcast.4), calls=%async_computation.1 | async-start | bytes 524288 | tf_op jit(solution)/shard_map/all_to_all | solution.py:173
  33.6 0.0 collective-permute-done.1.two_ref
  33.6 0.1 collective-permute-start.2
  33.7 0.8 copy-done.5
  34.5 0.0 collective-permute-start
  35.2 0.0 copy-start.4
  35.2 0.7 copy-done.4
  35.9 0.0 collective-permute-done.2.three_ref
  35.9 0.2 collective-permute-done.one_ref
  36.1 10.0 %all-to-all-done.1 = bf16[64,16,128]{2,1,0:T(8,128)(2,1)S(1)} async-done(((bf16[64,16,128]{2,1,0:T(8,128)(2,1)}), bf16[64,16,128]{2,1,0:T(8,128)(2,1)S(1)}, u32[]{:S(2)}, u32[]{:S(2)}) %all-to-all-start.1) | async-done | bytes 262176 | tf_op jit(solution)/shard_map/all_to_all | solution.py:173
  46.1 0.7 shard_map.89
  46.8 0.0 copy-start.2
  46.8 1.5 %collective-permute-start.4 = (f32[32,256]{1,0:T(8,128)S(1)}, f32[32,256]{1,0:T(8,128)S(1)}, u32[]{:S(2)}, u32[]{:S(2)}) collective-permute-start(f32[32,256]{1,0:T(8,128)S(1)} %get-tuple-element.17.own_ref), channel_id=1, source_target_pairs={{0,2},{1,3},{2,0},{3,1},{4,6},{5,7},{6,4},{7,5},{8,10},{9,11},{10,... | collective-permute-start | bytes 98312 | tf_op jit(solution)/shard_map/ppermute | solution.py:177
  48.3 0.0 collective-permute-start.3
  48.3 4.0 %collective-permute-done.4.two_ref = f32[32,256]{1,0:T(8,128)S(1)} collective-permute-done((f32[32,256]{1,0:T(8,128)S(1)}, f32[32,256]{1,0:T(8,128)S(1)}, u32[]{:S(2)}, u32[]{:S(2)}) %collective-permute-start.4) | collective-permute-done | bytes 32800 | tf_op jit(solution)/shard_map/ppermute | solution.py:177
  52.3 0.0 collective-permute-start.5
  52.3 1.2 %collective-permute-done.5.three_ref = f32[32,256]{1,0:T(8,128)S(1)} collective-permute-done((f32[32,256]{1,0:T(8,128)S(1)}, f32[32,256]{1,0:T(8,128)S(1)}, u32[]{:S(2)}, u32[]{:S(2)}) %collective-permute-start.5) | collective-permute-done | bytes 32800 | tf_op jit(solution)/shard_map/ppermute | solution.py:177
  53.5 0.4 shard_map.90
  54.0 18.2 %all_to_all.20 = bf16[64,16,128]{2,1,0:T(8,128)(2,1)S(1)} all-to-all(bf16[64,16,128]{2,1,0:T(8,128)(2,1)S(1)} %bitcast.19), channel_id=1, replica_groups=mesh['dp'=64,'tensor'=4] {'dp'}, dimensions={0} | all-to-all | bytes 524288 | tf_op jit(solution)/shard_map/all_to_all | solution.py:173
  72.2 1.0 %shard_map.92 = f32[256,128]{1,0:T(8,128)} custom-call(bf16[1024,128]{1,0:T(8,128)(2,1)S(1)} %bitcast.17, bf16[512,128]{1,0:T(8,128)(2,1)S(1)} %bitcast.15), custom_call_target="tpu_custom_call" | custom-call | tf_op jit(solution)/shard_map/pallas_call | solution.py:243
  73.2 5.0 %all-to-all-start.3 = ((f32[64,4,128]{2,1,0:T(4,128)}), f32[64,4,128]{2,1,0:T(4,128)S(1)}, u32[]{:S(2)}, u32[]{:S(2)}) async-start(f32[64,4,128]{2,1,0:T(4,128)} %bitcast.10), calls=%async_computation.3 | async-start | bytes 262144 | tf_op jit(solution)/shard_map/all_to_all | solution.py:173
  78.2 1.4 %shard_map.91 = bf16[256,2048]{1,0:T(8,128)(2,1)} custom-call(bf16[32,256]{1,0:T(8,128)(2,1)S(1)} %get-tuple-element.20.ranks_ref, bf16[64,2048]{1,0:T(8,128)(2,1)S(1)} %copy-done.3), custom_call_target="tpu_custom_call" | custom-call | flops 33554432 | bytes 2097152 | tf_op jit(solution)/shard_map/pallas_call | solution.py:237
  79.6 9.1 %all-to-all-done.3 = f32[64,4,128]{2,1,0:T(4,128)S(1)} async-done(((f32[64,4,128]{2,1,0:T(4,128)}), f32[64,4,128]{2,1,0:T(4,128)S(1)}, u32[]{:S(2)}, u32[]{:S(2)}) %all-to-all-start.3) | async-done | bytes 131104 | tf_op jit(solution)/shard_map/all_to_all | solution.py:173
  88.8 0.7 shard_map.93
  (10 shorter events, 0.0 us)
Async XLA Ops:
  2.2 23.8 %all-to-all-start = ((bf16[64,8,128]{2,1,0:T(8,128)(2,1)}), bf16[64,8,128]{2,1,0:T(8,128)(2,1)S(1)}, u32[]{:S(2)}, u32[]{:S(2)}) async-start(bf16[64,8,128]{2,1,0:T(8,128)(2,1)} %bitcast.20), calls=%async_computation | async-start | bytes 262144 | tf_op jit(solution)/shard_map/all_to_all | solution.py:173
  17.2 16.3 %collective-permute-start.1 = (bf16[128,2048]{1,0:T(8,128)(2,1)}, bf16[128,2048]{1,0:T(8,128)(2,1)S(1)}, u32[]{:S(2)}, u32[]{:S(2)}) collective-permute-start(bf16[128,2048]{1,0:T(8,128)(2,1)} %shard_map.88), channel_id=1, source_target_pairs={{0,2},{1,3},{2,0},{3,1},{4,6},{5,7},{6,4},{7,5},{8,10},{9,11},{10,... | collective-permute-start | bytes 1572872 | tf_op jit(solution)/shard_map/ppermute | solution.py:177
  19.5 26.6 %copy-start.1 = (bf16[256,2048]{1,0:T(8,128)(2,1)S(1)}, bf16[256,2048]{1,0:T(8,128)(2,1)}, u32[]{:S(2)}) copy-start(bf16[256,2048]{1,0:T(8,128)(2,1)} %attn_ref.3) | copy-start | bytes 3145732
  21.2 24.9 %copy-start = (bf16[64,8192]{1,0:T(8,128)(2,1)S(1)}, bf16[64,8192]{1,0:T(8,128)(2,1)}, u32[]{:S(2)}) copy-start(bf16[64,8192]{1,0:T(8,128)(2,1)} %tokens_ref.1) | copy-start | bytes 3145732
  27.0 19.0 %all-to-all-start.1 = ((bf16[64,16,128]{2,1,0:T(8,128)(2,1)}), bf16[64,16,128]{2,1,0:T(8,128)(2,1)S(1)}, u32[]{:S(2)}, u32[]{:S(2)}) async-start(bf16[64,16,128]{2,1,0:T(8,128)(2,1)} %bitcast.4), calls=%async_computation.1 | async-start | bytes 524288 | tf_op jit(solution)/shard_map/all_to_all | solution.py:173
  33.6 1.0 %copy-start.5 = (bf16[64,2048]{1,0:T(8,128)(2,1)S(1)}, bf16[64,2048]{1,0:T(8,128)(2,1)}, u32[]{:S(2)}) copy-start(bf16[64,2048]{1,0:T(8,128)(2,1)} %shard_map.86) | copy-start | bytes 786436
  33.6 2.2 %collective-permute-start.2 = (bf16[64,2048]{1,0:T(8,128)(2,1)S(1)}, bf16[64,2048]{1,0:T(8,128)(2,1)S(1)}, u32[]{:S(2)}, u32[]{:S(2)}) collective-permute-start(bf16[64,2048]{1,0:T(8,128)(2,1)S(1)} %slice.4), channel_id=1, source_target_pairs={{0,1},{1,0},{2,3},{3,2},{4,5},{5,4},{6,7},{7,6},{8,9},{9,8},{10,11... | collective-permute-start | bytes 786440 | tf_op jit(solution)/shard_map/ppermute | solution.py:177
  34.5 1.5 %collective-permute-start = (bf16[64,2048]{1,0:T(8,128)(2,1)S(1)}, bf16[64,2048]{1,0:T(8,128)(2,1)S(1)}, u32[]{:S(2)}, u32[]{:S(2)}) collective-permute-start(bf16[64,2048]{1,0:T(8,128)(2,1)S(1)} %copy-done.5), channel_id=1, source_target_pairs={{0,1},{1,0},{2,3},{3,2},{4,5},{5,4},{6,7},{7,6},{8,9},{9,8},{10,11... | collective-permute-start | bytes 786440 | tf_op jit(solution)/shard_map/ppermute | solution.py:177
  35.2 0.7 copy-start.4
  46.8 7.2 %copy-start.2 = (bf16[64,2048]{1,0:T(8,128)(2,1)}, bf16[64,2048]{1,0:T(8,128)(2,1)S(1)}, u32[]{:S(2)}) copy-start(bf16[64,2048]{1,0:T(8,128)(2,1)S(1)} %get-tuple-element.21.maps_ref) | copy-start | bytes 786436
  46.8 5.5 %collective-permute-start.4 = (f32[32,256]{1,0:T(8,128)S(1)}, f32[32,256]{1,0:T(8,128)S(1)}, u32[]{:S(2)}, u32[]{:S(2)}) collective-permute-start(f32[32,256]{1,0:T(8,128)S(1)} %get-tuple-element.17.own_ref), channel_id=1, source_target_pairs={{0,2},{1,3},{2,0},{3,1},{4,6},{5,7},{6,4},{7,5},{8,10},{9,11},{10,... | collective-permute-start | bytes 98312 | tf_op jit(solution)/shard_map/ppermute | solution.py:177
  48.3 4.0 %collective-permute-start.3 = (f32[32,256]{1,0:T(8,128)S(1)}, f32[32,256]{1,0:T(8,128)S(1)}, u32[]{:S(2)}, u32[]{:S(2)}) collective-permute-start(f32[32,256]{1,0:T(8,128)S(1)} %get-tuple-element.17.own_ref), channel_id=1, source_target_pairs={{0,1},{1,0},{2,3},{3,2},{4,5},{5,4},{6,7},{7,6},{8,9},{9,8},{10,11... | collective-permute-start | bytes 98312 | tf_op jit(solution)/shard_map/ppermute | solution.py:177
  52.3 1.2 %collective-permute-start.5 = (f32[32,256]{1,0:T(8,128)S(1)}, f32[32,256]{1,0:T(8,128)S(1)}, u32[]{:S(2)}, u32[]{:S(2)}) collective-permute-start(f32[32,256]{1,0:T(8,128)S(1)} %collective-permute-done.4.two_ref), channel_id=1, source_target_pairs={{0,1},{1,0},{2,3},{3,2},{4,5},{5,4},{6,7},{7,6},{8,9},{9,8},{10,11... | collective-permute-start | bytes 98312 | tf_op jit(solution)/shard_map/ppermute | solution.py:177
  73.2 5.0 %copy-start.3 = (bf16[64,2048]{1,0:T(8,128)(2,1)S(1)}, bf16[64,2048]{1,0:T(8,128)(2,1)}, u32[]{:S(2)}) copy-start(bf16[64,2048]{1,0:T(8,128)(2,1)} %copy-done.2) | copy-start | bytes 786436
  73.2 15.6 %all-to-all-start.3 = ((f32[64,4,128]{2,1,0:T(4,128)}), f32[64,4,128]{2,1,0:T(4,128)S(1)}, u32[]{:S(2)}, u32[]{:S(2)}) async-start(f32[64,4,128]{2,1,0:T(4,128)} %bitcast.10), calls=%async_computation.3 | async-start | bytes 262144 | tf_op jit(solution)/shard_map/all_to_all | solution.py:173

commit v12 on v9

--- a/solution.py
+++ b/solution.py
@@ -59,6 +59,10 @@
         copy.wait()
 
 
+def copy_place(place_ref, out_ref):
+    out_ref[0] = place_ref[0]
+
+
 def pick_rows(in_ref, out_ref, in_f, out_f):
     in_f[...] = in_ref[...].astype(F32)
     table = jnp.concatenate([in_f[rows_of(k, PEERS, 8), :] for k in range(4)], axis=1).astype(BF16)
@@ -73,7 +77,9 @@
     out_ref[...] = out_f[...].astype(BF16)
 
 
-def project(place_ref, picked_ref, attn_ref, tokens_ref, one_ref, two_ref, three_ref, maps_ref, grad_ref, part_ref):
+def project(
+    place_ref, order_ref, picked_ref, attn_ref, tokens_ref, one_ref, two_ref, three_ref, maps_ref, grad_ref, part_ref
+):
     me = place_ref[0]
     width = grad_ref.shape[1]
     own = tokens_ref[:, pl.ds(pl.multiple_of(me * width, width), width)]
@@ -199,10 +205,17 @@
         [pltpu.SemaphoreType.DMA((3,))],
         limit=56 * MIB,
     )(me, output_gradient, packed)
+    order = pl.pallas_call(
+        copy_place,
+        out_shape=jax.ShapeDtypeStruct((1,), jnp.int32),
+        in_specs=[SMEM],
+        out_specs=SMEM,
+        cost_estimate=pl.CostEstimate(flops=10 ** 10, bytes_accessed=8, transcendentals=0),
+    )(me)
     live = (adapter_of_row >= 0) & (jnp.arange(2 * BLOCK, dtype=jnp.int32) < lengths[0])
     live = live.astype(F32).reshape(2, BLOCK)
     tables = swap(packed)
-    tables, near, far = lax.optimization_barrier((tables, near, far))
+    tables, order = lax.optimization_barrier((tables, order))
     near, far = from_peer(near, 1), from_peer(far, 2)
     odd, live = lax.optimization_barrier((from_peer(far[64:], 1), live))
     pieces = [near, far, odd]
@@ -216,8 +229,8 @@
     maps, grad, part = call(
         project,
         [((64, width), BF16), ((2 * BLOCK, width), BF16), ((32, 2 * BLOCK), F32)],
-        [SMEM] + [VMEM] * 6,
-    )(me, picked, attn, output_gradient, *pieces)
+        [SMEM, ANY] + [VMEM] * 6,
+    )(me, order, picked, attn, output_gradient, *pieces)
     parts = [part] + [from_peer(part, k) for k in (1, 2, 3)]
     ranks, terms = call(
         make_terms,

time: 89.8 us -> 89 us (level)
  waiting for transfers between devices: 29.7 us -> 27.6 us
  Pallas kernels: 8.93 us -> 9.94 us
    ppermute x6, waiting for transfers between devices: 10 us -> 2.71 us  [from_peer(): return lax.ppermute(x, 'tensor', [(i, i ^ k) for i in range(4)])]
    all_to_all x3, waiting for transfers between devices: 19.7 us -> 24.9 us  [swap(): return lax.all_to_all(chunks, 'dp', 0, 0, tiled=True).reshape(x.shape)]
  transfers between devices with their start and end apart: 9 -> 9, of which waited for: 7 -> 7; matrix products, arithmetic and copies ran while one was open for 0% -> 0% of each run, Pallas kernels for 5% -> 6%
where the time goes in v12:
time: 89 us; the launch traced here: 88.5 us
  starting transfers between devices  29.6 us (33%)
  waiting for transfers between devices  27.6 us (31%)
  blocking collectives  18.9 us (21%)
  Pallas kernels  9.94 us (11%)
  between operations  1.44 us (2%)
  local copies, waits for them, and re-layouts  1.04 us (1%)
    all_to_all x3, waiting for transfers between devices, swap(): return lax.all_to_all(chunks, 'dp', 0, 0, tiled=True).reshape(x.shape)  24.9 us
    all_to_all x3, starting transfers between devices, swap(): return lax.all_to_all(chunks, 'dp', 0, 0, tiled=True).reshape(x.shape)  23.6 us
    all_to_all x1, blocking collectives, swap(): return lax.all_to_all(chunks, 'dp', 0, 0, tiled=True).reshape(x.shape)  18.9 us
    ppermute x6, starting transfers between devices, from_peer(): return lax.ppermute(x, 'tensor', [(i, i ^ k) for i in range(4)])  5.92 us
    ppermute x6, waiting for transfers between devices, from_peer(): return lax.ppermute(x, 'tensor', [(i, i ^ k) for i in range(4)])  2.71 us
    pallas_call x1, Pallas kernels, per_device(): call(cut_tokens, [((64, width), BF16), ((128, width), BF16)], [SMEM, ANY,...  2.02 us
  transfers between devices with their start and end apart: 9, of which 7 were waited for; matrix products, arithmetic and copies ran while one was open for 0% of the time, Pallas kernels for 6%

profile of v12, /device:TPU:2, one launch (start us, length us, event | category | flops | bytes accessed | tf_op | source)
XLA Modules:
  0.0 88.5 jit_solution(17677019632006914883)
XLA Ops:
  0.6 1.5 %shard_map.85.packed_hbm = bf16[512,128]{1,0:T(8,128)(2,1)} custom-call(bf16[8,2048]{1,0:T(8,128)(2,1)} %down_hbm.1, bf16[8,2048]{1,0:T(8,128)(2,1)} %up_hbm.1, s32[2,128]{1,0:T(2,128)} %bitcast.21), custom_call_target="tpu_custom_call" | custom-call | tf_op jit(solution)/shard_map/pallas_call | solution.py:187
  2.2 13.2 %all-to-all-start = ((bf16[64,8,128]{2,1,0:T(8,128)(2,1)}), bf16[64,8,128]{2,1,0:T(8,128)(2,1)S(1)}, u32[]{:S(2)}, u32[]{:S(2)}) async-start(bf16[64,8,128]{2,1,0:T(8,128)(2,1)} %bitcast.20), calls=%async_computation | async-start | bytes 262144 | tf_op jit(solution)/shard_map/all_to_all | solution.py:176
  15.4 2.0 %shard_map.88 = (bf16[64,2048]{1,0:T(8,128)(2,1)}, bf16[128,2048]{1,0:T(8,128)(2,1)}) custom-call(s32[1]{0:T(128)} %bitcast.place_ref, bf16[64,8192]{1,0:T(8,128)(2,1)} %tokens_ref.1, bf16[512,128]{1,0:T(8,128)(2,1)} %shard_map.85.packed_hbm), custom_call_target="tpu_custom_call" | custom-call | tf_op jit(solution)/shard_map/pallas_call | solution.py:201
  17.4 2.2 %collective-permute-start.1 = (bf16[128,2048]{1,0:T(8,128)(2,1)}, bf16[128,2048]{1,0:T(8,128)(2,1)S(1)}, u32[]{:S(2)}, u32[]{:S(2)}) collective-permute-start(bf16[128,2048]{1,0:T(8,128)(2,1)} %get-tuple-element.19), channel_id=1, source_target_pairs={{0,2},{1,3},{2,0},{3,1},{4,6},{5,7},{6,4},{7,5},{8,10},{9,11},{10,... | collective-permute-start | bytes 1572872 | tf_op jit(solution)/shard_map/ppermute | solution.py:180
  19.6 0.5 shard_map.86.order_ref
  20.2 0.0 copy-start
  20.2 5.8 %all-to-all-done = bf16[64,8,128]{2,1,0:T(8,128)(2,1)S(1)} async-done(((bf16[64,8,128]{2,1,0:T(8,128)(2,1)}), bf16[64,8,128]{2,1,0:T(8,128)(2,1)S(1)}, u32[]{:S(2)}, u32[]{:S(2)}) %all-to-all-start) | async-done | bytes 131104 | tf_op jit(solution)/shard_map/all_to_all | solution.py:176
  26.0 1.0 %shard_map.87 = bf16[1024,128]{1,0:T(8,128)(2,1)} custom-call(bf16[512,128]{1,0:T(8,128)(2,1)S(1)} %bitcast.14), custom_call_target="tpu_custom_call" | custom-call | tf_op jit(solution)/shard_map/pallas_call | solution.py:222
  27.0 5.5 %all-to-all-start.1 = ((bf16[64,16,128]{2,1,0:T(8,128)(2,1)}), bf16[64,16,128]{2,1,0:T(8,128)(2,1)S(1)}, u32[]{:S(2)}, u32[]{:S(2)}) async-start(bf16[64,16,128]{2,1,0:T(8,128)(2,1)} %bitcast.4), calls=%async_computation.1 | async-start | bytes 524288 | tf_op jit(solution)/shard_map/all_to_all | solution.py:176
  32.5 0.5 collective-permute-done.1.two_ref
  33.0 0.1 collective-permute-start.2
  33.1 0.3 copy-done.5
  33.5 0.2 collective-permute-start
  34.3 0.0 copy-start.4
  34.3 0.7 copy-done.4
  35.0 0.1 collective-permute-done.one_ref
  35.0 10.0 %all-to-all-done.1 = bf16[64,16,128]{2,1,0:T(8,128)(2,1)S(1)} async-done(((bf16[64,16,128]{2,1,0:T(8,128)(2,1)}), bf16[64,16,128]{2,1,0:T(8,128)(2,1)S(1)}, u32[]{:S(2)}, u32[]{:S(2)}) %all-to-all-start.1) | async-done | bytes 262176 | tf_op jit(solution)/shard_map/all_to_all | solution.py:176
  45.0 1.4 %shard_map.89 = (bf16[64,2048]{1,0:T(8,128)(2,1)S(1)}, bf16[256,2048]{1,0:T(8,128)(2,1)S(1)}, f32[32,256]{1,0:T(8,128)S(1)}) custom-call(s32[1]{0:T(128)} %bitcast.place_ref, s32[1]{0:T(128)} %shard_map.86.order_ref, bf16[1024,128]{1,0:T(8,128)(2,1)S(1)} %bitcast.16, bf16[256,2048]{1,0:T(8,128)(2,1)S(1)} %copy-done.1, bf16[64,8192]{1,0:T(8,128)(2,1)S(1)} %copy-done, ...), custom_call_target="tpu_custom_call" | custom-call | tf_op jit(solution)/shard_map/pallas_call | solution.py:229
  46.4 0.0 copy-start.2
  46.4 0.1 collective-permute-start.5
  46.5 1.6 %collective-permute-start.4 = (f32[32,256]{1,0:T(8,128)S(1)}, f32[32,256]{1,0:T(8,128)S(1)}, u32[]{:S(2)}, u32[]{:S(2)}) collective-permute-start(f32[32,256]{1,0:T(8,128)S(1)} %get-tuple-element.21.own_ref), channel_id=1, source_target_pairs={{0,2},{1,3},{2,0},{3,1},{4,6},{5,7},{6,4},{7,5},{8,10},{9,11},{10,... | collective-permute-start | bytes 98312 | tf_op jit(solution)/shard_map/ppermute | solution.py:180
  48.0 1.8 %collective-permute-start.3 = (f32[32,256]{1,0:T(8,128)S(1)}, f32[32,256]{1,0:T(8,128)S(1)}, u32[]{:S(2)}, u32[]{:S(2)}) collective-permute-start(f32[32,256]{1,0:T(8,128)S(1)} %get-tuple-element.21.own_ref), channel_id=1, source_target_pairs={{0,1},{1,0},{2,3},{3,2},{4,5},{5,4},{6,7},{7,6},{8,9},{9,8},{10,11... | collective-permute-start | bytes 98312 | tf_op jit(solution)/shard_map/ppermute | solution.py:180
  49.8 1.5 %collective-permute-done.5.three_ref = f32[32,256]{1,0:T(8,128)S(1)} collective-permute-done((f32[32,256]{1,0:T(8,128)S(1)}, f32[32,256]{1,0:T(8,128)S(1)}, u32[]{:S(2)}, u32[]{:S(2)}) %collective-permute-start.5) | collective-permute-done | bytes 32800 | tf_op jit(solution)/shard_map/ppermute | solution.py:180
  51.3 0.7 collective-permute-done.4.two_ref
  52.0 0.0 collective-permute-done.3.one_ref
  52.0 0.4 shard_map.90
  52.4 18.9 %all_to_all.20 = bf16[64,16,128]{2,1,0:T(8,128)(2,1)S(1)} all-to-all(bf16[64,16,128]{2,1,0:T(8,128)(2,1)S(1)} %bitcast.19), channel_id=1, replica_groups=mesh['dp'=64,'tensor'=4] {'dp'}, dimensions={0} | all-to-all | bytes 524288 | tf_op jit(solution)/shard_map/all_to_all | solution.py:176
  71.3 1.0 %shard_map.92 = f32[256,128]{1,0:T(8,128)} custom-call(bf16[1024,128]{1,0:T(8,128)(2,1)S(1)} %bitcast.17, bf16[512,128]{1,0:T(8,128)(2,1)S(1)} %bitcast.15), custom_call_target="tpu_custom_call" | custom-call | tf_op jit(solution)/shard_map/pallas_call | solution.py:247
  72.3 4.9 %all-to-all-start.3 = ((f32[64,4,128]{2,1,0:T(4,128)}), f32[64,4,128]{2,1,0:T(4,128)S(1)}, u32[]{:S(2)}, u32[]{:S(2)}) async-start(f32[64,4,128]{2,1,0:T(4,128)} %bitcast.10), calls=%async_computation.3 | async-start | bytes 262144 | tf_op jit(solution)/shard_map/all_to_all | solution.py:176
  77.3 1.4 %shard_map.91 = bf16[256,2048]{1,0:T(8,128)(2,1)} custom-call(bf16[32,256]{1,0:T(8,128)(2,1)S(1)} %get-tuple-element.24.ranks_ref, bf16[64,2048]{1,0:T(8,128)(2,1)S(1)} %copy-done.3), custom_call_target="tpu_custom_call" | custom-call | flops 33554432 | bytes 2097152 | tf_op jit(solution)/shard_map/pallas_call | solution.py:241
  78.7 9.2 %all-to-all-done.3 = f32[64,4,128]{2,1,0:T(4,128)S(1)} async-done(((f32[64,4,128]{2,1,0:T(4,128)}), f32[64,4,128]{2,1,0:T(4,128)S(1)}, u32[]{:S(2)}, u32[]{:S(2)}) %all-to-all-start.3) | async-done | bytes 131104 | tf_op jit(solution)/shard_map/all_to_all | solution.py:176
  87.9 0.7 shard_map.93
  (10 shorter events, 0.0 us)
Async XLA Ops:
  2.2 23.8 %all-to-all-start = ((bf16[64,8,128]{2,1,0:T(8,128)(2,1)}), bf16[64,8,128]{2,1,0:T(8,128)(2,1)S(1)}, u32[]{:S(2)}, u32[]{:S(2)}) async-start(bf16[64,8,128]{2,1,0:T(8,128)(2,1)} %bitcast.20), calls=%async_computation | async-start | bytes 262144 | tf_op jit(solution)/shard_map/all_to_all | solution.py:176
  17.4 15.6 %collective-permute-start.1 = (bf16[128,2048]{1,0:T(8,128)(2,1)}, bf16[128,2048]{1,0:T(8,128)(2,1)S(1)}, u32[]{:S(2)}, u32[]{:S(2)}) collective-permute-start(bf16[128,2048]{1,0:T(8,128)(2,1)} %get-tuple-element.19), channel_id=1, source_target_pairs={{0,2},{1,3},{2,0},{3,1},{4,6},{5,7},{6,4},{7,5},{8,10},{9,11},{10,... | collective-permute-start | bytes 1572872 | tf_op jit(solution)/shard_map/ppermute | solution.py:180
  19.6 25.4 %copy-start.1 = (bf16[256,2048]{1,0:T(8,128)(2,1)S(1)}, bf16[256,2048]{1,0:T(8,128)(2,1)}, u32[]{:S(2)}) copy-start(bf16[256,2048]{1,0:T(8,128)(2,1)} %attn_ref.3) | copy-start | bytes 3145732
  20.2 24.8 %copy-start = (bf16[64,8192]{1,0:T(8,128)(2,1)S(1)}, bf16[64,8192]{1,0:T(8,128)(2,1)}, u32[]{:S(2)}) copy-start(bf16[64,8192]{1,0:T(8,128)(2,1)} %tokens_ref.1) | copy-start | bytes 3145732
  27.0 18.0 %all-to-all-start.1 = ((bf16[64,16,128]{2,1,0:T(8,128)(2,1)}), bf16[64,16,128]{2,1,0:T(8,128)(2,1)S(1)}, u32[]{:S(2)}, u32[]{:S(2)}) async-start(bf16[64,16,128]{2,1,0:T(8,128)(2,1)} %bitcast.4), calls=%async_computation.1 | async-start | bytes 524288 | tf_op jit(solution)/shard_map/all_to_all | solution.py:176
  32.5 1.0 %copy-start.5 = (bf16[64,2048]{1,0:T(8,128)(2,1)S(1)}, bf16[64,2048]{1,0:T(8,128)(2,1)}, u32[]{:S(2)}) copy-start(bf16[64,2048]{1,0:T(8,128)(2,1)} %get-tuple-element.18) | copy-start | bytes 786436
  33.0 1.9 %collective-permute-start.2 = (bf16[64,2048]{1,0:T(8,128)(2,1)S(1)}, bf16[64,2048]{1,0:T(8,128)(2,1)S(1)}, u32[]{:S(2)}, u32[]{:S(2)}) collective-permute-start(bf16[64,2048]{1,0:T(8,128)(2,1)S(1)} %slice.4), channel_id=1, source_target_pairs={{0,1},{1,0},{2,3},{3,2},{4,5},{5,4},{6,7},{7,6},{8,9},{9,8},{10,11... | collective-permute-start | bytes 786440 | tf_op jit(solution)/shard_map/ppermute | solution.py:180
  33.5 1.6 %collective-permute-start = (bf16[64,2048]{1,0:T(8,128)(2,1)S(1)}, bf16[64,2048]{1,0:T(8,128)(2,1)S(1)}, u32[]{:S(2)}, u32[]{:S(2)}) collective-permute-start(bf16[64,2048]{1,0:T(8,128)(2,1)S(1)} %copy-done.5), channel_id=1, source_target_pairs={{0,1},{1,0},{2,3},{3,2},{4,5},{5,4},{6,7},{7,6},{8,9},{9,8},{10,11... | collective-permute-start | bytes 786440 | tf_op jit(solution)/shard_map/ppermute | solution.py:180
  34.3 0.7 copy-start.4
  46.4 6.0 %copy-start.2 = (bf16[64,2048]{1,0:T(8,128)(2,1)}, bf16[64,2048]{1,0:T(8,128)(2,1)S(1)}, u32[]{:S(2)}) copy-start(bf16[64,2048]{1,0:T(8,128)(2,1)S(1)} %get-tuple-element.25.maps_ref) | copy-start | bytes 786436
  46.4 4.9 %collective-permute-start.5 = (f32[32,256]{1,0:T(8,128)S(1)}, f32[32,256]{1,0:T(8,128)S(1)}, u32[]{:S(2)}, u32[]{:S(2)}) collective-permute-start(f32[32,256]{1,0:T(8,128)S(1)} %get-tuple-element.21.own_ref), channel_id=1, source_target_pairs={{0,3},{1,2},{2,1},{3,0},{4,7},{5,6},{6,5},{7,4},{8,11},{9,10},{10,... | collective-permute-start | bytes 98312 | tf_op jit(solution)/shard_map/ppermute | solution.py:180
  46.5 5.5 %collective-permute-start.4 = (f32[32,256]{1,0:T(8,128)S(1)}, f32[32,256]{1,0:T(8,128)S(1)}, u32[]{:S(2)}, u32[]{:S(2)}) collective-permute-start(f32[32,256]{1,0:T(8,128)S(1)} %get-tuple-element.21.own_ref), channel_id=1, source_target_pairs={{0,2},{1,3},{2,0},{3,1},{4,6},{5,7},{6,4},{7,5},{8,10},{9,11},{10,... | collective-permute-start | bytes 98312 | tf_op jit(solution)/shard_map/ppermute | solution.py:180
  48.0 4.0 %collective-permute-start.3 = (f32[32,256]{1,0:T(8,128)S(1)}, f32[32,256]{1,0:T(8,128)S(1)}, u32[]{:S(2)}, u32[]{:S(2)}) collective-permute-start(f32[32,256]{1,0:T(8,128)S(1)} %get-tuple-element.21.own_ref), channel_id=1, source_target_pairs={{0,1},{1,0},{2,3},{3,2},{4,5},{5,4},{6,7},{7,6},{8,9},{9,8},{10,11... | collective-permute-start | bytes 98312 | tf_op jit(solution)/shard_map/ppermute | solution.py:180
  72.3 4.9 %copy-start.3 = (bf16[64,2048]{1,0:T(8,128)(2,1)S(1)}, bf16[64,2048]{1,0:T(8,128)(2,1)}, u32[]{:S(2)}) copy-start(bf16[64,2048]{1,0:T(8,128)(2,1)} %copy-done.2) | copy-start | bytes 786436
  72.3 15.5 %all-to-all-start.3 = ((f32[64,4,128]{2,1,0:T(4,128)}), f32[64,4,128]{2,1,0:T(4,128)S(1)}, u32[]{:S(2)}, u32[]{:S(2)}) async-start(f32[64,4,128]{2,1,0:T(4,128)} %bitcast.10), calls=%async_computation.3 | async-start | bytes 262144 | tf_op jit(solution)/shard_map/all_to_all | solution.py:176

commit v13 on v12

--- a/solution.py
+++ b/solution.py
@@ -77,9 +77,7 @@
     out_ref[...] = out_f[...].astype(BF16)
 
 
-def project(
-    place_ref, order_ref, picked_ref, attn_ref, tokens_ref, one_ref, two_ref, three_ref, maps_ref, grad_ref, part_ref
-):
+def project(place_ref, picked_ref, attn_ref, tokens_ref, one_ref, two_ref, three_ref, maps_ref, grad_ref, part_ref):
     me = place_ref[0]
     width = grad_ref.shape[1]
     own = tokens_ref[:, pl.ds(pl.multiple_of(me * width, width), width)]
@@ -123,7 +121,7 @@
             term_ref[c * 64 + q * 16:c * 64 + (q + 1) * 16, :] = pair.astype(BF16)
 
 
-def go_back(ranks_ref, maps_ref, back_ref):
+def go_back(order_ref, ranks_ref, maps_ref, back_ref):
     row = lax.broadcasted_iota(jnp.int32, (32, BLOCK), 0)
     over_first = (((0,), (0,)), ((), ()))
     for b in range(2):
@@ -229,8 +227,8 @@
     maps, grad, part = call(
         project,
         [((64, width), BF16), ((2 * BLOCK, width), BF16), ((32, 2 * BLOCK), F32)],
-        [SMEM, ANY] + [VMEM] * 6,
-    )(me, order, picked, attn, output_gradient, *pieces)
+        [SMEM] + [VMEM] * 6,
+    )(me, picked, attn, output_gradient, *pieces)
     parts = [part] + [from_peer(part, k) for k in (1, 2, 3)]
     ranks, terms = call(
         make_terms,
@@ -241,9 +239,9 @@
     (attention_gradient,) = call(
         go_back,
         [((2 * BLOCK, width), BF16)],
-        [VMEM] * 2,
+        [ANY] + [VMEM] * 2,
         cost=pl.CostEstimate(flops=2 * 32 * 256 * 2048, bytes_accessed=2 << 20, transcendentals=0),
-    )(ranks, maps)
+    )(order, ranks, maps)
     (sums,) = call(
         add_up,
         [((4 * PEERS, LANES), F32)],

time: 89 us -> 89.2 us (level)
  local copies, waits for them, and re-layouts: 1.04 us -> 2.68 us
  waiting for transfers between devices: 27.6 us -> 26.3 us
    unnamed x12, local copies, waits for them, and re-layouts: 1.02 us -> 2.66 us
    all_to_all x3, waiting for transfers between devices: 24.9 us -> 23.6 us  [swap(): return lax.all_to_all(chunks, 'dp', 0, 0, tiled=True).reshape(x.shape)]
where the time goes in v13:
time: 89.2 us; the launch traced here: 88.7 us
  starting transfers between devices  29.4 us (33%)
  waiting for transfers between devices  26.3 us (29%)
  blocking collectives  18.9 us (21%)
  Pallas kernels  9.93 us (11%)
  local copies, waits for them, and re-layouts  2.68 us (3%)
  between operations  1.42 us (2%)
    all_to_all x3, waiting for transfers between devices, swap(): return lax.all_to_all(chunks, 'dp', 0, 0, tiled=True).reshape(x.shape)  23.6 us
    all_to_all x3, starting transfers between devices, swap(): return lax.all_to_all(chunks, 'dp', 0, 0, tiled=True).reshape(x.shape)  23.5 us
    all_to_all x1, blocking collectives, swap(): return lax.all_to_all(chunks, 'dp', 0, 0, tiled=True).reshape(x.shape)  18.9 us
    ppermute x6, starting transfers between devices, from_peer(): return lax.ppermute(x, 'tensor', [(i, i ^ k) for i in range(4)])  5.92 us
    ppermute x6, waiting for transfers between devices, from_peer(): return lax.ppermute(x, 'tensor', [(i, i ^ k) for i in range(4)])  2.71 us
    unnamed x12, local copies, waits for them, and re-layouts  2.66 us
    pallas_call x1, Pallas kernels, per_device(): call(go_back, [((2 * BLOCK, width), BF16)], [ANY] + [VMEM] * 2, cost=pl.C...  2.08 us
    pallas_call x1, Pallas kernels, per_device(): call(cut_tokens, [((64, width), BF16), ((128, width), BF16)], [SMEM, ANY,...  2.02 us
  transfers between devices with their start and end apart: 9, of which 7 were waited for; matrix products, arithmetic and copies ran while one was open for 0% of the time, Pallas kernels for 6%

profile of v13, /device:TPU:2, one launch (start us, length us, event | category | flops | bytes accessed | tf_op | source)
XLA Modules:
  0.0 88.7 jit_solution(14764473558417081048)
XLA Ops:
  0.6 1.5 %shard_map.85.packed_hbm = bf16[512,128]{1,0:T(8,128)(2,1)} custom-call(bf16[8,2048]{1,0:T(8,128)(2,1)} %down_hbm.1, bf16[8,2048]{1,0:T(8,128)(2,1)} %up_hbm.1, s32[2,128]{1,0:T(2,128)} %bitcast.21), custom_call_target="tpu_custom_call" | custom-call | tf_op jit(solution)/shard_map/pallas_call | solution.py:185
  2.2 13.2 %all-to-all-start = ((bf16[64,8,128]{2,1,0:T(8,128)(2,1)}), bf16[64,8,128]{2,1,0:T(8,128)(2,1)S(1)}, u32[]{:S(2)}, u32[]{:S(2)}) async-start(bf16[64,8,128]{2,1,0:T(8,128)(2,1)} %bitcast.20), calls=%async_computation | async-start | bytes 262144 | tf_op jit(solution)/shard_map/all_to_all | solution.py:174
  15.4 2.0 %shard_map.88 = (bf16[64,2048]{1,0:T(8,128)(2,1)}, bf16[128,2048]{1,0:T(8,128)(2,1)}) custom-call(s32[1]{0:T(128)} %bitcast.3.place_ref, bf16[64,8192]{1,0:T(8,128)(2,1)} %tokens_ref.1, bf16[512,128]{1,0:T(8,128)(2,1)} %shard_map.85.packed_hbm), custom_call_target="tpu_custom_call" | custom-call | tf_op jit(solution)/shard_map/pallas_call | solution.py:199
  17.4 2.2 %collective-permute-start.1 = (bf16[128,2048]{1,0:T(8,128)(2,1)}, bf16[128,2048]{1,0:T(8,128)(2,1)S(1)}, u32[]{:S(2)}, u32[]{:S(2)}) collective-permute-start(bf16[128,2048]{1,0:T(8,128)(2,1)} %get-tuple-element.19), channel_id=1, source_target_pairs={{0,2},{1,3},{2,0},{3,1},{4,6},{5,7},{6,4},{7,5},{8,10},{9,11},{10,... | collective-permute-start | bytes 1572872 | tf_op jit(solution)/shard_map/ppermute | solution.py:178
  19.6 0.5 shard_map.86.order_ref
  20.2 0.0 copy-start
  20.2 5.8 %all-to-all-done = bf16[64,8,128]{2,1,0:T(8,128)(2,1)S(1)} async-done(((bf16[64,8,128]{2,1,0:T(8,128)(2,1)}), bf16[64,8,128]{2,1,0:T(8,128)(2,1)S(1)}, u32[]{:S(2)}, u32[]{:S(2)}) %all-to-all-start) | async-done | bytes 131104 | tf_op jit(solution)/shard_map/all_to_all | solution.py:174
  26.0 1.0 %shard_map.87 = bf16[1024,128]{1,0:T(8,128)(2,1)} custom-call(bf16[512,128]{1,0:T(8,128)(2,1)S(1)} %bitcast.14), custom_call_target="tpu_custom_call" | custom-call | tf_op jit(solution)/shard_map/pallas_call | solution.py:220
  27.0 5.5 %all-to-all-start.1 = ((bf16[64,16,128]{2,1,0:T(8,128)(2,1)}), bf16[64,16,128]{2,1,0:T(8,128)(2,1)S(1)}, u32[]{:S(2)}, u32[]{:S(2)}) async-start(bf16[64,16,128]{2,1,0:T(8,128)(2,1)} %bitcast.4), calls=%async_computation.1 | async-start | bytes 524288 | tf_op jit(solution)/shard_map/all_to_all | solution.py:174
  32.5 0.5 collective-permute-done.1.two_ref
  33.0 0.1 collective-permute-start.2
  33.1 0.3 copy-done.5
  33.5 0.2 collective-permute-start
  34.3 0.0 copy-start.4
  34.3 0.7 copy-done.4
  35.0 0.1 collective-permute-done.one_ref
  35.0 0.7 copy-done.2
  35.7 9.3 %all-to-all-done.1 = bf16[64,16,128]{2,1,0:T(8,128)(2,1)S(1)} async-done(((bf16[64,16,128]{2,1,0:T(8,128)(2,1)}), bf16[64,16,128]{2,1,0:T(8,128)(2,1)S(1)}, u32[]{:S(2)}, u32[]{:S(2)}) %all-to-all-start.1) | async-done | bytes 262176 | tf_op jit(solution)/shard_map/all_to_all | solution.py:174
  45.0 0.9 %copy-done.3 = bf16[64,2048]{1,0:T(8,128)(2,1)S(1)} copy-done((bf16[64,2048]{1,0:T(8,128)(2,1)S(1)}, bf16[64,2048]{1,0:T(8,128)(2,1)}, u32[]{:S(2)}) %copy-start.3) | copy-done | bytes 262168
  46.0 0.7 shard_map.89
  46.7 0.1 collective-permute-start.5
  46.8 1.6 %collective-permute-start.4 = (f32[32,256]{1,0:T(8,128)S(1)}, f32[32,256]{1,0:T(8,128)S(1)}, u32[]{:S(2)}, u32[]{:S(2)}) collective-permute-start(f32[32,256]{1,0:T(8,128)S(1)} %get-tuple-element.21.own_ref), channel_id=1, source_target_pairs={{0,2},{1,3},{2,0},{3,1},{4,6},{5,7},{6,4},{7,5},{8,10},{9,11},{10,... | collective-permute-start | bytes 98312 | tf_op jit(solution)/shard_map/ppermute | solution.py:178
  48.3 1.8 %collective-permute-start.3 = (f32[32,256]{1,0:T(8,128)S(1)}, f32[32,256]{1,0:T(8,128)S(1)}, u32[]{:S(2)}, u32[]{:S(2)}) collective-permute-start(f32[32,256]{1,0:T(8,128)S(1)} %get-tuple-element.21.own_ref), channel_id=1, source_target_pairs={{0,1},{1,0},{2,3},{3,2},{4,5},{5,4},{6,7},{7,6},{8,9},{9,8},{10,11... | collective-permute-start | bytes 98312 | tf_op jit(solution)/shard_map/ppermute | solution.py:178
  50.1 1.5 %collective-permute-done.5.three_ref = f32[32,256]{1,0:T(8,128)S(1)} collective-permute-done((f32[32,256]{1,0:T(8,128)S(1)}, f32[32,256]{1,0:T(8,128)S(1)}, u32[]{:S(2)}, u32[]{:S(2)}) %collective-permute-start.5) | collective-permute-done | bytes 32800 | tf_op jit(solution)/shard_map/ppermute | solution.py:178
  51.6 0.7 collective-permute-done.4.two_ref
  52.3 0.4 shard_map.90
  52.7 18.9 %all_to_all.20 = bf16[64,16,128]{2,1,0:T(8,128)(2,1)S(1)} all-to-all(bf16[64,16,128]{2,1,0:T(8,128)(2,1)S(1)} %bitcast.19), channel_id=1, replica_groups=mesh['dp'=64,'tensor'=4] {'dp'}, dimensions={0} | all-to-all | bytes 524288 | tf_op jit(solution)/shard_map/all_to_all | solution.py:174
  71.6 1.0 %shard_map.92 = f32[256,128]{1,0:T(8,128)} custom-call(bf16[1024,128]{1,0:T(8,128)(2,1)S(1)} %bitcast.17, bf16[512,128]{1,0:T(8,128)(2,1)S(1)} %bitcast.15), custom_call_target="tpu_custom_call" | custom-call | tf_op jit(solution)/shard_map/pallas_call | solution.py:245
  72.6 4.8 %all-to-all-start.3 = ((f32[64,4,128]{2,1,0:T(4,128)}), f32[64,4,128]{2,1,0:T(4,128)S(1)}, u32[]{:S(2)}, u32[]{:S(2)}) async-start(f32[64,4,128]{2,1,0:T(4,128)} %bitcast.10), calls=%async_computation.3 | async-start | bytes 262144 | tf_op jit(solution)/shard_map/all_to_all | solution.py:174
  77.4 2.1 %shard_map.91 = bf16[256,2048]{1,0:T(8,128)(2,1)} custom-call(s32[1]{0:T(128)} %shard_map.86.order_ref, bf16[32,256]{1,0:T(8,128)(2,1)S(1)} %get-tuple-element.24.ranks_ref, bf16[64,2048]{1,0:T(8,128)(2,1)S(1)} %get-tuple-element.25.maps_ref), custom_call_target="tpu_custom_call" | custom-call | flops 33554432 | bytes 2097152 | tf_op jit(solution)/shard_map/pallas_call | solution.py:239
  79.5 8.5 %all-to-all-done.3 = f32[64,4,128]{2,1,0:T(4,128)S(1)} async-done(((f32[64,4,128]{2,1,0:T(4,128)}), f32[64,4,128]{2,1,0:T(4,128)S(1)}, u32[]{:S(2)}, u32[]{:S(2)}) %all-to-all-start.3) | async-done | bytes 131104 | tf_op jit(solution)/shard_map/all_to_all | solution.py:174
  88.0 0.7 shard_map.93
  (10 shorter events, 0.0 us)
Async XLA Ops:
  2.2 23.8 %all-to-all-start = ((bf16[64,8,128]{2,1,0:T(8,128)(2,1)}), bf16[64,8,128]{2,1,0:T(8,128)(2,1)S(1)}, u32[]{:S(2)}, u32[]{:S(2)}) async-start(bf16[64,8,128]{2,1,0:T(8,128)(2,1)} %bitcast.20), calls=%async_computation | async-start | bytes 262144 | tf_op jit(solution)/shard_map/all_to_all | solution.py:174
  17.4 15.6 %collective-permute-start.1 = (bf16[128,2048]{1,0:T(8,128)(2,1)}, bf16[128,2048]{1,0:T(8,128)(2,1)S(1)}, u32[]{:S(2)}, u32[]{:S(2)}) collective-permute-start(bf16[128,2048]{1,0:T(8,128)(2,1)} %get-tuple-element.19), channel_id=1, source_target_pairs={{0,2},{1,3},{2,0},{3,1},{4,6},{5,7},{6,4},{7,5},{8,10},{9,11},{10,... | collective-permute-start | bytes 1572872 | tf_op jit(solution)/shard_map/ppermute | solution.py:178
  19.6 25.4 %copy-start.1 = (bf16[256,2048]{1,0:T(8,128)(2,1)S(1)}, bf16[256,2048]{1,0:T(8,128)(2,1)}, u32[]{:S(2)}) copy-start(bf16[256,2048]{1,0:T(8,128)(2,1)} %attn_ref.3) | copy-start | bytes 3145732
  20.2 24.8 %copy-start = (bf16[64,8192]{1,0:T(8,128)(2,1)S(1)}, bf16[64,8192]{1,0:T(8,128)(2,1)}, u32[]{:S(2)}) copy-start(bf16[64,8192]{1,0:T(8,128)(2,1)} %tokens_ref.1) | copy-start | bytes 3145732
  27.0 18.0 %all-to-all-start.1 = ((bf16[64,16,128]{2,1,0:T(8,128)(2,1)}), bf16[64,16,128]{2,1,0:T(8,128)(2,1)S(1)}, u32[]{:S(2)}, u32[]{:S(2)}) async-start(bf16[64,16,128]{2,1,0:T(8,128)(2,1)} %bitcast.4), calls=%async_computation.1 | async-start | bytes 524288 | tf_op jit(solution)/shard_map/all_to_all | solution.py:174
  32.5 1.0 %copy-start.5 = (bf16[64,2048]{1,0:T(8,128)(2,1)S(1)}, bf16[64,2048]{1,0:T(8,128)(2,1)}, u32[]{:S(2)}) copy-start(bf16[64,2048]{1,0:T(8,128)(2,1)} %get-tuple-element.18) | copy-start | bytes 786436
  33.0 1.9 %collective-permute-start.2 = (bf16[64,2048]{1,0:T(8,128)(2,1)S(1)}, bf16[64,2048]{1,0:T(8,128)(2,1)S(1)}, u32[]{:S(2)}, u32[]{:S(2)}) collective-permute-start(bf16[64,2048]{1,0:T(8,128)(2,1)S(1)} %slice.4), channel_id=1, source_target_pairs={{0,1},{1,0},{2,3},{3,2},{4,5},{5,4},{6,7},{7,6},{8,9},{9,8},{10,11... | collective-permute-start | bytes 786440 | tf_op jit(solution)/shard_map/ppermute | solution.py:178
  33.5 1.6 %collective-permute-start = (bf16[64,2048]{1,0:T(8,128)(2,1)S(1)}, bf16[64,2048]{1,0:T(8,128)(2,1)S(1)}, u32[]{:S(2)}, u32[]{:S(2)}) collective-permute-start(bf16[64,2048]{1,0:T(8,128)(2,1)S(1)} %copy-done.5), channel_id=1, source_target_pairs={{0,1},{1,0},{2,3},{3,2},{4,5},{5,4},{6,7},{7,6},{8,9},{9,8},{10,11... | collective-permute-start | bytes 786440 | tf_op jit(solution)/shard_map/ppermute | solution.py:178
  34.3 0.7 copy-start.4
  35.0 0.7 copy-start.2
  45.0 1.0 %copy-start.3 = (bf16[64,2048]{1,0:T(8,128)(2,1)S(1)}, bf16[64,2048]{1,0:T(8,128)(2,1)}, u32[]{:S(2)}) copy-start(bf16[64,2048]{1,0:T(8,128)(2,1)} %copy-done.2) | copy-start | bytes 786436
  46.7 4.9 %collective-permute-start.5 = (f32[32,256]{1,0:T(8,128)S(1)}, f32[32,256]{1,0:T(8,128)S(1)}, u32[]{:S(2)}, u32[]{:S(2)}) collective-permute-start(f32[32,256]{1,0:T(8,128)S(1)} %get-tuple-element.21.own_ref), channel_id=1, source_target_pairs={{0,3},{1,2},{2,1},{3,0},{4,7},{5,6},{6,5},{7,4},{8,11},{9,10},{10,... | collective-permute-start | bytes 98312 | tf_op jit(solution)/shard_map/ppermute | solution.py:178
  46.8 5.5 %collective-permute-start.4 = (f32[32,256]{1,0:T(8,128)S(1)}, f32[32,256]{1,0:T(8,128)S(1)}, u32[]{:S(2)}, u32[]{:S(2)}) collective-permute-start(f32[32,256]{1,0:T(8,128)S(1)} %get-tuple-element.21.own_ref), channel_id=1, source_target_pairs={{0,2},{1,3},{2,0},{3,1},{4,6},{5,7},{6,4},{7,5},{8,10},{9,11},{10,... | collective-permute-start | bytes 98312 | tf_op jit(solution)/shard_map/ppermute | solution.py:178
  48.3 4.0 %collective-permute-start.3 = (f32[32,256]{1,0:T(8,128)S(1)}, f32[32,256]{1,0:T(8,128)S(1)}, u32[]{:S(2)}, u32[]{:S(2)}) collective-permute-start(f32[32,256]{1,0:T(8,128)S(1)} %get-tuple-element.21.own_ref), channel_id=1, source_target_pairs={{0,1},{1,0},{2,3},{3,2},{4,5},{5,4},{6,7},{7,6},{8,9},{9,8},{10,11... | collective-permute-start | bytes 98312 | tf_op jit(solution)/shard_map/ppermute | solution.py:178
  72.6 15.4 %all-to-all-start.3 = ((f32[64,4,128]{2,1,0:T(4,128)}), f32[64,4,128]{2,1,0:T(4,128)S(1)}, u32[]{:S(2)}, u32[]{:S(2)}) async-start(f32[64,4,128]{2,1,0:T(4,128)} %bitcast.10), calls=%async_computation.3 | async-start | bytes 262144 | tf_op jit(solution)/shard_map/all_to_all | solution.py:174

commit v14 on v12

--- a/solution.py
+++ b/solution.py
@@ -60,7 +60,7 @@
 
 
 def copy_place(place_ref, out_ref):
-    out_ref[0] = place_ref[0]
+    out_ref[...] = jnp.full(out_ref.shape, place_ref[0], jnp.int32)
 
 
 def pick_rows(in_ref, out_ref, in_f, out_f):
@@ -207,9 +207,9 @@
     )(me, output_gradient, packed)
     order = pl.pallas_call(
         copy_place,
-        out_shape=jax.ShapeDtypeStruct((1,), jnp.int32),
+        out_shape=jax.ShapeDtypeStruct((8, LANES), jnp.int32),
         in_specs=[SMEM],
-        out_specs=SMEM,
+        out_specs=VMEM,
         cost_estimate=pl.CostEstimate(flops=10 ** 10, bytes_accessed=8, transcendentals=0),
     )(me)
     live = (adapter_of_row >= 0) & (jnp.arange(2 * BLOCK, dtype=jnp.int32) < lengths[0])
@@ -229,7 +229,7 @@
     maps, grad, part = call(
         project,
         [((64, width), BF16), ((2 * BLOCK, width), BF16), ((32, 2 * BLOCK), F32)],
-        [SMEM, ANY] + [VMEM] * 6,
+        [SMEM] + [VMEM] * 7,
     )(me, order, picked, attn, output_gradient, *pieces)
     parts = [part] + [from_peer(part, k) for k in (1, 2, 3)]
     ranks, terms = call(

time: 89 us -> 88.4 us (level)
  transfers between devices with their start and end apart: 9 -> 9, of which waited for: 7 -> 8; matrix products, arithmetic and copies ran while one was open for 0% -> 0% of each run, Pallas kernels for 6% -> 6%
where the time goes in v14:
time: 88.4 us; the launch traced here: 87.9 us
  starting transfers between devices  29.6 us (33%)
  waiting for transfers between devices  28.2 us (32%)
  blocking collectives  18.9 us (21%)
  Pallas kernels  9.39 us (11%)
  between operations  1.44 us (2%)
    all_to_all x3, waiting for transfers between devices, swap(): return lax.all_to_all(chunks, 'dp', 0, 0, tiled=True).reshape(x.shape)  24.9 us
    all_to_all x3, starting transfers between devices, swap(): return lax.all_to_all(chunks, 'dp', 0, 0, tiled=True).reshape(x.shape)  23.7 us
    all_to_all x1, blocking collectives, swap(): return lax.all_to_all(chunks, 'dp', 0, 0, tiled=True).reshape(x.shape)  18.9 us
    ppermute x6, starting transfers between devices, from_peer(): return lax.ppermute(x, 'tensor', [(i, i ^ k) for i in range(4)])  5.86 us
    ppermute x6, waiting for transfers between devices, from_peer(): return lax.ppermute(x, 'tensor', [(i, i ^ k) for i in range(4)])  3.33 us
    pallas_call x1, Pallas kernels, per_device(): call(cut_tokens, [((64, width), BF16), ((128, width), BF16)], [SMEM, ANY,...  2.02 us
  transfers between devices with their start and end apart: 9, of which 8 were waited for; matrix products, arithmetic and copies ran while one was open for 0% of the time, Pallas kernels for 6%

profile of v14, /device:TPU:2, one launch (start us, length us, event | category | flops | bytes accessed | tf_op | source)
XLA Modules:
  0.0 87.9 jit_solution(3722726343072572603)
XLA Ops:
  0.6 1.5 %shard_map.85.packed_hbm = bf16[512,128]{1,0:T(8,128)(2,1)} custom-call(bf16[8,2048]{1,0:T(8,128)(2,1)} %down_hbm.1, bf16[8,2048]{1,0:T(8,128)(2,1)} %up_hbm.1, s32[2,128]{1,0:T(2,128)} %bitcast.21), custom_call_target="tpu_custom_call" | custom-call | tf_op jit(solution)/shard_map/pallas_call | solution.py:187
  2.1 13.2 %all-to-all-start = ((bf16[64,8,128]{2,1,0:T(8,128)(2,1)}), bf16[64,8,128]{2,1,0:T(8,128)(2,1)S(1)}, u32[]{:S(2)}, u32[]{:S(2)}) async-start(bf16[64,8,128]{2,1,0:T(8,128)(2,1)} %bitcast.20), calls=%async_computation | async-start | bytes 262144 | tf_op jit(solution)/shard_map/all_to_all | solution.py:176
  15.4 2.0 %shard_map.88 = (bf16[64,2048]{1,0:T(8,128)(2,1)}, bf16[128,2048]{1,0:T(8,128)(2,1)}) custom-call(s32[1]{0:T(128)} %bitcast.place_ref, bf16[64,8192]{1,0:T(8,128)(2,1)} %tokens_ref.1, bf16[512,128]{1,0:T(8,128)(2,1)} %shard_map.85.packed_hbm), custom_call_target="tpu_custom_call" | custom-call | tf_op jit(solution)/shard_map/pallas_call | solution.py:201
  17.4 2.2 %collective-permute-start.1 = (bf16[128,2048]{1,0:T(8,128)(2,1)}, bf16[128,2048]{1,0:T(8,128)(2,1)S(1)}, u32[]{:S(2)}, u32[]{:S(2)}) collective-permute-start(bf16[128,2048]{1,0:T(8,128)(2,1)} %get-tuple-element.19), channel_id=1, source_target_pairs={{0,2},{1,3},{2,0},{3,1},{4,6},{5,7},{6,4},{7,5},{8,10},{9,11},{10,... | collective-permute-start | bytes 1572872 | tf_op jit(solution)/shard_map/ppermute | solution.py:180
  19.6 0.6 shard_map.86.order_ref
  20.2 5.8 %all-to-all-done = bf16[64,8,128]{2,1,0:T(8,128)(2,1)S(1)} async-done(((bf16[64,8,128]{2,1,0:T(8,128)(2,1)}), bf16[64,8,128]{2,1,0:T(8,128)(2,1)S(1)}, u32[]{:S(2)}, u32[]{:S(2)}) %all-to-all-start) | async-done | bytes 131104 | tf_op jit(solution)/shard_map/all_to_all | solution.py:176
  26.0 1.0 %shard_map.87 = bf16[1024,128]{1,0:T(8,128)(2,1)} custom-call(bf16[512,128]{1,0:T(8,128)(2,1)S(1)} %bitcast.14), custom_call_target="tpu_custom_call" | custom-call | tf_op jit(solution)/shard_map/pallas_call | solution.py:222
  27.0 5.5 %all-to-all-start.1 = ((bf16[64,16,128]{2,1,0:T(8,128)(2,1)}), bf16[64,16,128]{2,1,0:T(8,128)(2,1)S(1)}, u32[]{:S(2)}, u32[]{:S(2)}) async-start(bf16[64,16,128]{2,1,0:T(8,128)(2,1)} %bitcast.4), calls=%async_computation.1 | async-start | bytes 524288 | tf_op jit(solution)/shard_map/all_to_all | solution.py:176
  32.6 0.0 copy-start.6
  32.6 0.4 collective-permute-done.1.two_ref
  33.0 0.1 collective-permute-start.2
  33.1 0.4 copy-done.6
  33.5 0.1 collective-permute-start
  34.3 0.0 copy-done.5
  34.3 0.3 collective-permute-done.2.three_ref
  34.7 0.4 collective-permute-done.one_ref
  35.1 10.0 %all-to-all-done.1 = bf16[64,16,128]{2,1,0:T(8,128)(2,1)S(1)} async-done(((bf16[64,16,128]{2,1,0:T(8,128)(2,1)}), bf16[64,16,128]{2,1,0:T(8,128)(2,1)S(1)}, u32[]{:S(2)}, u32[]{:S(2)}) %all-to-all-start.1) | async-done | bytes 262176 | tf_op jit(solution)/shard_map/all_to_all | solution.py:176
  45.1 0.7 shard_map.89
  45.8 0.0 copy-start.2
  45.8 0.1 collective-permute-start.5
  45.9 1.5 %collective-permute-start.4 = (f32[32,256]{1,0:T(8,128)S(1)}, f32[32,256]{1,0:T(8,128)S(1)}, u32[]{:S(2)}, u32[]{:S(2)}) collective-permute-start(f32[32,256]{1,0:T(8,128)S(1)} %get-tuple-element.21.own_ref), channel_id=1, source_target_pairs={{0,2},{1,3},{2,0},{3,1},{4,6},{5,7},{6,4},{7,5},{8,10},{9,11},{10,... | collective-permute-start | bytes 98312 | tf_op jit(solution)/shard_map/ppermute | solution.py:180
  47.4 1.8 %collective-permute-start.3 = (f32[32,256]{1,0:T(8,128)S(1)}, f32[32,256]{1,0:T(8,128)S(1)}, u32[]{:S(2)}, u32[]{:S(2)}) collective-permute-start(f32[32,256]{1,0:T(8,128)S(1)} %get-tuple-element.21.own_ref), channel_id=1, source_target_pairs={{0,1},{1,0},{2,3},{3,2},{4,5},{5,4},{6,7},{7,6},{8,9},{9,8},{10,11... | collective-permute-start | bytes 98312 | tf_op jit(solution)/shard_map/ppermute | solution.py:180
  49.3 1.5 %collective-permute-done.5.three_ref = f32[32,256]{1,0:T(8,128)S(1)} collective-permute-done((f32[32,256]{1,0:T(8,128)S(1)}, f32[32,256]{1,0:T(8,128)S(1)}, u32[]{:S(2)}, u32[]{:S(2)}) %collective-permute-start.5) | collective-permute-done | bytes 32800 | tf_op jit(solution)/shard_map/ppermute | solution.py:180
  50.7 0.7 collective-permute-done.4.two_ref
  51.4 0.0 collective-permute-done.3.one_ref
  51.4 0.4 shard_map.90
  51.9 18.9 %all_to_all.20 = bf16[64,16,128]{2,1,0:T(8,128)(2,1)S(1)} all-to-all(bf16[64,16,128]{2,1,0:T(8,128)(2,1)S(1)} %bitcast.19), channel_id=1, replica_groups=mesh['dp'=64,'tensor'=4] {'dp'}, dimensions={0} | all-to-all | bytes 524288 | tf_op jit(solution)/shard_map/all_to_all | solution.py:176
  70.7 1.0 %shard_map.92 = f32[256,128]{1,0:T(8,128)} custom-call(bf16[1024,128]{1,0:T(8,128)(2,1)S(1)} %bitcast.17, bf16[512,128]{1,0:T(8,128)(2,1)S(1)} %bitcast.15), custom_call_target="tpu_custom_call" | custom-call | tf_op jit(solution)/shard_map/pallas_call | solution.py:247
  71.7 4.9 %all-to-all-start.3 = ((f32[64,4,128]{2,1,0:T(4,128)}), f32[64,4,128]{2,1,0:T(4,128)S(1)}, u32[]{:S(2)}, u32[]{:S(2)}) async-start(f32[64,4,128]{2,1,0:T(4,128)} %bitcast.10), calls=%async_computation.3 | async-start | bytes 262144 | tf_op jit(solution)/shard_map/all_to_all | solution.py:176
  76.7 1.4 %shard_map.91 = bf16[256,2048]{1,0:T(8,128)(2,1)} custom-call(bf16[32,256]{1,0:T(8,128)(2,1)S(1)} %get-tuple-element.24.ranks_ref, bf16[64,2048]{1,0:T(8,128)(2,1)S(1)} %copy-done.3), custom_call_target="tpu_custom_call" | custom-call | flops 33554432 | bytes 2097152 | tf_op jit(solution)/shard_map/pallas_call | solution.py:241
  78.1 9.2 %all-to-all-done.3 = f32[64,4,128]{2,1,0:T(4,128)S(1)} async-done(((f32[64,4,128]{2,1,0:T(4,128)}), f32[64,4,128]{2,1,0:T(4,128)S(1)}, u32[]{:S(2)}, u32[]{:S(2)}) %all-to-all-start.3) | async-done | bytes 131104 | tf_op jit(solution)/shard_map/all_to_all | solution.py:176
  87.3 0.7 shard_map.93
  (12 shorter events, 0.0 us)
Async XLA Ops:
  2.1 23.8 %all-to-all-start = ((bf16[64,8,128]{2,1,0:T(8,128)(2,1)}), bf16[64,8,128]{2,1,0:T(8,128)(2,1)S(1)}, u32[]{:S(2)}, u32[]{:S(2)}) async-start(bf16[64,8,128]{2,1,0:T(8,128)(2,1)} %bitcast.20), calls=%async_computation | async-start | bytes 262144 | tf_op jit(solution)/shard_map/all_to_all | solution.py:176
  17.4 15.6 %collective-permute-start.1 = (bf16[128,2048]{1,0:T(8,128)(2,1)}, bf16[128,2048]{1,0:T(8,128)(2,1)S(1)}, u32[]{:S(2)}, u32[]{:S(2)}) collective-permute-start(bf16[128,2048]{1,0:T(8,128)(2,1)} %get-tuple-element.19), channel_id=1, source_target_pairs={{0,2},{1,3},{2,0},{3,1},{4,6},{5,7},{6,4},{7,5},{8,10},{9,11},{10,... | collective-permute-start | bytes 1572872 | tf_op jit(solution)/shard_map/ppermute | solution.py:180
  19.6 25.4 %copy-start.1 = (bf16[256,2048]{1,0:T(8,128)(2,1)S(1)}, bf16[256,2048]{1,0:T(8,128)(2,1)}, u32[]{:S(2)}) copy-start(bf16[256,2048]{1,0:T(8,128)(2,1)} %attn_ref.3) | copy-start | bytes 3145732
  20.2 24.8 %copy-start = (bf16[64,8192]{1,0:T(8,128)(2,1)S(1)}, bf16[64,8192]{1,0:T(8,128)(2,1)}, u32[]{:S(2)}) copy-start(bf16[64,8192]{1,0:T(8,128)(2,1)} %tokens_ref.1) | copy-start | bytes 3145732
  27.0 18.0 %all-to-all-start.1 = ((bf16[64,16,128]{2,1,0:T(8,128)(2,1)}), bf16[64,16,128]{2,1,0:T(8,128)(2,1)S(1)}, u32[]{:S(2)}, u32[]{:S(2)}) async-start(bf16[64,16,128]{2,1,0:T(8,128)(2,1)} %bitcast.4), calls=%async_computation.1 | async-start | bytes 524288 | tf_op jit(solution)/shard_map/all_to_all | solution.py:176
  32.6 1.0 %copy-start.6 = (bf16[64,2048]{1,0:T(8,128)(2,1)S(1)}, bf16[64,2048]{1,0:T(8,128)(2,1)}, u32[]{:S(2)}) copy-start(bf16[64,2048]{1,0:T(8,128)(2,1)} %get-tuple-element.18) | copy-start | bytes 786436
  33.0 1.3 %copy-start.5 = (s32[256]{0:T(256)S(1)}, s32[256]{0:T(256)}, u32[]{:S(2)}) copy-start(s32[256]{0:T(256)} %param.10) | copy-start | bytes 3076
  33.0 1.6 %collective-permute-start.2 = (bf16[64,2048]{1,0:T(8,128)(2,1)S(1)}, bf16[64,2048]{1,0:T(8,128)(2,1)S(1)}, u32[]{:S(2)}, u32[]{:S(2)}) collective-permute-start(bf16[64,2048]{1,0:T(8,128)(2,1)S(1)} %slice.4), channel_id=1, source_target_pairs={{0,1},{1,0},{2,3},{3,2},{4,5},{5,4},{6,7},{7,6},{8,9},{9,8},{10,11... | collective-permute-start | bytes 786440 | tf_op jit(solution)/shard_map/ppermute | solution.py:180
  33.5 11.5 %copy-start.4 = (s32[8,128]{1,0:T(8,128)S(1)}, s32[8,128]{1,0:T(8,128)}, u32[]{:S(2)}) copy-start(s32[8,128]{1,0:T(8,128)} %shard_map.86.order_ref) | copy-start | bytes 12292
  33.5 1.5 %collective-permute-start = (bf16[64,2048]{1,0:T(8,128)(2,1)S(1)}, bf16[64,2048]{1,0:T(8,128)(2,1)S(1)}, u32[]{:S(2)}, u32[]{:S(2)}) collective-permute-start(bf16[64,2048]{1,0:T(8,128)(2,1)S(1)} %copy-done.6), channel_id=1, source_target_pairs={{0,1},{1,0},{2,3},{3,2},{4,5},{5,4},{6,7},{7,6},{8,9},{9,8},{10,11... | collective-permute-start | bytes 786440 | tf_op jit(solution)/shard_map/ppermute | solution.py:180
  45.8 6.0 %copy-start.2 = (bf16[64,2048]{1,0:T(8,128)(2,1)}, bf16[64,2048]{1,0:T(8,128)(2,1)S(1)}, u32[]{:S(2)}) copy-start(bf16[64,2048]{1,0:T(8,128)(2,1)S(1)} %get-tuple-element.25.maps_ref) | copy-start | bytes 786436
  45.8 4.9 %collective-permute-start.5 = (f32[32,256]{1,0:T(8,128)S(1)}, f32[32,256]{1,0:T(8,128)S(1)}, u32[]{:S(2)}, u32[]{:S(2)}) collective-permute-start(f32[32,256]{1,0:T(8,128)S(1)} %get-tuple-element.21.own_ref), channel_id=1, source_target_pairs={{0,3},{1,2},{2,1},{3,0},{4,7},{5,6},{6,5},{7,4},{8,11},{9,10},{10,... | collective-permute-start | bytes 98312 | tf_op jit(solution)/shard_map/ppermute | solution.py:180
  45.9 5.5 %collective-permute-start.4 = (f32[32,256]{1,0:T(8,128)S(1)}, f32[32,256]{1,0:T(8,128)S(1)}, u32[]{:S(2)}, u32[]{:S(2)}) collective-permute-start(f32[32,256]{1,0:T(8,128)S(1)} %get-tuple-element.21.own_ref), channel_id=1, source_target_pairs={{0,2},{1,3},{2,0},{3,1},{4,6},{5,7},{6,4},{7,5},{8,10},{9,11},{10,... | collective-permute-start | bytes 98312 | tf_op jit(solution)/shard_map/ppermute | solution.py:180
  47.4 4.0 %collective-permute-start.3 = (f32[32,256]{1,0:T(8,128)S(1)}, f32[32,256]{1,0:T(8,128)S(1)}, u32[]{:S(2)}, u32[]{:S(2)}) collective-permute-start(f32[32,256]{1,0:T(8,128)S(1)} %get-tuple-element.21.own_ref), channel_id=1, source_target_pairs={{0,1},{1,0},{2,3},{3,2},{4,5},{5,4},{6,7},{7,6},{8,9},{9,8},{10,11... | collective-permute-start | bytes 98312 | tf_op jit(solution)/shard_map/ppermute | solution.py:180
  71.7 4.9 %copy-start.3 = (bf16[64,2048]{1,0:T(8,128)(2,1)S(1)}, bf16[64,2048]{1,0:T(8,128)(2,1)}, u32[]{:S(2)}) copy-start(bf16[64,2048]{1,0:T(8,128)(2,1)} %copy-done.2) | copy-start | bytes 786436
  71.7 15.5 %all-to-all-start.3 = ((f32[64,4,128]{2,1,0:T(4,128)}), f32[64,4,128]{2,1,0:T(4,128)S(1)}, u32[]{:S(2)}, u32[]{:S(2)}) async-start(f32[64,4,128]{2,1,0:T(4,128)} %bitcast.10), calls=%async_computation.3 | async-start | bytes 262144 | tf_op jit(solution)/shard_map/all_to_all | solution.py:176

commit v15 on v14

--- a/solution.py
+++ b/solution.py
@@ -63,7 +63,7 @@
     out_ref[...] = jnp.full(out_ref.shape, place_ref[0], jnp.int32)
 
 
-def pick_rows(in_ref, out_ref, in_f, out_f):
+def pick_rows(in_ref, out_hbm, in_f, out_f, out_ref, sems):
     in_f[...] = in_ref[...].astype(F32)
     table = jnp.concatenate([in_f[rows_of(k, PEERS, 8), :] for k in range(4)], axis=1).astype(BF16)
     lane = lax.broadcasted_iota(jnp.int32, (PEERS, LANES), 1)
@@ -74,7 +74,14 @@
             picked = jnp.dot(chosen, table, preferred_element_type=F32)
             for k in range(4):
                 out_f[rows_of(b * 8 + h * 4 + k, PEERS, 16), :] = picked[:, k * LANES:(k + 1) * LANES]
-    out_ref[...] = out_f[...].astype(BF16)
+    copies = []
+    for n in range(4):
+        part = slice(n * 256, (n + 1) * 256)
+        out_ref[part, :] = out_f[part, :].astype(BF16)
+        copies.append(pltpu.make_async_copy(out_ref.at[pl.ds(n * 256, 256), :], out_hbm.at[pl.ds(n * 256, 256), :], sems.at[n]))
+        copies[-1].start()
+    for copy in copies:
+        copy.wait()
 
 
 def project(
@@ -159,12 +166,12 @@
             map_ref[:, c * LANES:(c + 1) * LANES] = rows_f[c * 8:(c + 1) * 8, :]
 
 
-def call(kernel, outs, specs, scratch=(), cost=None, limit=40 * MIB):
+def call(kernel, outs, specs, scratch=(), cost=None, limit=40 * MIB, places=None):
     return pl.pallas_call(
         kernel,
         out_shape=[jax.ShapeDtypeStruct(shape, dtype) for shape, dtype in outs],
         in_specs=specs,
-        out_specs=[VMEM] * len(outs),
+        out_specs=places or [VMEM] * len(outs),
         scratch_shapes=scratch,
         compiler_params=pltpu.CompilerParams(vmem_limit_bytes=limit),
         cost_estimate=cost,
@@ -223,7 +230,13 @@
         pick_rows,
         [((16 * PEERS, LANES), BF16)],
         [VMEM],
-        [pltpu.VMEM((8 * PEERS, LANES), F32), pltpu.VMEM((16 * PEERS, LANES), F32)],
+        [
+            pltpu.VMEM((8 * PEERS, LANES), F32),
+            pltpu.VMEM((16 * PEERS, LANES), F32),
+            pltpu.VMEM((16 * PEERS, LANES), BF16),
+            pltpu.SemaphoreType.DMA((4,)),
+        ],
+        places=[ANY],
     )(tables)
     picked = swap(picked)
     maps, grad, part = call(

time: 88.4 us -> 88.4 us (level)
  no operation moved by 1% of the time
where the time goes in v15:
time: 88.4 us; the launch traced here: 88 us
  starting transfers between devices  29.5 us (33%)
  waiting for transfers between devices  28.2 us (32%)
  blocking collectives  18.9 us (21%)
  Pallas kernels  9.39 us (11%)
  between operations  1.45 us (2%)
    all_to_all x3, waiting for transfers between devices, swap(): return lax.all_to_all(chunks, 'dp', 0, 0, tiled=True).reshape(x.shape)  24.9 us
    all_to_all x3, starting transfers between devices, swap(): return lax.all_to_all(chunks, 'dp', 0, 0, tiled=True).reshape(x.shape)  23.7 us
    all_to_all x1, blocking collectives, swap(): return lax.all_to_all(chunks, 'dp', 0, 0, tiled=True).reshape(x.shape)  18.9 us
    ppermute x6, starting transfers between devices, from_peer(): return lax.ppermute(x, 'tensor', [(i, i ^ k) for i in range(4)])  5.84 us
    ppermute x6, waiting for transfers between devices, from_peer(): return lax.ppermute(x, 'tensor', [(i, i ^ k) for i in range(4)])  3.33 us
    pallas_call x1, Pallas kernels, per_device(): call(cut_tokens, [((64, width), BF16), ((128, width), BF16)], [SMEM, ANY,...  2.02 us
  transfers between devices with their start and end apart: 9, of which 8 were waited for; matrix products, arithmetic and copies ran while one was open for 0% of the time, Pallas kernels for 6%

profile of v15, /device:TPU:2, one launch (start us, length us, event | category | flops | bytes accessed | tf_op | source)
XLA Modules:
  0.0 88.0 jit_solution(2483376932764893591)
XLA Ops:
  0.6 1.5 %shard_map.85.packed_hbm = bf16[512,128]{1,0:T(8,128)(2,1)} custom-call(bf16[8,2048]{1,0:T(8,128)(2,1)} %down_hbm.1, bf16[8,2048]{1,0:T(8,128)(2,1)} %up_hbm.1, s32[2,128]{1,0:T(2,128)} %bitcast.21), custom_call_target="tpu_custom_call" | custom-call | tf_op jit(solution)/shard_map/pallas_call | solution.py:194
  2.1 13.2 %all-to-all-start = ((bf16[64,8,128]{2,1,0:T(8,128)(2,1)}), bf16[64,8,128]{2,1,0:T(8,128)(2,1)S(1)}, u32[]{:S(2)}, u32[]{:S(2)}) async-start(bf16[64,8,128]{2,1,0:T(8,128)(2,1)} %bitcast.20), calls=%async_computation | async-start | bytes 262144 | tf_op jit(solution)/shard_map/all_to_all | solution.py:183
  15.4 2.0 %shard_map.88 = (bf16[64,2048]{1,0:T(8,128)(2,1)}, bf16[128,2048]{1,0:T(8,128)(2,1)}) custom-call(s32[1]{0:T(128)} %bitcast.place_ref, bf16[64,8192]{1,0:T(8,128)(2,1)} %tokens_ref.1, bf16[512,128]{1,0:T(8,128)(2,1)} %shard_map.85.packed_hbm), custom_call_target="tpu_custom_call" | custom-call | tf_op jit(solution)/shard_map/pallas_call | solution.py:208
  17.4 2.2 %collective-permute-start.1 = (bf16[128,2048]{1,0:T(8,128)(2,1)}, bf16[128,2048]{1,0:T(8,128)(2,1)S(1)}, u32[]{:S(2)}, u32[]{:S(2)}) collective-permute-start(bf16[128,2048]{1,0:T(8,128)(2,1)} %get-tuple-element.19), channel_id=1, source_target_pairs={{0,2},{1,3},{2,0},{3,1},{4,6},{5,7},{6,4},{7,5},{8,10},{9,11},{10,... | collective-permute-start | bytes 1572872 | tf_op jit(solution)/shard_map/ppermute | solution.py:187
  19.6 0.6 shard_map.86.order_ref
  20.2 5.8 %all-to-all-done = bf16[64,8,128]{2,1,0:T(8,128)(2,1)S(1)} async-done(((bf16[64,8,128]{2,1,0:T(8,128)(2,1)}), bf16[64,8,128]{2,1,0:T(8,128)(2,1)S(1)}, u32[]{:S(2)}, u32[]{:S(2)}) %all-to-all-start) | async-done | bytes 131104 | tf_op jit(solution)/shard_map/all_to_all | solution.py:183
  26.0 1.0 %shard_map.87 = bf16[1024,128]{1,0:T(8,128)(2,1)} custom-call(bf16[512,128]{1,0:T(8,128)(2,1)S(1)} %bitcast.14), custom_call_target="tpu_custom_call" | custom-call | tf_op jit(solution)/shard_map/pallas_call | solution.py:229
  27.0 5.6 %all-to-all-start.1 = ((bf16[64,16,128]{2,1,0:T(8,128)(2,1)}), bf16[64,16,128]{2,1,0:T(8,128)(2,1)S(1)}, u32[]{:S(2)}, u32[]{:S(2)}) async-start(bf16[64,16,128]{2,1,0:T(8,128)(2,1)} %bitcast.4), calls=%async_computation.1 | async-start | bytes 524288 | tf_op jit(solution)/shard_map/all_to_all | solution.py:183
  32.6 0.4 collective-permute-done.1.two_ref
  33.0 0.1 collective-permute-start.2
  33.1 0.4 copy-done.6
  33.6 0.1 collective-permute-start
  34.3 0.3 collective-permute-done.2.three_ref
  34.7 0.4 collective-permute-done.one_ref
  35.1 10.0 %all-to-all-done.1 = bf16[64,16,128]{2,1,0:T(8,128)(2,1)S(1)} async-done(((bf16[64,16,128]{2,1,0:T(8,128)(2,1)}), bf16[64,16,128]{2,1,0:T(8,128)(2,1)S(1)}, u32[]{:S(2)}, u32[]{:S(2)}) %all-to-all-start.1) | async-done | bytes 262176 | tf_op jit(solution)/shard_map/all_to_all | solution.py:183
  45.1 0.0 copy-done.4
  45.1 0.7 shard_map.89
  45.8 0.0 copy-start.2
  45.8 0.1 collective-permute-start.5
  45.9 1.5 %collective-permute-start.4 = (f32[32,256]{1,0:T(8,128)S(1)}, f32[32,256]{1,0:T(8,128)S(1)}, u32[]{:S(2)}, u32[]{:S(2)}) collective-permute-start(f32[32,256]{1,0:T(8,128)S(1)} %get-tuple-element.21.own_ref), channel_id=1, source_target_pairs={{0,2},{1,3},{2,0},{3,1},{4,6},{5,7},{6,4},{7,5},{8,10},{9,11},{10,... | collective-permute-start | bytes 98312 | tf_op jit(solution)/shard_map/ppermute | solution.py:187
  47.5 1.8 %collective-permute-start.3 = (f32[32,256]{1,0:T(8,128)S(1)}, f32[32,256]{1,0:T(8,128)S(1)}, u32[]{:S(2)}, u32[]{:S(2)}) collective-permute-start(f32[32,256]{1,0:T(8,128)S(1)} %get-tuple-element.21.own_ref), channel_id=1, source_target_pairs={{0,1},{1,0},{2,3},{3,2},{4,5},{5,4},{6,7},{7,6},{8,9},{9,8},{10,11... | collective-permute-start | bytes 98312 | tf_op jit(solution)/shard_map/ppermute | solution.py:187
  49.3 1.5 %collective-permute-done.5.three_ref = f32[32,256]{1,0:T(8,128)S(1)} collective-permute-done((f32[32,256]{1,0:T(8,128)S(1)}, f32[32,256]{1,0:T(8,128)S(1)}, u32[]{:S(2)}, u32[]{:S(2)}) %collective-permute-start.5) | collective-permute-done | bytes 32800 | tf_op jit(solution)/shard_map/ppermute | solution.py:187
  50.8 0.7 collective-permute-done.4.two_ref
  51.4 0.0 collective-permute-done.3.one_ref
  51.5 0.4 shard_map.90
  51.9 0.0 copy-done.2
  51.9 18.9 %all_to_all.20 = bf16[64,16,128]{2,1,0:T(8,128)(2,1)S(1)} all-to-all(bf16[64,16,128]{2,1,0:T(8,128)(2,1)S(1)} %bitcast.19), channel_id=1, replica_groups=mesh['dp'=64,'tensor'=4] {'dp'}, dimensions={0} | all-to-all | bytes 524288 | tf_op jit(solution)/shard_map/all_to_all | solution.py:183
  70.8 1.0 %shard_map.92 = f32[256,128]{1,0:T(8,128)} custom-call(bf16[1024,128]{1,0:T(8,128)(2,1)S(1)} %bitcast.17, bf16[512,128]{1,0:T(8,128)(2,1)S(1)} %bitcast.15), custom_call_target="tpu_custom_call" | custom-call | tf_op jit(solution)/shard_map/pallas_call | solution.py:260
  71.7 4.9 %all-to-all-start.3 = ((f32[64,4,128]{2,1,0:T(4,128)}), f32[64,4,128]{2,1,0:T(4,128)S(1)}, u32[]{:S(2)}, u32[]{:S(2)}) async-start(f32[64,4,128]{2,1,0:T(4,128)} %bitcast.10), calls=%async_computation.3 | async-start | bytes 262144 | tf_op jit(solution)/shard_map/all_to_all | solution.py:183
  76.7 1.4 %shard_map.91 = bf16[256,2048]{1,0:T(8,128)(2,1)} custom-call(bf16[32,256]{1,0:T(8,128)(2,1)S(1)} %get-tuple-element.24.ranks_ref, bf16[64,2048]{1,0:T(8,128)(2,1)S(1)} %copy-done.3), custom_call_target="tpu_custom_call" | custom-call | flops 33554432 | bytes 2097152 | tf_op jit(solution)/shard_map/pallas_call | solution.py:254
  78.1 9.2 %all-to-all-done.3 = f32[64,4,128]{2,1,0:T(4,128)S(1)} async-done(((f32[64,4,128]{2,1,0:T(4,128)}), f32[64,4,128]{2,1,0:T(4,128)S(1)}, u32[]{:S(2)}, u32[]{:S(2)}) %all-to-all-start.3) | async-done | bytes 131104 | tf_op jit(solution)/shard_map/all_to_all | solution.py:183
  87.3 0.7 shard_map.93
  (12 shorter events, 0.0 us)
Async XLA Ops:
  2.1 23.8 %all-to-all-start = ((bf16[64,8,128]{2,1,0:T(8,128)(2,1)}), bf16[64,8,128]{2,1,0:T(8,128)(2,1)S(1)}, u32[]{:S(2)}, u32[]{:S(2)}) async-start(bf16[64,8,128]{2,1,0:T(8,128)(2,1)} %bitcast.20), calls=%async_computation | async-start | bytes 262144 | tf_op jit(solution)/shard_map/all_to_all | solution.py:183
  17.4 15.6 %collective-permute-start.1 = (bf16[128,2048]{1,0:T(8,128)(2,1)}, bf16[128,2048]{1,0:T(8,128)(2,1)S(1)}, u32[]{:S(2)}, u32[]{:S(2)}) collective-permute-start(bf16[128,2048]{1,0:T(8,128)(2,1)} %get-tuple-element.19), channel_id=1, source_target_pairs={{0,2},{1,3},{2,0},{3,1},{4,6},{5,7},{6,4},{7,5},{8,10},{9,11},{10,... | collective-permute-start | bytes 1572872 | tf_op jit(solution)/shard_map/ppermute | solution.py:187
  19.6 25.5 %copy-start.1 = (bf16[256,2048]{1,0:T(8,128)(2,1)S(1)}, bf16[256,2048]{1,0:T(8,128)(2,1)}, u32[]{:S(2)}) copy-start(bf16[256,2048]{1,0:T(8,128)(2,1)} %attn_ref.3) | copy-start | bytes 3145732
  20.2 24.9 %copy-start = (bf16[64,8192]{1,0:T(8,128)(2,1)S(1)}, bf16[64,8192]{1,0:T(8,128)(2,1)}, u32[]{:S(2)}) copy-start(bf16[64,8192]{1,0:T(8,128)(2,1)} %tokens_ref.1) | copy-start | bytes 3145732
  27.0 18.0 %all-to-all-start.1 = ((bf16[64,16,128]{2,1,0:T(8,128)(2,1)}), bf16[64,16,128]{2,1,0:T(8,128)(2,1)S(1)}, u32[]{:S(2)}, u32[]{:S(2)}) async-start(bf16[64,16,128]{2,1,0:T(8,128)(2,1)} %bitcast.4), calls=%async_computation.1 | async-start | bytes 524288 | tf_op jit(solution)/shard_map/all_to_all | solution.py:183
  32.6 1.0 %copy-start.6 = (bf16[64,2048]{1,0:T(8,128)(2,1)S(1)}, bf16[64,2048]{1,0:T(8,128)(2,1)}, u32[]{:S(2)}) copy-start(bf16[64,2048]{1,0:T(8,128)(2,1)} %get-tuple-element.18) | copy-start | bytes 786436
  33.0 1.3 %copy-start.5 = (s32[256]{0:T(256)S(1)}, s32[256]{0:T(256)}, u32[]{:S(2)}) copy-start(s32[256]{0:T(256)} %param.10) | copy-start | bytes 3076
  33.0 1.6 %collective-permute-start.2 = (bf16[64,2048]{1,0:T(8,128)(2,1)S(1)}, bf16[64,2048]{1,0:T(8,128)(2,1)S(1)}, u32[]{:S(2)}, u32[]{:S(2)}) collective-permute-start(bf16[64,2048]{1,0:T(8,128)(2,1)S(1)} %slice.4), channel_id=1, source_target_pairs={{0,1},{1,0},{2,3},{3,2},{4,5},{5,4},{6,7},{7,6},{8,9},{9,8},{10,11... | collective-permute-start | bytes 786440 | tf_op jit(solution)/shard_map/ppermute | solution.py:187
  33.5 11.5 %copy-start.4 = (s32[8,128]{1,0:T(8,128)S(1)}, s32[8,128]{1,0:T(8,128)}, u32[]{:S(2)}) copy-start(s32[8,128]{1,0:T(8,128)} %shard_map.86.order_ref) | copy-start | bytes 12292
  33.6 1.5 %collective-permute-start = (bf16[64,2048]{1,0:T(8,128)(2,1)S(1)}, bf16[64,2048]{1,0:T(8,128)(2,1)S(1)}, u32[]{:S(2)}, u32[]{:S(2)}) collective-permute-start(bf16[64,2048]{1,0:T(8,128)(2,1)S(1)} %copy-done.6), channel_id=1, source_target_pairs={{0,1},{1,0},{2,3},{3,2},{4,5},{5,4},{6,7},{7,6},{8,9},{9,8},{10,11... | collective-permute-start | bytes 786440 | tf_op jit(solution)/shard_map/ppermute | solution.py:187
  45.8 6.0 %copy-start.2 = (bf16[64,2048]{1,0:T(8,128)(2,1)}, bf16[64,2048]{1,0:T(8,128)(2,1)S(1)}, u32[]{:S(2)}) copy-start(bf16[64,2048]{1,0:T(8,128)(2,1)S(1)} %get-tuple-element.25.maps_ref) | copy-start | bytes 786436
  45.8 4.9 %collective-permute-start.5 = (f32[32,256]{1,0:T(8,128)S(1)}, f32[32,256]{1,0:T(8,128)S(1)}, u32[]{:S(2)}, u32[]{:S(2)}) collective-permute-start(f32[32,256]{1,0:T(8,128)S(1)} %get-tuple-element.21.own_ref), channel_id=1, source_target_pairs={{0,3},{1,2},{2,1},{3,0},{4,7},{5,6},{6,5},{7,4},{8,11},{9,10},{10,... | collective-permute-start | bytes 98312 | tf_op jit(solution)/shard_map/ppermute | solution.py:187
  45.9 5.5 %collective-permute-start.4 = (f32[32,256]{1,0:T(8,128)S(1)}, f32[32,256]{1,0:T(8,128)S(1)}, u32[]{:S(2)}, u32[]{:S(2)}) collective-permute-start(f32[32,256]{1,0:T(8,128)S(1)} %get-tuple-element.21.own_ref), channel_id=1, source_target_pairs={{0,2},{1,3},{2,0},{3,1},{4,6},{5,7},{6,4},{7,5},{8,10},{9,11},{10,... | collective-permute-start | bytes 98312 | tf_op jit(solution)/shard_map/ppermute | solution.py:187
  47.5 4.0 %collective-permute-start.3 = (f32[32,256]{1,0:T(8,128)S(1)}, f32[32,256]{1,0:T(8,128)S(1)}, u32[]{:S(2)}, u32[]{:S(2)}) collective-permute-start(f32[32,256]{1,0:T(8,128)S(1)} %get-tuple-element.21.own_ref), channel_id=1, source_target_pairs={{0,1},{1,0},{2,3},{3,2},{4,5},{5,4},{6,7},{7,6},{8,9},{9,8},{10,11... | collective-permute-start | bytes 98312 | tf_op jit(solution)/shard_map/ppermute | solution.py:187
  71.7 4.9 %copy-start.3 = (bf16[64,2048]{1,0:T(8,128)(2,1)S(1)}, bf16[64,2048]{1,0:T(8,128)(2,1)}, u32[]{:S(2)}) copy-start(bf16[64,2048]{1,0:T(8,128)(2,1)} %copy-done.2) | copy-start | bytes 786436
  71.7 15.5 %all-to-all-start.3 = ((f32[64,4,128]{2,1,0:T(4,128)}), f32[64,4,128]{2,1,0:T(4,128)S(1)}, u32[]{:S(2)}, u32[]{:S(2)}) async-start(f32[64,4,128]{2,1,0:T(4,128)} %bitcast.10), calls=%async_computation.3 | async-start | bytes 262144 | tf_op jit(solution)/shard_map/all_to_all | solution.py:183
